TPU v7x, 32 devices: a whole 2x2x4 slice. The times are simulated.
32 devices in a mesh: arm: 4 (over x, core), space: 8 (over z, y).
Axes of the slice: x: 2, y: 2, z: 4, core: 2. Of those that a mesh axis runs over, the one named last changes fastest.
Arguments:
- fields: float32 [2, 32, 64, 128], P(None, 'space'), may hold values from -2.5 to 2.5
- starts: float32 [16, 32, 64, 128], P('arm', 'space'), may hold values from 0.6 to 1.4
- labels: int32 [16], P('arm'), may hold values from 0 to 1
Outputs:
- density: float32 [2, 32, 64, 128], P(None, 'space', 'arm')
- new_fields: float32 [2, 32, 64, 128], P(None, 'space', 'arm')
All inputs are finite; a program needn't handle non-finite values.
Results may differ from a plain program's by a relative error of at most 0.0003.
Values sent between devices are 32-bit elements; how exact they have to be, the bound alone decides.
No kernel may reach another device: no remote copies, remote signals or barrier semaphores. Data moves between devices by JAX's collectives and lax.ppermute only.
A program may use at most 64 MiB of HBM per device.

v0:
```python
import jax
import jax.numpy as jnp
from jax import lax
from jax.sharding import PartitionSpec as P

coupling_full = 0.15
contour_step = 0.05
chi_value = 2.0
mixing = 0.5


def padded_2(block, sides, width):
    for axis, dim in sides:
        count = lax.axis_size(axis)
        forward = [(i, i + 1) for i in range(count - 1)]
        forward.append((count - 1, 0))
        backward = [(target, source) for source, target in forward]
        low = lax.ppermute(
            lax.slice_in_dim(block, block.shape[dim] - width, None, axis=dim), axis, forward
        )
        high = lax.ppermute(lax.slice_in_dim(block, 0, width, axis=dim), axis, backward)
        block = jnp.concatenate([low, block, high], axis=dim)
    return block


def stencil_inner(padded, coupling):
    middle = padded[:, 1:-1]
    beside = padded[:, 2:] + padded[:, :-2]
    beside = beside + jnp.roll(middle, 1, 2) + jnp.roll(middle, -1, 2)
    beside = beside + jnp.roll(middle, 1, 3) + jnp.roll(middle, -1, 3)
    return (1.0 - 6.0 * coupling) * middle + coupling * beside


def sub_valid(values, factor, coupling):
    return factor[:, 1:-1] * stencil_inner(factor * values, coupling)


def extrapolate(values, half_factor, full_factor):
    halves = sub_valid(values, half_factor, coupling_full / 2)
    halves = sub_valid(halves, half_factor[:, 1:-1], coupling_full / 2)
    whole_step = sub_valid(values[:, 1:-1], full_factor[:, 1:-1], coupling_full)
    return (4.0 * halves - whole_step) / 3.0


def arm_field(fields, labels):
    is_type_a = (labels == 0)[:, None, None, None]
    return jnp.where(is_type_a, fields[0][None], fields[1][None])


def factors(field_arm):
    return (jnp.exp(-field_arm * (contour_step / 4)), jnp.exp(-field_arm * (contour_step / 2)))


def local(fields, starts, labels):
    widened = padded_2(fields, (("space", 1),), 2)
    half_factor, full_factor = factors(arm_field(widened, labels))

    def one_step(values):
        padded = padded_2(values, (("space", 1),), 2)
        return extrapolate(padded, half_factor, full_factor)

    def advance(values):
        step_one = one_step(values)
        return (step_one, one_step(step_one))

    step_one, step_two = advance(starts)
    own_product = jnp.prod(step_two, axis=0)
    gathered = lax.all_gather(own_product[None], "arm", axis=0, tiled=True)
    junction = jnp.prod(gathered, axis=0)
    partition_sum = lax.psum(jnp.sum(junction), "space")
    cell_count = fields.shape[1] * lax.axis_size("space") * fields.shape[2] * fields.shape[3]
    arm_count = labels.shape[0] * lax.axis_size("arm")
    partition = partition_sum / cell_count
    back_one, back_two = advance(junction[None] / step_two)
    segment = 0.25 * back_two + 0.5 * step_one * back_one + 0.25 * junction[None]
    segment = segment / (arm_count * partition)
    is_type_a = (labels == 0)[:, None, None, None]
    partial_value = jnp.stack(
        [
            jnp.sum(jnp.where(is_type_a, segment, 0.0), axis=0),
            jnp.sum(jnp.where(is_type_a, 0.0, segment), axis=0),
        ]
    )
    density = lax.psum_scatter(partial_value, "arm", scatter_dimension=2, tiled=True)
    owned_rows = density.shape[2]
    owned = lax.dynamic_slice_in_dim(fields, lax.axis_index("arm") * owned_rows, owned_rows, 2)
    pressure = 0.5 * (owned[0] + owned[1] - chi_value)
    update_a = owned[0] + mixing * (chi_value * density[1] + pressure - owned[0])
    update_b = owned[1] + mixing * (chi_value * density[0] + pressure - owned[1])
    return (density, jnp.stack([update_a, update_b]))


def solution(mesh):
    in_specs = (P(None, "space", None, None), P("arm", "space", None, None), P("arm"))
    out_specs = (P(None, "space", "arm", None), P(None, "space", "arm", None))
    return jax.shard_map(local, mesh=mesh, in_specs=in_specs, out_specs=out_specs, check_vma=False)
```

profile of v0, /device:TPU:0, one launch (start us, length us, event | category | flops | bytes accessed | tf_op | source)
XLA Modules:
  0.0 142.7 jit_solution(11746455409576310191)
XLA Ops:
  7.2 1.0 fusion.161
  8.3 3.0 %collective-permute-start = (f32[2,2,64,128]{3,2,1,0:T(8,128)S(1)}, f32[2,2,64,128]{3,2,1,0:T(8,128)S(1)}, u32[]{:S(2)}, u32[]{:S(2)}) collective-permute-start(f32[2,2,64,128]{3,2,1,0:T(8,128)S(1)} %get-tuple-element.126), channel_id=1, source_target_pairs={{0,1},{1,2},{2,3},{3,4},{4,5},{5,6},{6,7},{7,0},{8,9},{9,10},{10,1... | collective-permute-start | bytes 393224 | tf_op jit(solution)/shard_map/ppermute | solution.py:18
  11.3 3.1 %collective-permute-start.1 = (f32[2,2,64,128]{3,2,1,0:T(8,128)S(1)}, f32[2,2,64,128]{3,2,1,0:T(8,128)S(1)}, u32[]{:S(2)}, u32[]{:S(2)}) collective-permute-start(f32[2,2,64,128]{3,2,1,0:T(8,128)S(1)} %get-tuple-element.125), channel_id=1, source_target_pairs={{1,0},{2,1},{3,2},{4,3},{5,4},{6,5},{7,6},{0,7},{9,8},{10,9},{11,1... | collective-permute-start | bytes 393224 | tf_op jit(solution)/shard_map/ppermute | solution.py:21
  14.5 4.7 %collective-permute-start.3 = (f32[4,2,64,128]{3,2,1,0:T(8,128)S(1)}, f32[4,2,64,128]{3,2,1,0:T(8,128)S(1)}, u32[]{:S(2)}, u32[]{:S(2)}) collective-permute-start(f32[4,2,64,128]{3,2,1,0:T(8,128)S(1)} %get-tuple-element.121), channel_id=1, source_target_pairs={{1,0},{2,1},{3,2},{4,3},{5,4},{6,5},{7,6},{0,7},{9,8},{10,9},{11,1... | collective-permute-start | bytes 786440 | tf_op jit(solution)/shard_map/ppermute | solution.py:21
  19.2 3.7 %collective-permute-done = f32[2,2,64,128]{3,2,1,0:T(8,128)S(1)} collective-permute-done((f32[2,2,64,128]{3,2,1,0:T(8,128)S(1)}, f32[2,2,64,128]{3,2,1,0:T(8,128)S(1)}, u32[]{:S(2)}, u32[]{:S(2)}) %collective-permute-start) | collective-permute-done | bytes 131104 | tf_op jit(solution)/shard_map/ppermute | solution.py:18
  23.0 2.8 %collective-permute-done.1 = f32[2,2,64,128]{3,2,1,0:T(8,128)S(1)} collective-permute-done((f32[2,2,64,128]{3,2,1,0:T(8,128)S(1)}, f32[2,2,64,128]{3,2,1,0:T(8,128)S(1)}, u32[]{:S(2)}, u32[]{:S(2)}) %collective-permute-start.1) | collective-permute-done | bytes 131104 | tf_op jit(solution)/shard_map/ppermute | solution.py:21
  25.9 2.2 %collective-permute-done.2 = f32[4,2,64,128]{3,2,1,0:T(8,128)S(1)} collective-permute-done((f32[4,2,64,128]{3,2,1,0:T(8,128)S(1)}, f32[4,2,64,128]{3,2,1,0:T(8,128)S(1)}, u32[]{:S(2)}, u32[]{:S(2)}) %collective-permute-start.2) | collective-permute-done | bytes 262176 | tf_op jit(solution)/shard_map/ppermute | solution.py:18
  28.2 2.1 %collective-permute-done.3 = f32[4,2,64,128]{3,2,1,0:T(8,128)S(1)} collective-permute-done((f32[4,2,64,128]{3,2,1,0:T(8,128)S(1)}, f32[4,2,64,128]{3,2,1,0:T(8,128)S(1)}, u32[]{:S(2)}, u32[]{:S(2)}) %collective-permute-start.3) | collective-permute-done | bytes 262176 | tf_op jit(solution)/shard_map/ppermute | solution.py:21
  30.3 0.6 multiply_exponential_fusion.1
  30.9 0.3 fusion.121
  31.2 0.3 fusion.122
  31.5 0.1 fusion.123
  31.7 0.7 multiply_multiply_fusion.3
  32.4 0.2 fusion.152
  32.7 0.2 fusion.151
  33.2 0.2 fusion.155
  33.4 0.2 fusion.156
  33.6 1.8 %broadcast_multiply_fusion = (f32[4,4,64,128]{3,2,1,0:T(8,128)S(1)}, f32[4,4,64,128]{3,2,1,0:T(8,128)}) fusion(f32[4,4,64,1]{3,2,1,0:T(8,128)S(1)} %get-tuple-element.107, f32[4,4,64,127]{3,2,1,0:T(8,128)S(1)} %get-tuple-element.109, f32[4,4,64,127]{3,2,1,0:T(8,128)S(1)} %get-tuple-element.108, f32[4,4,64,1]{3,2,1,0:T(8,128)S(1)} %get-tuple-element.106, ...), kind=kLoop, calls=%fused_computation.142 | loop fusion | flops 3801088 | bytes 9437184 | tf_op jit(solution)/shard_map/div | solution.py:42
  35.5 0.4 collective-permute-start.4
  35.9 4.4 %collective-permute-start.5 = (f32[4,2,64,128]{3,2,1,0:T(8,128)S(1)}, f32[4,2,64,128]{3,2,1,0:T(8,128)S(1)}, u32[]{:S(2)}, u32[]{:S(2)}) collective-permute-start(f32[4,2,64,128]{3,2,1,0:T(8,128)S(1)} %get-tuple-element.118), channel_id=1, source_target_pairs={{1,0},{2,1},{3,2},{4,3},{5,4},{6,5},{7,6},{0,7},{9,8},{10,9},{11,1... | collective-permute-start | bytes 786440 | tf_op jit(solution)/shard_map/ppermute | solution.py:21
  40.3 6.6 %collective-permute-done.4 = f32[4,2,64,128]{3,2,1,0:T(8,128)S(1)} collective-permute-done((f32[4,2,64,128]{3,2,1,0:T(8,128)S(1)}, f32[4,2,64,128]{3,2,1,0:T(8,128)S(1)}, u32[]{:S(2)}, u32[]{:S(2)}) %collective-permute-start.4) | collective-permute-done | bytes 262176 | tf_op jit(solution)/shard_map/ppermute | solution.py:18
  46.9 3.2 %collective-permute-done.5 = f32[4,2,64,128]{3,2,1,0:T(8,128)S(1)} collective-permute-done((f32[4,2,64,128]{3,2,1,0:T(8,128)S(1)}, f32[4,2,64,128]{3,2,1,0:T(8,128)S(1)}, u32[]{:S(2)}, u32[]{:S(2)}) %collective-permute-start.5) | collective-permute-done | bytes 262176 | tf_op jit(solution)/shard_map/ppermute | solution.py:21
  50.1 0.3 fusion.2
  50.4 0.3 fusion.117
  50.7 0.3 fusion.118
  51.0 0.1 fusion.119
  51.1 0.7 multiply_multiply_fusion.2
  52.0 0.2 fusion.143
  52.2 0.2 fusion.144
  52.6 0.2 fusion.147
  52.8 0.2 fusion.148
  53.1 1.0 fusion.106
  54.1 7.6 %all-gather = f32[16,64,128]{2,1,0:T(8,128)} all-gather(f32[4,64,128]{2,1,0:T(8,128)S(1)} %get-tuple-element.4), channel_id=2, replica_groups=mesh['arm'=4,'space'=8] {'arm'}, dimensions={0}, use_global_device_ids=true | all-gather | bytes 655360 | tf_op jit(solution)/shard_map/all_gather | solution.py:68
  61.7 1.1 reduce_prod.19
  63.0 4.7 %collective-permute-start.7 = (f32[4,2,64,128]{3,2,1,0:T(8,128)S(1)}, f32[4,2,64,128]{3,2,1,0:T(8,128)S(1)}, u32[]{:S(2)}, u32[]{:S(2)}) collective-permute-start(f32[4,2,64,128]{3,2,1,0:T(8,128)S(1)} %get-tuple-element.116), channel_id=1, source_target_pairs={{1,0},{2,1},{3,2},{4,3},{5,4},{6,5},{7,6},{0,7},{9,8},{10,9},{11,1... | collective-permute-start | bytes 786440 | tf_op jit(solution)/shard_map/ppermute | solution.py:21
  67.7 7.3 %collective-permute-done.6 = f32[4,2,64,128]{3,2,1,0:T(8,128)S(1)} collective-permute-done((f32[4,2,64,128]{3,2,1,0:T(8,128)S(1)}, f32[4,2,64,128]{3,2,1,0:T(8,128)S(1)}, u32[]{:S(2)}, u32[]{:S(2)}) %collective-permute-start.6) | collective-permute-done | bytes 262176 | tf_op jit(solution)/shard_map/ppermute | solution.py:18
  75.0 3.1 %collective-permute-done.7 = f32[4,2,64,128]{3,2,1,0:T(8,128)S(1)} collective-permute-done((f32[4,2,64,128]{3,2,1,0:T(8,128)S(1)}, f32[4,2,64,128]{3,2,1,0:T(8,128)S(1)}, u32[]{:S(2)}, u32[]{:S(2)}) %collective-permute-start.7) | collective-permute-done | bytes 262176 | tf_op jit(solution)/shard_map/ppermute | solution.py:21
  78.1 0.3 fusion.1
  78.4 0.3 fusion.113
  78.7 0.3 fusion.114
  79.1 0.7 multiply_multiply_fusion.1
  79.9 0.2 fusion.137
  80.1 0.2 fusion.138
  80.5 0.2 fusion.133
  80.7 0.2 fusion.134
  81.1 1.0 fusion.56
  82.1 0.8 fusion.157
  82.9 4.7 %collective-permute-start.9 = (f32[4,2,64,128]{3,2,1,0:T(8,128)}, f32[4,2,64,128]{3,2,1,0:T(8,128)}, u32[]{:S(2)}, u32[]{:S(2)}) collective-permute-start(f32[4,2,64,128]{3,2,1,0:T(8,128)} %get-tuple-element.114), channel_id=1, source_target_pairs={{1,0},{2,1},{3,2},{4,3},{5,4},{6,5},{7,6},{0,7},{9,8},{10,9},{11,1... | collective-permute-start | bytes 786440 | tf_op jit(solution)/shard_map/ppermute | solution.py:21
  87.6 1.2 broadcast_multiply_fusion.1
  88.9 20.2 %psum.7 = f32[]{:T(128)} all-reduce(f32[]{:T(128)} %get-tuple-element.128), channel_id=1, replica_groups=mesh['arm'=4,'space'=8] {'space'}, use_global_device_ids=true, to_apply=%region_3.4 | all-reduce | flops 1 | bytes 8 | tf_op jit(solution)/shard_map/psum | solution.py:70
  109.8 1.3 fusion
  111.1 0.3 fusion.110
  111.5 0.3 fusion.109
  111.8 0.8 multiply_multiply_fusion
  112.7 0.2 fusion.125
  112.9 0.2 fusion.126
  113.2 0.2 fusion.129
  113.4 0.2 fusion.130
  113.8 0.9 copy-done
  114.7 1.2 select_reduce_fusion.1
  115.8 0.7 pad_maximum_fusion.3
  116.6 17.9 %reduce-scatter.2.cloned.1.call-done = f32[2,4,16,128]{3,2,1,0:T(8,128)} async-done(((f32[2,4,64,128]{3,2,1,0:T(8,128)}), f32[2,4,16,128]{3,2,1,0:T(8,128)}) %reduce-scatter.2.cloned.1.call-update) | async-done | bytes 65552 | tf_op jit(solution)/shard_map/reduce_scatter | solution.py:84
  134.5 0.8 fusion.105
  135.3 0.6 pad_maximum_fusion.4
  (53 shorter events, 2.0 us)
Async XLA Ops:
  7.2 7.2 %copy-start.1 = (f32[4,4,64,128]{3,2,1,0:T(8,128)S(1)}, f32[4,4,64,128]{3,2,1,0:T(8,128)}, u32[]{:S(2)}) copy-start(f32[4,4,64,128]{3,2,1,0:T(8,128)} %param.4) | copy-start | bytes 1572868
  7.2 127.3 %reduce-scatter.2.cloned.1.call-start = ((), (), s32[]{:S(2)}) async-start(), calls=%async_computation.1 | async-start | bytes 327680 | tf_op jit(solution)/shard_map/reduce_scatter | solution.py:84
  8.3 14.7 %collective-permute-start = (f32[2,2,64,128]{3,2,1,0:T(8,128)S(1)}, f32[2,2,64,128]{3,2,1,0:T(8,128)S(1)}, u32[]{:S(2)}, u32[]{:S(2)}) collective-permute-start(f32[2,2,64,128]{3,2,1,0:T(8,128)S(1)} %get-tuple-element.126), channel_id=1, source_target_pairs={{0,1},{1,2},{2,3},{3,4},{4,5},{5,6},{6,7},{7,0},{8,9},{9,10},{10,1... | collective-permute-start | bytes 393224 | tf_op jit(solution)/shard_map/ppermute | solution.py:18
  11.3 14.5 %collective-permute-start.1 = (f32[2,2,64,128]{3,2,1,0:T(8,128)S(1)}, f32[2,2,64,128]{3,2,1,0:T(8,128)S(1)}, u32[]{:S(2)}, u32[]{:S(2)}) collective-permute-start(f32[2,2,64,128]{3,2,1,0:T(8,128)S(1)} %get-tuple-element.125), channel_id=1, source_target_pairs={{1,0},{2,1},{3,2},{4,3},{5,4},{6,5},{7,6},{0,7},{9,8},{10,9},{11,1... | collective-permute-start | bytes 393224 | tf_op jit(solution)/shard_map/ppermute | solution.py:21
  14.4 4.8 %copy-start.4 = (s32[4]{0:T(128)S(1)}, s32[4]{0:T(128)}, u32[]{:S(2)}) copy-start(s32[4]{0:T(128)} %param.5) | copy-start | bytes 52
  14.4 8.5 %copy-start.2 = (f32[2,4,64,128]{3,2,1,0:T(8,128)S(1)}, f32[2,4,64,128]{3,2,1,0:T(8,128)}, u32[]{:S(2)}) copy-start(f32[2,4,64,128]{3,2,1,0:T(8,128)} %param.3) | copy-start | bytes 786436
  14.5 13.6 %collective-permute-start.2 = (f32[4,2,64,128]{3,2,1,0:T(8,128)S(1)}, f32[4,2,64,128]{3,2,1,0:T(8,128)S(1)}, u32[]{:S(2)}, u32[]{:S(2)}) collective-permute-start(f32[4,2,64,128]{3,2,1,0:T(8,128)S(1)} %get-tuple-element.122), channel_id=1, source_target_pairs={{0,1},{1,2},{2,3},{3,4},{4,5},{5,6},{6,7},{7,0},{8,9},{9,10},{10,1... | collective-permute-start | bytes 786440 | tf_op jit(solution)/shard_map/ppermute | solution.py:18
  14.5 15.8 %collective-permute-start.3 = (f32[4,2,64,128]{3,2,1,0:T(8,128)S(1)}, f32[4,2,64,128]{3,2,1,0:T(8,128)S(1)}, u32[]{:S(2)}, u32[]{:S(2)}) collective-permute-start(f32[4,2,64,128]{3,2,1,0:T(8,128)S(1)} %get-tuple-element.121), channel_id=1, source_target_pairs={{1,0},{2,1},{3,2},{4,3},{5,4},{6,5},{7,6},{0,7},{9,8},{10,9},{11,1... | collective-permute-start | bytes 786440 | tf_op jit(solution)/shard_map/ppermute | solution.py:21
  35.5 11.4 %collective-permute-start.4 = (f32[4,2,64,128]{3,2,1,0:T(8,128)S(1)}, f32[4,2,64,128]{3,2,1,0:T(8,128)S(1)}, u32[]{:S(2)}, u32[]{:S(2)}) collective-permute-start(f32[4,2,64,128]{3,2,1,0:T(8,128)S(1)} %get-tuple-element.117), channel_id=1, source_target_pairs={{0,1},{1,2},{2,3},{3,4},{4,5},{5,6},{6,7},{7,0},{8,9},{9,10},{10,1... | collective-permute-start | bytes 786440 | tf_op jit(solution)/shard_map/ppermute | solution.py:18
  35.9 14.2 %collective-permute-start.5 = (f32[4,2,64,128]{3,2,1,0:T(8,128)S(1)}, f32[4,2,64,128]{3,2,1,0:T(8,128)S(1)}, u32[]{:S(2)}, u32[]{:S(2)}) collective-permute-start(f32[4,2,64,128]{3,2,1,0:T(8,128)S(1)} %get-tuple-element.118), channel_id=1, source_target_pairs={{1,0},{2,1},{3,2},{4,3},{5,4},{6,5},{7,6},{0,7},{9,8},{10,9},{11,1... | collective-permute-start | bytes 786440 | tf_op jit(solution)/shard_map/ppermute | solution.py:21
  62.9 12.0 %collective-permute-start.6 = (f32[4,2,64,128]{3,2,1,0:T(8,128)S(1)}, f32[4,2,64,128]{3,2,1,0:T(8,128)S(1)}, u32[]{:S(2)}, u32[]{:S(2)}) collective-permute-start(f32[4,2,64,128]{3,2,1,0:T(8,128)S(1)} %get-tuple-element.115), channel_id=1, source_target_pairs={{0,1},{1,2},{2,3},{3,4},{4,5},{5,6},{6,7},{7,0},{8,9},{9,10},{10,1... | collective-permute-start | bytes 786440 | tf_op jit(solution)/shard_map/ppermute | solution.py:18
  63.0 15.1 %collective-permute-start.7 = (f32[4,2,64,128]{3,2,1,0:T(8,128)S(1)}, f32[4,2,64,128]{3,2,1,0:T(8,128)S(1)}, u32[]{:S(2)}, u32[]{:S(2)}) collective-permute-start(f32[4,2,64,128]{3,2,1,0:T(8,128)S(1)} %get-tuple-element.116), channel_id=1, source_target_pairs={{1,0},{2,1},{3,2},{4,3},{5,4},{6,5},{7,6},{0,7},{9,8},{10,9},{11,1... | collective-permute-start | bytes 786440 | tf_op jit(solution)/shard_map/ppermute | solution.py:21
  82.9 26.8 %collective-permute-start.8 = (f32[4,2,64,128]{3,2,1,0:T(8,128)}, f32[4,2,64,128]{3,2,1,0:T(8,128)}, u32[]{:S(2)}, u32[]{:S(2)}) collective-permute-start(f32[4,2,64,128]{3,2,1,0:T(8,128)} %get-tuple-element.113), channel_id=1, source_target_pairs={{0,1},{1,2},{2,3},{3,4},{4,5},{5,6},{6,7},{7,0},{8,9},{9,10},{10,1... | collective-permute-start | bytes 786440 | tf_op jit(solution)/shard_map/ppermute | solution.py:18
  82.9 26.8 %collective-permute-start.9 = (f32[4,2,64,128]{3,2,1,0:T(8,128)}, f32[4,2,64,128]{3,2,1,0:T(8,128)}, u32[]{:S(2)}, u32[]{:S(2)}) collective-permute-start(f32[4,2,64,128]{3,2,1,0:T(8,128)} %get-tuple-element.114), channel_id=1, source_target_pairs={{1,0},{2,1},{3,2},{4,3},{5,4},{6,5},{7,6},{0,7},{9,8},{10,9},{11,1... | collective-permute-start | bytes 786440 | tf_op jit(solution)/shard_map/ppermute | solution.py:21
  113.6 1.0 copy-start
  113.6 1.1 copy-start.3
Sparse Core Ops, SparseCore 0:
  116.7 17.7 reduce-scatter.1
where the time goes:
time: 143 us
  waiting for transfers between devices  48.9 us (34%)
  blocking collectives  27.8 us (19%)
  starting transfers between devices  25.2 us (18%)
  other arithmetic  15.5 us (11%)
  between operations  15.1 us (11%)
  local copies, waits for them, and re-layouts  10.2 us (7%)
    ppermute x5, starting transfers between devices, padded_2(): lax.ppermute(lax.slice_in_dim(block, 0, width, axis=dim), axis, backward)  21.6 us
    psum x1, blocking collectives, local(): partition_sum = lax.psum(jnp.sum(junction), 'space')  20.2 us
    ppermute x5, waiting for transfers between devices, padded_2(): lax.ppermute(lax.slice_in_dim(block, block.shape[dim] - width, None, axis...  19.8 us
    reduce_scatter x1, waiting for transfers between devices, local(): lax.psum_scatter(partial_value, 'arm', scatter_dimension=2, tiled=True)  17.9 us
    ppermute x5, waiting for transfers between devices, padded_2(): lax.ppermute(lax.slice_in_dim(block, 0, width, axis=dim), axis, backward)  11.2 us
    all_gather x1, blocking collectives, local(): gathered = lax.all_gather(own_product[None], 'arm', axis=0, tiled=True)  7.62 us
    slice x24, local copies, waits for them, and re-layouts, stencil_inner(): beside = beside + jnp.roll(middle, 1, 3) + jnp.roll(middle, -1, 3)  5.7 us
    mul x10, other arithmetic, sub_valid(): return factor[:, 1:-1] * stencil_inner(factor * values, coupling)  5.22 us
  transfers between devices with their start and end apart: 11, of which 9 were waited for; matrix products, arithmetic and copies ran while one was open for 1% of the time, Pallas kernels for 0%

commit v1 on v0

v1 whole, which is shorter than its diff:
```python
import functools

import jax
import jax.numpy as jnp
from jax import lax
from jax.experimental import pallas as pl
from jax.experimental.pallas import tpu as pltpu
from jax.sharding import PartitionSpec as P

coupling_full = 0.15
contour_step = 0.05
chi_value = 2.0
mixing = 0.5
reach = 2

AXES = ("arm", "space")


def beside(plane):
    rows, columns = plane.shape
    total = pltpu.roll(plane, 1, 0) + pltpu.roll(plane, rows - 1, 0)
    return total + (pltpu.roll(plane, 1, 1) + pltpu.roll(plane, columns - 1, 1))


def contour(first, last, arms, factor, values, store, p_ref, t_ref, s_ref):
    half = coupling_full / 2
    centre_half, centre_full = 1.0 - 6.0 * half, 1.0 - 6.0 * coupling_full

    def scale(i, _):
        for j in range(arms):
            u = factor(j, i)
            p = u * values(j, i)
            p_ref[j, i] = p
            t_ref[j, i] = u * p

    def inner(i, _):
        for j in range(arms):
            u = factor(j, i)
            p = p_ref[j, i]
            around = beside(p) + (p_ref[j, i - 1] + p_ref[j, i + 1])
            s_ref[j, i] = (u * u) * (centre_half * p + half * around)

    def outer(i, _):
        for j in range(arms):
            u = factor(j, i)
            s, t = s_ref[j, i], t_ref[j, i]
            s_around = beside(s) + (s_ref[j, i - 1] + s_ref[j, i + 1])
            t_around = beside(t) + (t_ref[j, i - 1] + t_ref[j, i + 1])
            halves = (4.0 / 3.0 * centre_half) * s + (4.0 / 3.0 * half) * s_around
            whole = (centre_full / 3.0) * t + (coupling_full / 3.0) * t_around
            store(j, i, u * (halves - u * whole))

    lax.fori_loop(first, last, scale, None)
    lax.fori_loop(first + 1, last - 1, inner, None)
    lax.fori_loop(first + 2, last - 2, outer, None)


def forward_kernel(
    labels, starts, swap, straight, across, fields,
    f_swap, f_straight, f_across, g_swap, g_straight, g_across,
    u_ref, one_ref, low_ref, high_ref, keep_ref, send_ref,
    q_ref, p_ref, t_ref, s_ref, product_ref,
):
    block = starts.shape[1]
    arms = swap.shape[0]
    side = lax.rem(lax.axis_index("space"), 2)
    core = lax.rem(lax.axis_index("arm"), 2)
    own_at, swap_at = block + side * block, 2 * block - side * block
    straight_at, across_at = 3 * block * (1 - side), 3 * block * side

    def gain(field):
        return jnp.exp(field * (-contour_step / 4))

    def fill(i, _):
        for kind in range(2):
            u_ref[kind, own_at + i] = gain(fields[kind, i])
        for at, mine, other in (
            (swap_at, f_swap, g_swap),
            (straight_at, f_straight, g_straight),
            (across_at, f_across, g_across),
        ):
            u_ref[core, at + i] = gain(mine[i])
            u_ref[1 - core, at + i] = gain(other[i])
        for j in range(arms):
            q_ref[j, own_at + i] = starts[side * arms + j, i]
            q_ref[j, swap_at + i] = swap[j, i]
            q_ref[j, straight_at + i] = straight[j, i]
            q_ref[j, across_at + i] = across[j, i]

    lax.fori_loop(0, block, fill, None)
    kinds = [labels[side * arms + j] for j in range(arms)]

    def factor(j, i):
        return u_ref[kinds[j], i]

    def values(j, i):
        return q_ref[j, i]

    def store(j, i, value):
        q_ref[j, i] = value

    inner_at = block - 2 * reach
    contour(inner_at, 4 * block - inner_at, arms, factor, values, store, p_ref, t_ref, s_ref)
    for j in range(arms):
        one_ref[j] = q_ref[j, block : 3 * block]
    inner_at = block - reach
    contour(inner_at, 4 * block - inner_at, arms, factor, values, store, p_ref, t_ref, s_ref)

    def finish(i, _):
        low, high = q_ref[0, block + i], q_ref[0, 2 * block + i]
        low_ref[0, i], high_ref[0, i] = low, high
        for j in range(1, arms):
            low_next, high_next = q_ref[j, block + i], q_ref[j, 2 * block + i]
            low_ref[j, i], high_ref[j, i] = low_next, high_next
            low, high = low * low_next, high * high_next
        product_ref[0, i], product_ref[1, i] = low, high
        keep_ref[i] = product_ref[core, i]
        send_ref[i] = product_ref[1 - core, i]

    lax.fori_loop(0, block, finish, None)


def backward_kernel(
    labels, u_ref, one_ref, two_left, two_low, two_high, two_right,
    j_mine, j_other, j_halo, j_halo_other,
    keep_ref, send_ref,
    junction_ref, q_ref, p_ref, t_ref, s_ref, density_ref,
):
    arms, block = two_low.shape[0], two_low.shape[1]
    side = lax.rem(lax.axis_index("space"), 2)
    core = lax.rem(lax.axis_index("arm"), 2)
    kinds = [labels[side * arms + j] for j in range(arms)]

    def fill(i, _):
        junction_ref[block + core * block + i] = j_mine[i]
        junction_ref[2 * block - core * block + i] = j_other[i]
        junction_ref[3 * block * (1 - core) + i] = j_halo[i]
        junction_ref[3 * block * core + i] = j_halo_other[i]
        for place, two in enumerate((two_left, two_low, two_high, two_right)):
            whole = junction_ref[place * block + i]
            for j in range(arms):
                q_ref[j, place * block + i] = whole / two[j, i]

    lax.fori_loop(0, block, fill, None)

    def factor(j, i):
        return u_ref[kinds[j], i]

    def values(j, i):
        return q_ref[j, i]

    def store(j, i, value):
        q_ref[j, i] = value

    inner_at = block - 2 * reach
    contour(inner_at, 4 * block - inner_at, arms, factor, values, store, p_ref, t_ref, s_ref)
    for j in range(arms):
        one_ref_j = one_ref[j]
        density_ref[j] = 0.5 * one_ref_j * q_ref[j, block : 3 * block]
    inner_at = block - reach
    contour(inner_at, 4 * block - inner_at, arms, factor, values, store, p_ref, t_ref, s_ref)

    is_a = [(kind == 0).astype(jnp.float32) for kind in kinds]

    def segment(i, _):
        quarter = 0.25 * junction_ref[block + i]
        total_a = total_b = None
        for j in range(arms):
            value = density_ref[j, i] + 0.25 * q_ref[j, block + i] + quarter
            part_a, part_b = is_a[j] * value, (1.0 - is_a[j]) * value
            total_a = part_a if j == 0 else total_a + part_a
            total_b = part_b if j == 0 else total_b + part_b
        s_ref[0, i], s_ref[1, i] = total_a, total_b

    lax.fori_loop(0, 2 * block, segment, None)
    chips, owned = keep_ref.shape[0], keep_ref.shape[4]

    def spread(i, _):
        for chip in range(chips):
            mine = pl.ds(pl.multiple_of((2 * chip + core) * owned, 8), owned)
            other = pl.ds(pl.multiple_of((2 * chip + 1 - core) * owned, 8), owned)
            for part in range(2):
                for kind in range(2):
                    keep_ref[chip, part, kind, i] = s_ref[kind, part * block + i, mine]
                    send_ref[chip, part, kind, i] = s_ref[kind, part * block + i, other]

    lax.fori_loop(0, block, spread, None)


def meet_kernel(keep, received, own_ref, *out_refs):
    chips = keep.shape[0]
    side = lax.rem(lax.axis_index("space"), 2)
    chip = lax.div(lax.axis_index("arm"), 2)
    own_ref[...] = keep[chip, side] + received[chip, side]
    for out_ref, (step, flip) in zip(out_refs, other_chips(chips)):
        to_chip = lax.rem(chip + step, chips)
        to_side = 1 - side if flip else side
        out_ref[...] = keep[to_chip, to_side] + received[to_chip, to_side]


def final_kernel(cell_count, arm_count, fields, total, own, *refs):
    *others, density_ref, new_ref = refs
    owned = own.shape[2]
    scale = cell_count / (arm_count * jnp.sum(total[...]))
    rows = pl.ds(pl.multiple_of(lax.axis_index("arm") * owned, 8), owned)
    density = own[...]
    for other in others:
        density = density + other[...]
    density = density * scale
    density_ref[...] = density
    field_a, field_b = fields[0, :, rows], fields[1, :, rows]
    pressure = 0.5 * (field_a + field_b - chi_value)
    new_ref[0] = field_a + mixing * (chi_value * density[1] + pressure - field_a)
    new_ref[1] = field_b + mixing * (chi_value * density[0] + pressure - field_b)


def other_chips(chips):
    return [(step, flip) for step in range(chips) for flip in (False, True) if step or flip]


def vmem(shape):
    return pltpu.VMEM(shape, jnp.float32)


def f32(shape):
    return jax.ShapeDtypeStruct(shape, jnp.float32)


def call(kernel, out_shape, scratch, smem, *args, cost=1_000_000):
    specs = [pl.BlockSpec(memory_space=pltpu.SMEM if k < smem else pltpu.VMEM) for k in range(len(args))]
    return pl.pallas_call(
        kernel,
        out_shape=out_shape,
        in_specs=specs,
        out_specs=jax.tree.map(lambda _: pl.BlockSpec(memory_space=pltpu.VMEM), out_shape),
        scratch_shapes=scratch,
        compiler_params=pltpu.CompilerParams(vmem_limit_bytes=40 * 1024 * 1024),
        cost_estimate=pl.CostEstimate(flops=cost, bytes_accessed=cost, transcendentals=0),
    )(*args)


def local(fields, starts, labels):
    arm_size, space_size = lax.axis_size("arm"), lax.axis_size("space")
    chips, pairs = arm_size // 2, space_size // 2
    held, block, rows, columns = starts.shape
    arms = held // 2
    owned = rows // arm_size
    side = lax.rem(lax.axis_index("space"), 2)
    core = lax.rem(lax.axis_index("arm"), 2)

    def send(value, target):
        perm = []
        for a in range(arm_size):
            for s in range(space_size):
                chip_to, core_to, pair_to, side_to = target(a // 2, a % 2, s // 2, s % 2)
                to = (2 * (chip_to % chips) + core_to) * space_size + 2 * (pair_to % pairs) + side_to
                perm.append((a * space_size + s, to))
        return lax.ppermute(value, AXES, perm)

    def to_core(value):
        return send(value, lambda x, c, p, h: (x, 1 - c, p, h))

    def to_side(value):
        return send(value, lambda x, c, p, h: (x, c, p, 1 - h))

    def to_straight(value):
        return send(value, lambda x, c, p, h: (x, c, p + 2 * h - 1, h))

    def to_across(value):
        return send(value, lambda x, c, p, h: (x, c, p + 2 * h - 1, 1 - h))

    field_own = lax.dynamic_index_in_dim(fields, core, 0, keepdims=False)
    field_got = [to_side(field_own), to_straight(field_own), to_across(field_own)]
    start_own = lax.dynamic_slice_in_dim(starts, side * arms, arms, 0)
    start_other = lax.dynamic_slice_in_dim(starts, (1 - side) * arms, arms, 0)
    start_got = [to_side(start_other), to_straight(start_own), to_across(start_other)]
    field_more = [to_core(value) for value in field_got]

    wide = vmem((arms, 4 * block, rows, columns))
    whole = (arms, 2 * block, rows, columns)
    part = (arms, block, rows, columns)
    one = (block, rows, columns)
    factor, step_one, low, high, keep, give = call(
        forward_kernel,
        (f32((2, 4 * block, rows, columns)), f32(whole), f32(part), f32(part), f32(one), f32(one)),
        [wide, wide, wide, wide, vmem((2,) + one)],
        1,
        labels, starts, *start_got, fields, *field_got, *field_more,
        cost=8_000_000,
    )
    right = send(low, lambda x, c, p, h: (x, c, p - 1, h))
    left = send(high, lambda x, c, p, h: (x, c, p + 1, h))
    mine = keep * to_core(give)
    junction = mine
    for step, flip in other_chips(chips):
        junction = junction * send(
            mine, lambda x, c, p, h, step=step, flip=flip: (x + step, c, p, 1 - h if flip else h)
        )
    junction_other = to_core(junction)
    halo = send(junction, lambda x, c, p, h: (x, c, p + 2 * c - 1, h))
    halo_other = to_core(halo)

    total = jnp.sum(junction.reshape(-1, 8, columns), axis=0)
    total = total + to_core(total)
    if pairs & (pairs - 1) == 0:
        step = 1
        while step < pairs:
            total = total + send(total, lambda x, c, p, h, step=step: (x, c, p + step, h))
            step *= 2
    else:
        total = lax.psum(total, "space") / 2.0

    parts = (chips, 2, 2, block, owned, columns)
    keep, give = call(
        backward_kernel,
        (f32(parts), f32(parts)),
        [vmem((4 * block, rows, columns)), wide, wide, wide, wide, vmem(whole)],
        1,
        labels, factor, step_one, left, low, high, right, junction, junction_other, halo, halo_other,
        cost=8_000_000,
    )
    places = other_chips(chips)
    own, *gives = call(
        meet_kernel, (f32(parts[2:]),) * (1 + len(places)), [], 0, keep, to_core(give)
    )
    received = [
        send(value, lambda x, c, p, h, step=step, flip=flip: (x + step, c, p, 1 - h if flip else h))
        for value, (step, flip) in zip(gives, places)
    ]
    cell_count = block * space_size * rows * columns
    return call(
        functools.partial(final_kernel, cell_count, held * arm_size),
        (f32(parts[2:]), f32(parts[2:])),
        [],
        0,
        fields, total, own, *received,
    )


def solution(mesh):
    in_specs = (P(None, "space", None, None), P("arm", "space", None, None), P("arm"))
    out_specs = (P(None, "space", "arm", None), P(None, "space", "arm", None))
    return jax.shard_map(local, mesh=mesh, in_specs=in_specs, out_specs=out_specs, check_vma=False)
```

time: 143 us -> 83.2 us (0.58)
  blocking collectives: 27.8 us -> 0 us
  other arithmetic: 15.5 us -> 0.1 us
  Pallas kernels: 0 us -> 14.5 us
  between operations: 15.1 us -> 0.74 us
  waiting for transfers between devices: 48.9 us -> 39.5 us
  local copies, waits for them, and re-layouts: 10.2 us -> 2.07 us
    psum x1 -> x0, blocking collectives: 20.2 us -> none  [local(): partition_sum = lax.psum(jnp.sum(junction), 'space')]
    reduce_scatter x1 -> x0, waiting for transfers between devices: 17.9 us -> none  [local(): lax.psum_scatter(partial_value, 'arm', scatter_dimension=2, tiled=True)]
    pallas_call x0 -> x4, Pallas kernels: none -> 14.5 us  [call(): pl.pallas_call(kernel, out_shape=out_shape, in_specs=specs, out_specs=jax...]
    slice x53 -> x0, local copies, waits for them, and re-layouts: 9.16 us -> none  [the longest x24 5.7 us: stencil_inner(): beside = beside + jnp.roll(middle, 1, 3) + jnp.roll(middle, -1, 3)]
    ppermute x10 -> x25, waiting for transfers between devices: 31 us -> 39.5 us  [send(): return lax.ppermute(value, AXES, perm)]
    all_gather x1 -> x0, blocking collectives: 7.62 us -> none  [local(): gathered = lax.all_gather(own_product[None], 'arm', axis=0, tiled=True)]
    mul x11 -> x2, other arithmetic: 6.47 us -> 0.05 us  [the longest x1 0.03 us: local(): junction * send(mine, lambda x, c, p, h, step=step, flip=flip: (x + step,...]
    div x3 -> x0, other arithmetic: 2.94 us -> none  [the longest x2 2.85 us: extrapolate(): return (4.0 * halves - whole_step) / 3.0]
  transfers between devices with their start and end apart: 11 -> 25, of which waited for: 9 -> 15; matrix products, arithmetic and copies ran while one was open for 1% -> 1% of each run, Pallas kernels for 0% -> 0%
where the time goes in v1:
time: 83.2 us; the launch traced here: 83 us
  waiting for transfers between devices  39.5 us (47%)
  starting transfers between devices  26.2 us (31%)
  Pallas kernels  14.5 us (17%)
  local copies, waits for them, and re-layouts  2.07 us (2%)
    ppermute x25, waiting for transfers between devices, send(): return lax.ppermute(value, AXES, perm)  39.5 us
    ppermute x25, starting transfers between devices, send(): return lax.ppermute(value, AXES, perm)  26.2 us
    pallas_call x4, Pallas kernels, call(): pl.pallas_call(kernel, out_shape=out_shape, in_specs=specs, out_specs=jax...  14.5 us
  transfers between devices with their start and end apart: 25, of which 15 were waited for; matrix products, arithmetic and copies ran while one was open for 1% of the time, Pallas kernels for 0%

profile of v1, /device:TPU:0, one launch (start us, length us, event | category | flops | bytes accessed | tf_op | source)
XLA Modules:
  0.0 83.0 jit_solution(13561180781355469785)
XLA Ops:
  0.6 0.9 %dynamic-slice_bitcast_fusion = f32[4,64,128]{2,1,0:T(8,128)S(1)} fusion(f32[2,4,64,128]{3,2,1,0:T(8,128)} %fields.3, s32[]{:T(128)S(6)} %select_n.12), kind=kLoop, calls=%fused_computation.1 | loop fusion | bytes 262148 | tf_op jit(solution)/shard_map/jit(dynamic_index_in_dim)/squeeze | solution.py:272
  1.6 6.1 %collective-permute-start.5 = (f32[4,64,128]{2,1,0:T(8,128)S(1)}, f32[4,64,128]{2,1,0:T(8,128)S(1)}, u32[]{:S(2)}, u32[]{:S(2)}) collective-permute-start(f32[4,64,128]{2,1,0:T(8,128)S(1)} %dynamic-slice_bitcast_fusion), channel_id=1, source_target_pairs={{0,7},{1,2},{2,1},{3,4},{4,3},{5,6},{6,5},{7,0},{8,15},{9,10},{10,... | collective-permute-start | bytes 393224 | tf_op jit(solution)/shard_map/ppermute | solution.py:258
  7.6 0.4 collective-permute-start.4
  8.1 0.0 collective-permute-start.3
  8.1 0.0 copy-start
  8.1 0.0 copy-start.1
  8.1 1.1 %constant_dynamic-slice_fusion = (f32[2,4,64,128]{3,2,1,0:T(8,128)S(1)}, f32[2,4,64,128]{3,2,1,0:T(8,128)S(1)}) fusion(f32[4,4,64,128]{3,2,1,0:T(8,128)} %starts.1, s32[]{:T(128)S(6)} %select_n.11, s32[]{:T(128)S(6)} %select_n.10), kind=kLoop, calls=%fused_computation.2 | loop fusion | bytes 1048584 | tf_op jit(solution)/shard_map/dynamic_slice | solution.py:274
  9.2 0.0 copy-start.2
  9.2 1.9 %collective-permute-start.1 = (f32[2,4,64,128]{3,2,1,0:T(8,128)S(1)}, f32[2,4,64,128]{3,2,1,0:T(8,128)S(1)}, u32[]{:S(2)}, u32[]{:S(2)}) collective-permute-start(f32[2,4,64,128]{3,2,1,0:T(8,128)S(1)} %get-tuple-element.26), channel_id=1, source_target_pairs={{0,6},{1,3},{2,0},{3,5},{4,2},{5,7},{6,4},{7,1},{8,14},{9,11},{10,... | collective-permute-start | bytes 786440 | tf_op jit(solution)/shard_map/ppermute | solution.py:258
  11.2 0.8 collective-permute-done.5.f_across
  12.0 0.0 collective-permute-start.8
  12.0 4.8 %collective-permute-start.2 = (f32[2,4,64,128]{3,2,1,0:T(8,128)S(1)}, f32[2,4,64,128]{3,2,1,0:T(8,128)S(1)}, u32[]{:S(2)}, u32[]{:S(2)}) collective-permute-start(f32[2,4,64,128]{3,2,1,0:T(8,128)S(1)} %get-tuple-element.27), channel_id=1, source_target_pairs={{0,7},{1,2},{2,1},{3,4},{4,3},{5,6},{6,5},{7,0},{8,15},{9,10},{10,... | collective-permute-start | bytes 786440 | tf_op jit(solution)/shard_map/ppermute | solution.py:258
  16.7 0.0 collective-permute-done.4.f_straight
  16.7 0.0 collective-permute-start
  16.7 0.0 collective-permute-done.3.f_swap
  16.7 0.3 collective-permute-start.7
  17.0 0.0 collective-permute-done.8.g_across
  17.0 0.3 collective-permute-start.6
  17.3 0.8 %collective-permute-done.7.g_straight = f32[4,64,128]{2,1,0:T(8,128)S(1)} collective-permute-done((f32[4,64,128]{2,1,0:T(8,128)S(1)}, f32[4,64,128]{2,1,0:T(8,128)S(1)}, u32[]{:S(2)}, u32[]{:S(2)}) %collective-permute-start.7) | collective-permute-done | bytes 131104 | tf_op jit(solution)/shard_map/ppermute | solution.py:258
  18.1 0.2 collective-permute-done.6.g_swap
  18.4 1.6 %collective-permute-done.1.straight = f32[2,4,64,128]{3,2,1,0:T(8,128)S(1)} collective-permute-done((f32[2,4,64,128]{3,2,1,0:T(8,128)S(1)}, f32[2,4,64,128]{3,2,1,0:T(8,128)S(1)}, u32[]{:S(2)}, u32[]{:S(2)}) %collective-permute-start.1) | collective-permute-done | bytes 262176 | tf_op jit(solution)/shard_map/ppermute | solution.py:258
  20.0 5.5 %collective-permute-done.2.across = f32[2,4,64,128]{3,2,1,0:T(8,128)S(1)} collective-permute-done((f32[2,4,64,128]{3,2,1,0:T(8,128)S(1)}, f32[2,4,64,128]{3,2,1,0:T(8,128)S(1)}, u32[]{:S(2)}, u32[]{:S(2)}) %collective-permute-start.2) | collective-permute-done | bytes 262176 | tf_op jit(solution)/shard_map/ppermute | solution.py:258
  25.5 4.6 %collective-permute-done.swap = f32[2,4,64,128]{3,2,1,0:T(8,128)S(1)} collective-permute-done((f32[2,4,64,128]{3,2,1,0:T(8,128)S(1)}, f32[2,4,64,128]{3,2,1,0:T(8,128)S(1)}, u32[]{:S(2)}, u32[]{:S(2)}) %collective-permute-start) | collective-permute-done | bytes 262176 | tf_op jit(solution)/shard_map/ppermute | solution.py:258
  30.1 0.0 copy-done
  30.1 0.0 copy-done.1
  30.1 0.0 copy-done.2
  30.1 6.8 %shard_map.50 = (f32[2,16,64,128]{3,2,1,0:T(8,128)S(1)}, f32[2,8,64,128]{3,2,1,0:T(8,128)S(1)}, f32[2,4,64,128]{3,2,1,0:T(8,128)S(1)}, f32[2,4,64,128]{3,2,1,0:T...) custom-call(s32[4]{0:T(128)S(1)} %copy-done.2, f32[4,4,64,128]{3,2,1,0:T(8,128)S(1)} %copy-done, ...), custom_call_target="tpu_custom_call" | custom-call | flops 8000000 | bytes 8000000 | tf_op jit(solution)/shard_map/pallas_call | solution.py:231
  36.9 0.1 collective-permute-start.9
  37.0 1.3 %collective-permute-done.9 = f32[4,64,128]{2,1,0:T(8,128)S(1)} collective-permute-done((f32[4,64,128]{2,1,0:T(8,128)S(1)}, f32[4,64,128]{2,1,0:T(8,128)S(1)}, u32[]{:S(2)}, u32[]{:S(2)}) %collective-permute-start.9) | collective-permute-done | bytes 131104 | tf_op jit(solution)/shard_map/ppermute | solution.py:258
  38.3 1.2 %collective-permute-start.12 = (f32[4,64,128]{2,1,0:T(8,128)S(1)}, f32[4,64,128]{2,1,0:T(8,128)S(1)}, u32[]{:S(2)}, u32[]{:S(2)}) collective-permute-start(f32[4,64,128]{2,1,0:T(8,128)S(1)} %mul.20), channel_id=1, source_target_pairs={{0,17},{1,16},{2,19},{3,18},{4,21},{5,20},{6,23},{7,22},{8,25},{9,... | collective-permute-start | bytes 393224 | tf_op jit(solution)/shard_map/ppermute | solution.py:258
  39.5 0.5 collective-permute-start.11
  40.0 1.9 %collective-permute-start.10 = (f32[4,64,128]{2,1,0:T(8,128)S(1)}, f32[4,64,128]{2,1,0:T(8,128)S(1)}, u32[]{:S(2)}, u32[]{:S(2)}) collective-permute-start(f32[4,64,128]{2,1,0:T(8,128)S(1)} %mul.20), channel_id=1, source_target_pairs={{0,1},{1,0},{2,3},{3,2},{4,5},{5,4},{6,7},{7,6},{8,9},{9,8},{10,11... | collective-permute-start | bytes 393224 | tf_op jit(solution)/shard_map/ppermute | solution.py:258
  41.9 0.0 collective-permute-start.16
  41.9 3.8 %collective-permute-start.17 = (f32[2,4,64,128]{3,2,1,0:T(8,128)S(1)}, f32[2,4,64,128]{3,2,1,0:T(8,128)S(1)}, u32[]{:S(2)}, u32[]{:S(2)}) collective-permute-start(f32[2,4,64,128]{3,2,1,0:T(8,128)S(1)} %get-tuple-element.19.two_low), channel_id=1, source_target_pairs={{0,6},{1,7},{2,0},{3,1},{4,2},{5,3},{6,4},{7,5},{8,14},{9,15},{10,... | collective-permute-start | bytes 786440 | tf_op jit(solution)/shard_map/ppermute | solution.py:258
  45.7 0.0 collective-permute-done.12
  45.7 0.8 collective-permute-done.11
  46.5 1.1 %collective-permute-done.10 = f32[4,64,128]{2,1,0:T(8,128)S(1)} collective-permute-done((f32[4,64,128]{2,1,0:T(8,128)S(1)}, f32[4,64,128]{2,1,0:T(8,128)S(1)}, u32[]{:S(2)}, u32[]{:S(2)}) %collective-permute-start.10) | collective-permute-done | bytes 131104 | tf_op jit(solution)/shard_map/ppermute | solution.py:258
  47.7 0.2 collective-permute-start.19
  47.9 0.0 collective-permute-start.18
  47.9 9.7 %collective-permute-done.19.j_halo = f32[4,64,128]{2,1,0:T(8,128)S(1)} collective-permute-done((f32[4,64,128]{2,1,0:T(8,128)S(1)}, f32[4,64,128]{2,1,0:T(8,128)S(1)}, u32[]{:S(2)}, u32[]{:S(2)}) %collective-permute-start.19) | collective-permute-done | bytes 131104 | tf_op jit(solution)/shard_map/ppermute | solution.py:258
  57.6 0.1 collective-permute-start.20
  57.8 0.0 collective-permute-done.16.two_left
  57.8 0.0 collective-permute-done.17.two_right
  57.8 0.0 collective-permute-done.18.j_other
  57.8 1.2 %collective-permute-done.20.j_halo_other = f32[4,64,128]{2,1,0:T(8,128)S(1)} collective-permute-done((f32[4,64,128]{2,1,0:T(8,128)S(1)}, f32[4,64,128]{2,1,0:T(8,128)S(1)}, u32[]{:S(2)}, u32[]{:S(2)}) %collective-permute-start.20) | collective-permute-done | bytes 131104 | tf_op jit(solution)/shard_map/ppermute | solution.py:258
  59.0 6.8 %shard_map.51 = (f32[2,2,2,4,16,128]{5,4,3,2,1,0:T(8,128)S(1)}, f32[2,2,2,4,16,128]{5,4,3,2,1,0:T(8,128)S(1)}) custom-call(s32[4]{0:T(128)S(1)} %copy-done.2, f32[2,16,64,128]{3,2,1,0:T(8,128)S(1)} %get-tuple-element.16.u_ref, f32[2,8,64,128]{3,2,1,0:T(8,128)S(1)} %get-tuple-element.17.one_ref, f32[2,4,64,128]{3,2,1,0:T(8,128)S(1)} %collective-permute-done.16.two_left, ...), custom_call_target="tpu_custom_call" | custom-call | flops 8000000 | bytes 8000000 | tf_op jit(solution)/shard_map/pallas_call | solution.py:231
  65.8 0.2 collective-permute-start.21
  66.1 1.4 %collective-permute-done.21.received = f32[2,2,2,4,16,128]{5,4,3,2,1,0:T(8,128)S(1)} collective-permute-done((f32[2,2,2,4,16,128]{5,4,3,2,1,0:T(8,128)S(1)}, f32[2,2,2,4,16,128]{5,4,3,2,1,0:T(8,128)S(1)}, u32[]{:S(2)}, u32[]{:S(2)}) %collective-permute-start.21) | collective-permute-done | bytes 262176 | tf_op jit(solution)/shard_map/ppermute | solution.py:258
  67.5 0.5 collective-permute-start.22
  67.9 1.3 %collective-permute-start.23 = (f32[2,4,16,128]{3,2,1,0:T(8,128)S(1)}, f32[2,4,16,128]{3,2,1,0:T(8,128)S(1)}, u32[]{:S(2)}, u32[]{:S(2)}) collective-permute-start(f32[2,4,16,128]{3,2,1,0:T(8,128)S(1)} %get-tuple-element.24), channel_id=1, source_target_pairs={{0,16},{1,17},{2,18},{3,19},{4,20},{5,21},{6,22},{7,23},{8,24},{9,... | collective-permute-start | bytes 196616 | tf_op jit(solution)/shard_map/ppermute | solution.py:258
  69.2 1.8 %collective-permute-start.24 = (f32[2,4,16,128]{3,2,1,0:T(8,128)S(1)}, f32[2,4,16,128]{3,2,1,0:T(8,128)S(1)}, u32[]{:S(2)}, u32[]{:S(2)}) collective-permute-start(f32[2,4,16,128]{3,2,1,0:T(8,128)S(1)} %get-tuple-element.25), channel_id=1, source_target_pairs={{0,17},{1,16},{2,19},{3,18},{4,21},{5,20},{6,23},{7,22},{8,25},{9,... | collective-permute-start | bytes 196616 | tf_op jit(solution)/shard_map/ppermute | solution.py:258
  71.1 0.1 collective-permute-start.13
  71.1 1.2 %collective-permute-done.13 = f32[8,128]{1,0:T(8,128)S(1)} collective-permute-done((f32[8,128]{1,0:T(8,128)S(1)}, f32[8,128]{1,0:T(8,128)S(1)}, u32[]{:S(2)}, u32[]{:S(2)}) %collective-permute-start.13) | collective-permute-done | bytes 4128 | tf_op jit(solution)/shard_map/ppermute | solution.py:258
  72.3 0.0 collective-permute-start.14
  72.3 5.4 %collective-permute-done.14 = f32[8,128]{1,0:T(8,128)S(1)} collective-permute-done((f32[8,128]{1,0:T(8,128)S(1)}, f32[8,128]{1,0:T(8,128)S(1)}, u32[]{:S(2)}, u32[]{:S(2)}) %collective-permute-start.14) | collective-permute-done | bytes 4128 | tf_op jit(solution)/shard_map/ppermute | solution.py:258
  77.7 0.8 collective-permute-start.15
  78.5 3.7 %collective-permute-done.15 = f32[8,128]{1,0:T(8,128)S(1)} collective-permute-done((f32[8,128]{1,0:T(8,128)S(1)}, f32[8,128]{1,0:T(8,128)S(1)}, u32[]{:S(2)}, u32[]{:S(2)}) %collective-permute-start.15) | collective-permute-done | bytes 4128 | tf_op jit(solution)/shard_map/ppermute | solution.py:258
  82.2 0.0 collective-permute-done.22.refs_0_
  82.2 0.0 collective-permute-done.23.refs_1_
  82.2 0.0 collective-permute-done.24.refs_2_
  82.2 0.8 shard_map.53
  (7 shorter events, 0.1 us)
Async XLA Ops:
  1.6 10.4 %collective-permute-start.5 = (f32[4,64,128]{2,1,0:T(8,128)S(1)}, f32[4,64,128]{2,1,0:T(8,128)S(1)}, u32[]{:S(2)}, u32[]{:S(2)}) collective-permute-start(f32[4,64,128]{2,1,0:T(8,128)S(1)} %dynamic-slice_bitcast_fusion), channel_id=1, source_target_pairs={{0,7},{1,2},{2,1},{3,4},{4,3},{5,6},{6,5},{7,0},{8,15},{9,10},{10,... | collective-permute-start | bytes 393224 | tf_op jit(solution)/shard_map/ppermute | solution.py:258
  7.6 9.1 %collective-permute-start.4 = (f32[4,64,128]{2,1,0:T(8,128)S(1)}, f32[4,64,128]{2,1,0:T(8,128)S(1)}, u32[]{:S(2)}, u32[]{:S(2)}) collective-permute-start(f32[4,64,128]{2,1,0:T(8,128)S(1)} %dynamic-slice_bitcast_fusion), channel_id=1, source_target_pairs={{0,6},{1,3},{2,0},{3,5},{4,2},{5,7},{6,4},{7,1},{8,14},{9,11},{10,... | collective-permute-start | bytes 393224 | tf_op jit(solution)/shard_map/ppermute | solution.py:258
  8.1 8.6 %collective-permute-start.3 = (f32[4,64,128]{2,1,0:T(8,128)S(1)}, f32[4,64,128]{2,1,0:T(8,128)S(1)}, u32[]{:S(2)}, u32[]{:S(2)}) collective-permute-start(f32[4,64,128]{2,1,0:T(8,128)S(1)} %dynamic-slice_bitcast_fusion), channel_id=1, source_target_pairs={{0,1},{1,0},{2,3},{3,2},{4,5},{5,4},{6,7},{7,6},{8,9},{9,8},{10,11... | collective-permute-start | bytes 393224 | tf_op jit(solution)/shard_map/ppermute | solution.py:258
  8.1 22.0 %copy-start = (f32[4,4,64,128]{3,2,1,0:T(8,128)S(1)}, f32[4,4,64,128]{3,2,1,0:T(8,128)}, u32[]{:S(2)}) copy-start(f32[4,4,64,128]{3,2,1,0:T(8,128)} %starts.1) | copy-start | bytes 1572868
  8.1 22.0 %copy-start.1 = (f32[2,4,64,128]{3,2,1,0:T(8,128)S(1)}, f32[2,4,64,128]{3,2,1,0:T(8,128)}, u32[]{:S(2)}) copy-start(f32[2,4,64,128]{3,2,1,0:T(8,128)} %fields.3) | copy-start | bytes 786436
  9.2 20.8 %copy-start.2 = (s32[4]{0:T(128)S(1)}, s32[4]{0:T(128)}, u32[]{:S(2)}) copy-start(s32[4]{0:T(128)} %labels.3) | copy-start | bytes 52
  9.2 10.7 %collective-permute-start.1 = (f32[2,4,64,128]{3,2,1,0:T(8,128)S(1)}, f32[2,4,64,128]{3,2,1,0:T(8,128)S(1)}, u32[]{:S(2)}, u32[]{:S(2)}) collective-permute-start(f32[2,4,64,128]{3,2,1,0:T(8,128)S(1)} %get-tuple-element.26), channel_id=1, source_target_pairs={{0,6},{1,3},{2,0},{3,5},{4,2},{5,7},{6,4},{7,1},{8,14},{9,11},{10,... | collective-permute-start | bytes 786440 | tf_op jit(solution)/shard_map/ppermute | solution.py:258
  12.0 5.1 %collective-permute-start.8 = (f32[4,64,128]{2,1,0:T(8,128)S(1)}, f32[4,64,128]{2,1,0:T(8,128)S(1)}, u32[]{:S(2)}, u32[]{:S(2)}) collective-permute-start(f32[4,64,128]{2,1,0:T(8,128)S(1)} %collective-permute-done.5.f_across), channel_id=1, source_target_pairs={{0,8},{1,9},{2,10},{3,11},{4,12},{5,13},{6,14},{7,15},{8,0},{9,1},... | collective-permute-start | bytes 393224 | tf_op jit(solution)/shard_map/ppermute | solution.py:258
  12.0 13.5 %collective-permute-start.2 = (f32[2,4,64,128]{3,2,1,0:T(8,128)S(1)}, f32[2,4,64,128]{3,2,1,0:T(8,128)S(1)}, u32[]{:S(2)}, u32[]{:S(2)}) collective-permute-start(f32[2,4,64,128]{3,2,1,0:T(8,128)S(1)} %get-tuple-element.27), channel_id=1, source_target_pairs={{0,7},{1,2},{2,1},{3,4},{4,3},{5,6},{6,5},{7,0},{8,15},{9,10},{10,... | collective-permute-start | bytes 786440 | tf_op jit(solution)/shard_map/ppermute | solution.py:258
  16.7 13.4 %collective-permute-start = (f32[2,4,64,128]{3,2,1,0:T(8,128)S(1)}, f32[2,4,64,128]{3,2,1,0:T(8,128)S(1)}, u32[]{:S(2)}, u32[]{:S(2)}) collective-permute-start(f32[2,4,64,128]{3,2,1,0:T(8,128)S(1)} %get-tuple-element.27), channel_id=1, source_target_pairs={{0,1},{1,0},{2,3},{3,2},{4,5},{5,4},{6,7},{7,6},{8,9},{9,8},{10,11... | collective-permute-start | bytes 786440 | tf_op jit(solution)/shard_map/ppermute | solution.py:258
  16.7 1.4 %collective-permute-start.7 = (f32[4,64,128]{2,1,0:T(8,128)S(1)}, f32[4,64,128]{2,1,0:T(8,128)S(1)}, u32[]{:S(2)}, u32[]{:S(2)}) collective-permute-start(f32[4,64,128]{2,1,0:T(8,128)S(1)} %collective-permute-done.4.f_straight), channel_id=1, source_target_pairs={{0,8},{1,9},{2,10},{3,11},{4,12},{5,13},{6,14},{7,15},{8,0},{9,1},... | collective-permute-start | bytes 393224 | tf_op jit(solution)/shard_map/ppermute | solution.py:258
  17.0 1.3 %collective-permute-start.6 = (f32[4,64,128]{2,1,0:T(8,128)S(1)}, f32[4,64,128]{2,1,0:T(8,128)S(1)}, u32[]{:S(2)}, u32[]{:S(2)}) collective-permute-start(f32[4,64,128]{2,1,0:T(8,128)S(1)} %collective-permute-done.3.f_swap), channel_id=1, source_target_pairs={{0,8},{1,9},{2,10},{3,11},{4,12},{5,13},{6,14},{7,15},{8,0},{9,1},... | collective-permute-start | bytes 393224 | tf_op jit(solution)/shard_map/ppermute | solution.py:258
  36.9 1.4 %collective-permute-start.9 = (f32[4,64,128]{2,1,0:T(8,128)S(1)}, f32[4,64,128]{2,1,0:T(8,128)S(1)}, u32[]{:S(2)}, u32[]{:S(2)}) collective-permute-start(f32[4,64,128]{2,1,0:T(8,128)S(1)} %get-tuple-element.15), channel_id=1, source_target_pairs={{0,8},{1,9},{2,10},{3,11},{4,12},{5,13},{6,14},{7,15},{8,0},{9,1},... | collective-permute-start | bytes 393224 | tf_op jit(solution)/shard_map/ppermute | solution.py:258
  38.3 7.4 %collective-permute-start.12 = (f32[4,64,128]{2,1,0:T(8,128)S(1)}, f32[4,64,128]{2,1,0:T(8,128)S(1)}, u32[]{:S(2)}, u32[]{:S(2)}) collective-permute-start(f32[4,64,128]{2,1,0:T(8,128)S(1)} %mul.20), channel_id=1, source_target_pairs={{0,17},{1,16},{2,19},{3,18},{4,21},{5,20},{6,23},{7,22},{8,25},{9,... | collective-permute-start | bytes 393224 | tf_op jit(solution)/shard_map/ppermute | solution.py:258
  39.5 7.0 %collective-permute-start.11 = (f32[4,64,128]{2,1,0:T(8,128)S(1)}, f32[4,64,128]{2,1,0:T(8,128)S(1)}, u32[]{:S(2)}, u32[]{:S(2)}) collective-permute-start(f32[4,64,128]{2,1,0:T(8,128)S(1)} %mul.20), channel_id=1, source_target_pairs={{0,16},{1,17},{2,18},{3,19},{4,20},{5,21},{6,22},{7,23},{8,24},{9,... | collective-permute-start | bytes 393224 | tf_op jit(solution)/shard_map/ppermute | solution.py:258
  40.0 7.6 %collective-permute-start.10 = (f32[4,64,128]{2,1,0:T(8,128)S(1)}, f32[4,64,128]{2,1,0:T(8,128)S(1)}, u32[]{:S(2)}, u32[]{:S(2)}) collective-permute-start(f32[4,64,128]{2,1,0:T(8,128)S(1)} %mul.20), channel_id=1, source_target_pairs={{0,1},{1,0},{2,3},{3,2},{4,5},{5,4},{6,7},{7,6},{8,9},{9,8},{10,11... | collective-permute-start | bytes 393224 | tf_op jit(solution)/shard_map/ppermute | solution.py:258
  41.9 15.9 %collective-permute-start.16 = (f32[2,4,64,128]{3,2,1,0:T(8,128)S(1)}, f32[2,4,64,128]{3,2,1,0:T(8,128)S(1)}, u32[]{:S(2)}, u32[]{:S(2)}) collective-permute-start(f32[2,4,64,128]{3,2,1,0:T(8,128)S(1)} %get-tuple-element.18.two_high), channel_id=1, source_target_pairs={{0,2},{1,3},{2,4},{3,5},{4,6},{5,7},{6,0},{7,1},{8,10},{9,11},{10,... | collective-permute-start | bytes 786440 | tf_op jit(solution)/shard_map/ppermute | solution.py:258
  41.9 15.9 %collective-permute-start.17 = (f32[2,4,64,128]{3,2,1,0:T(8,128)S(1)}, f32[2,4,64,128]{3,2,1,0:T(8,128)S(1)}, u32[]{:S(2)}, u32[]{:S(2)}) collective-permute-start(f32[2,4,64,128]{3,2,1,0:T(8,128)S(1)} %get-tuple-element.19.two_low), channel_id=1, source_target_pairs={{0,6},{1,7},{2,0},{3,1},{4,2},{5,3},{6,4},{7,5},{8,14},{9,15},{10,... | collective-permute-start | bytes 786440 | tf_op jit(solution)/shard_map/ppermute | solution.py:258
  47.7 10.0 %collective-permute-start.19 = (f32[4,64,128]{2,1,0:T(8,128)S(1)}, f32[4,64,128]{2,1,0:T(8,128)S(1)}, u32[]{:S(2)}, u32[]{:S(2)}) collective-permute-start(f32[4,64,128]{2,1,0:T(8,128)S(1)} %multiply_multiply_fusion.j_mine), channel_id=1, source_target_pairs={{0,6},{1,7},{2,0},{3,1},{4,2},{5,3},{6,4},{7,5},{8,10},{9,11},{10,... | collective-permute-start | bytes 393224 | tf_op jit(solution)/shard_map/ppermute | solution.py:258
  47.9 9.9 %collective-permute-start.18 = (f32[4,64,128]{2,1,0:T(8,128)S(1)}, f32[4,64,128]{2,1,0:T(8,128)S(1)}, u32[]{:S(2)}, u32[]{:S(2)}) collective-permute-start(f32[4,64,128]{2,1,0:T(8,128)S(1)} %multiply_multiply_fusion.j_mine), channel_id=1, source_target_pairs={{0,8},{1,9},{2,10},{3,11},{4,12},{5,13},{6,14},{7,15},{8,0},{9,1},... | collective-permute-start | bytes 393224 | tf_op jit(solution)/shard_map/ppermute | solution.py:258
  57.6 1.3 %collective-permute-start.20 = (f32[4,64,128]{2,1,0:T(8,128)S(1)}, f32[4,64,128]{2,1,0:T(8,128)S(1)}, u32[]{:S(2)}, u32[]{:S(2)}) collective-permute-start(f32[4,64,128]{2,1,0:T(8,128)S(1)} %collective-permute-done.19.j_halo), channel_id=1, source_target_pairs={{0,8},{1,9},{2,10},{3,11},{4,12},{5,13},{6,14},{7,15},{8,0},{9,1},... | collective-permute-start | bytes 393224 | tf_op jit(solution)/shard_map/ppermute | solution.py:258
  65.8 1.6 %collective-permute-start.21 = (f32[2,2,2,4,16,128]{5,4,3,2,1,0:T(8,128)S(1)}, f32[2,2,2,4,16,128]{5,4,3,2,1,0:T(8,128)S(1)}, u32[]{:S(2)}, u32[]{:S(2)}) collective-permute-start(f32[2,2,2,4,16,128]{5,4,3,2,1,0:T(8,128)S(1)} %get-tuple-element.21), channel_id=1, source_target_pairs={{0,8},{1,9},{2,10},{3,11},{4,12},{5,13},{6,14},{7,15},{8,0},{9,1},... | collective-permute-start | bytes 786440 | tf_op jit(solution)/shard_map/ppermute | solution.py:258
  67.5 14.7 %collective-permute-start.22 = (f32[2,4,16,128]{3,2,1,0:T(8,128)S(1)}, f32[2,4,16,128]{3,2,1,0:T(8,128)S(1)}, u32[]{:S(2)}, u32[]{:S(2)}) collective-permute-start(f32[2,4,16,128]{3,2,1,0:T(8,128)S(1)} %get-tuple-element.23), channel_id=1, source_target_pairs={{0,1},{1,0},{2,3},{3,2},{4,5},{5,4},{6,7},{7,6},{8,9},{9,8},{10,11... | collective-permute-start | bytes 196616 | tf_op jit(solution)/shard_map/ppermute | solution.py:258
  67.9 14.3 %collective-permute-start.23 = (f32[2,4,16,128]{3,2,1,0:T(8,128)S(1)}, f32[2,4,16,128]{3,2,1,0:T(8,128)S(1)}, u32[]{:S(2)}, u32[]{:S(2)}) collective-permute-start(f32[2,4,16,128]{3,2,1,0:T(8,128)S(1)} %get-tuple-element.24), channel_id=1, source_target_pairs={{0,16},{1,17},{2,18},{3,19},{4,20},{5,21},{6,22},{7,23},{8,24},{9,... | collective-permute-start | bytes 196616 | tf_op jit(solution)/shard_map/ppermute | solution.py:258
  69.2 13.0 %collective-permute-start.24 = (f32[2,4,16,128]{3,2,1,0:T(8,128)S(1)}, f32[2,4,16,128]{3,2,1,0:T(8,128)S(1)}, u32[]{:S(2)}, u32[]{:S(2)}) collective-permute-start(f32[2,4,16,128]{3,2,1,0:T(8,128)S(1)} %get-tuple-element.25), channel_id=1, source_target_pairs={{0,17},{1,16},{2,19},{3,18},{4,21},{5,20},{6,23},{7,22},{8,25},{9,... | collective-permute-start | bytes 196616 | tf_op jit(solution)/shard_map/ppermute | solution.py:258
  71.1 1.2 %collective-permute-start.13 = (f32[8,128]{1,0:T(8,128)S(1)}, f32[8,128]{1,0:T(8,128)S(1)}, u32[]{:S(2)}, u32[]{:S(2)}) collective-permute-start(f32[8,128]{1,0:T(8,128)S(1)} %reduce_sum.9), channel_id=1, source_target_pairs={{0,8},{1,9},{2,10},{3,11},{4,12},{5,13},{6,14},{7,15},{8,0},{9,1},... | collective-permute-start | bytes 12296 | tf_op jit(solution)/shard_map/ppermute | solution.py:258
  72.3 5.4 %collective-permute-start.14 = (f32[8,128]{1,0:T(8,128)S(1)}, f32[8,128]{1,0:T(8,128)S(1)}, u32[]{:S(2)}, u32[]{:S(2)}) collective-permute-start(f32[8,128]{1,0:T(8,128)S(1)} %add.22), channel_id=1, source_target_pairs={{0,2},{1,3},{2,4},{3,5},{4,6},{5,7},{6,0},{7,1},{8,10},{9,11},{10,... | collective-permute-start | bytes 12296 | tf_op jit(solution)/shard_map/ppermute | solution.py:258
  77.7 4.5 %collective-permute-start.15 = (f32[8,128]{1,0:T(8,128)S(1)}, f32[8,128]{1,0:T(8,128)S(1)}, u32[]{:S(2)}, u32[]{:S(2)}) collective-permute-start(f32[8,128]{1,0:T(8,128)S(1)} %add.23), channel_id=1, source_target_pairs={{0,4},{1,5},{2,6},{3,7},{4,0},{5,1},{6,2},{7,3},{8,12},{9,13},{10,... | collective-permute-start | bytes 12296 | tf_op jit(solution)/shard_map/ppermute | solution.py:258

commit v2 on v1

--- a/solution.py
+++ b/solution.py
@@ -50,19 +50,34 @@
             whole = (centre_full / 3.0) * t + (coupling_full / 3.0) * t_around
             store(j, i, u * (halves - u * whole))
 
-    lax.fori_loop(first, last, scale, None)
-    lax.fori_loop(first + 1, last - 1, inner, None)
-    lax.fori_loop(first + 2, last - 2, outer, None)
+    lax.fori_loop(first, last, scale, None, unroll=4)
+    lax.fori_loop(first + 1, last - 1, inner, None, unroll=4)
+    lax.fori_loop(first + 2, last - 2, outer, None, unroll=4)
+
+
+def pack_kernel(starts, fields, own_ref, other_ref, sems):
+    arms = starts.shape[0] // 2
+    side = lax.rem(lax.axis_index("space"), 2)
+    core = lax.rem(lax.axis_index("arm"), 2)
+    copies = []
+    for k, (out_ref, at) in enumerate(((other_ref, 1 - side), (own_ref, side))):
+        copies.append(
+            pltpu.make_async_copy(starts.at[pl.ds(at * arms, arms)], out_ref.at[pl.ds(0, arms)], sems.at[2 * k])
+        )
+        copies.append(pltpu.make_async_copy(fields.at[core], out_ref.at[arms], sems.at[2 * k + 1]))
+    for copy in copies:
+        copy.start()
+    for copy in copies:
+        copy.wait()
 
 
 def forward_kernel(
-    labels, starts, swap, straight, across, fields,
-    f_swap, f_straight, f_across, g_swap, g_straight, g_across,
+    labels, starts, fields, swap, straight, across, g_swap, g_straight, g_across,
     u_ref, one_ref, low_ref, high_ref, keep_ref, send_ref,
     q_ref, p_ref, t_ref, s_ref, product_ref,
 ):
     block = starts.shape[1]
-    arms = swap.shape[0]
+    arms = starts.shape[0] // 2
     side = lax.rem(lax.axis_index("space"), 2)
     core = lax.rem(lax.axis_index("arm"), 2)
     own_at, swap_at = block + side * block, 2 * block - side * block
@@ -75,12 +90,12 @@
         for kind in range(2):
             u_ref[kind, own_at + i] = gain(fields[kind, i])
         for at, mine, other in (
-            (swap_at, f_swap, g_swap),
-            (straight_at, f_straight, g_straight),
-            (across_at, f_across, g_across),
+            (swap_at, swap, g_swap),
+            (straight_at, straight, g_straight),
+            (across_at, across, g_across),
         ):
-            u_ref[core, at + i] = gain(mine[i])
-            u_ref[1 - core, at + i] = gain(other[i])
+            u_ref[core, at + i] = gain(mine[arms, i])
+            u_ref[1 - core, at + i] = gain(other[arms, i])
         for j in range(arms):
             q_ref[j, own_at + i] = starts[side * arms + j, i]
             q_ref[j, swap_at + i] = swap[j, i]
@@ -123,13 +138,15 @@
 def backward_kernel(
     labels, u_ref, one_ref, two_left, two_low, two_high, two_right,
     j_mine, j_other, j_halo, j_halo_other,
-    keep_ref, send_ref,
+    keep_ref, send_ref, total_ref,
     junction_ref, q_ref, p_ref, t_ref, s_ref, density_ref,
 ):
     arms, block = two_low.shape[0], two_low.shape[1]
     side = lax.rem(lax.axis_index("space"), 2)
     core = lax.rem(lax.axis_index("arm"), 2)
     kinds = [labels[side * arms + j] for j in range(arms)]
+
+    total_ref[...] = jnp.zeros_like(total_ref)
 
     def fill(i, _):
         junction_ref[block + core * block + i] = j_mine[i]
@@ -138,6 +155,7 @@
         junction_ref[3 * block * core + i] = j_halo_other[i]
         for place, two in enumerate((two_left, two_low, two_high, two_right)):
             whole = junction_ref[place * block + i]
+            total_ref[...] += jnp.sum(whole.reshape(-1, *total_ref.shape), axis=0)
             for j in range(arms):
                 q_ref[j, place * block + i] = whole / two[j, i]
 
@@ -269,12 +287,19 @@
     def to_across(value):
         return send(value, lambda x, c, p, h: (x, c, p + 2 * h - 1, 1 - h))
 
-    field_own = lax.dynamic_index_in_dim(fields, core, 0, keepdims=False)
-    field_got = [to_side(field_own), to_straight(field_own), to_across(field_own)]
-    start_own = lax.dynamic_slice_in_dim(starts, side * arms, arms, 0)
-    start_other = lax.dynamic_slice_in_dim(starts, (1 - side) * arms, arms, 0)
-    start_got = [to_side(start_other), to_straight(start_own), to_across(start_other)]
-    field_more = [to_core(value) for value in field_got]
+    message = f32((arms + 1, block, rows, columns))
+    own_set, other_set = pl.pallas_call(
+        pack_kernel,
+        out_shape=(message, message),
+        in_specs=[pl.BlockSpec(memory_space=pl.ANY)] * 2,
+        out_specs=[pl.BlockSpec(memory_space=pltpu.VMEM)] * 2,
+        scratch_shapes=[pltpu.SemaphoreType.DMA((4,))],
+    )(starts, fields)
+    across = to_across(other_set)
+    swap = to_side(other_set)
+    straight = to_straight(own_set)
+    got = [swap, straight, across]
+    got_more = [to_core(value) for value in got]
 
     wide = vmem((arms, 4 * block, rows, columns))
     whole = (arms, 2 * block, rows, columns)
@@ -285,7 +310,7 @@
         (f32((2, 4 * block, rows, columns)), f32(whole), f32(part), f32(part), f32(one), f32(one)),
         [wide, wide, wide, wide, vmem((2,) + one)],
         1,
-        labels, starts, *start_got, fields, *field_got, *field_more,
+        labels, starts, fields, *got, *got_more,
         cost=8_000_000,
     )
     right = send(low, lambda x, c, p, h: (x, c, p - 1, h))
@@ -296,29 +321,27 @@
         junction = junction * send(
             mine, lambda x, c, p, h, step=step, flip=flip: (x + step, c, p, 1 - h if flip else h)
         )
-    junction_other = to_core(junction)
     halo = send(junction, lambda x, c, p, h: (x, c, p + 2 * c - 1, h))
+    held_junction, left, right = lax.optimization_barrier((junction, left, right))
+    junction_other = to_core(held_junction)
     halo_other = to_core(halo)
 
-    total = jnp.sum(junction.reshape(-1, 8, columns), axis=0)
-    total = total + to_core(total)
-    if pairs & (pairs - 1) == 0:
-        step = 1
-        while step < pairs:
-            total = total + send(total, lambda x, c, p, h, step=step: (x, c, p + step, h))
-            step *= 2
-    else:
-        total = lax.psum(total, "space") / 2.0
-
     parts = (chips, 2, 2, block, owned, columns)
-    keep, give = call(
+    keep, give, total = call(
         backward_kernel,
-        (f32(parts), f32(parts)),
+        (f32(parts), f32(parts), f32((8, columns))),
         [vmem((4 * block, rows, columns)), wide, wide, wide, wide, vmem(whole)],
         1,
         labels, factor, step_one, left, low, high, right, junction, junction_other, halo, halo_other,
         cost=8_000_000,
     )
+    if pairs & (pairs - 1) == 0:
+        step = 2
+        while step < pairs:
+            total = total + send(total, lambda x, c, p, h, step=step: (x, c, p + step, h))
+            step *= 2
+    else:
+        total = lax.psum(total, "space") / 4.0
     places = other_chips(chips)
     own, *gives = call(
         meet_kernel, (f32(parts[2:]),) * (1 + len(places)), [], 0, keep, to_core(give)

time: 83.2 us -> 71.8 us (0.86)
  waiting for transfers between devices: 39.5 us -> 35.9 us
  starting transfers between devices: 26.2 us -> 22.9 us
  Pallas kernels: 14.5 us -> 12 us
  local copies, waits for them, and re-layouts: 2.07 us -> 0.01 us
    pallas_call x4, Pallas kernels: 14.5 us -> 9.92 us  [call(): pl.pallas_call(kernel, out_shape=out_shape, in_specs=specs, out_specs=jax...]
    ppermute x25 -> x20, waiting for transfers between devices: 39.5 us -> 35.9 us  [send(): return lax.ppermute(value, AXES, perm)]
    ppermute x25 -> x20, starting transfers between devices: 26.2 us -> 22.9 us  [send(): return lax.ppermute(value, AXES, perm)]
    pallas_call x0 -> x1, Pallas kernels: none -> 2.13 us  [local(): pl.pallas_call(pack_kernel, out_shape=(message, message), in_specs=[pl.Bl...]
    dynamic_slice x1 -> x0, local copies, waits for them, and re-layouts: 1.14 us -> none  [local(): start_own = lax.dynamic_slice_in_dim(starts, side * arms, arms, 0)]
    squeeze x1 -> x0, local copies, waits for them, and re-layouts: 0.92 us -> none  [local(): field_own = lax.dynamic_index_in_dim(fields, core, 0, keepdims=False)]
  transfers between devices with their start and end apart: 25 -> 20, of which waited for: 15 -> 14; matrix products, arithmetic and copies ran while one was open for 1% -> 0% of each run, Pallas kernels for 0% -> 0%
where the time goes in v2:
time: 71.8 us; the launch traced here: 71.6 us
  waiting for transfers between devices  35.9 us (50%)
  starting transfers between devices  22.9 us (32%)
  Pallas kernels  12 us (17%)
  between operations  0.72 us (1%)
    ppermute x20, waiting for transfers between devices, send(): return lax.ppermute(value, AXES, perm)  35.9 us
    ppermute x20, starting transfers between devices, send(): return lax.ppermute(value, AXES, perm)  22.9 us
    pallas_call x4, Pallas kernels, call(): pl.pallas_call(kernel, out_shape=out_shape, in_specs=specs, out_specs=jax...  9.92 us
    pallas_call x1, Pallas kernels, local(): pl.pallas_call(pack_kernel, out_shape=(message, message), in_specs=[pl.Bl...  2.13 us
  transfers between devices with their start and end apart: 20, of which 14 were waited for; matrix products, arithmetic and copies ran while one was open for 0% of the time, Pallas kernels for 0%

profile of v2, /device:TPU:0, one launch (start us, length us, event | category | flops | bytes accessed | tf_op | source)
XLA Modules:
  0.0 71.6 jit_solution(5841023918028801499)
XLA Ops:
  0.6 0.0 copy-start
  0.6 0.0 copy-start.1
  0.6 2.1 %shard_map.50 = (f32[3,4,64,128]{3,2,1,0:T(8,128)}, f32[3,4,64,128]{3,2,1,0:T(8,128)}) custom-call(f32[4,4,64,128]{3,2,1,0:T(8,128)} %starts.3, f32[2,4,64,128]{3,2,1,0:T(8,128)} %fields.5), custom_call_target="tpu_custom_call" | custom-call | tf_op jit(solution)/shard_map/pallas_call | solution.py:291
  2.8 0.0 copy-start.2
  2.8 5.1 %collective-permute-start.1 = (f32[3,4,64,128]{3,2,1,0:T(8,128)}, f32[3,4,64,128]{3,2,1,0:T(8,128)S(1)}, u32[]{:S(2)}, u32[]{:S(2)}) collective-permute-start(f32[3,4,64,128]{3,2,1,0:T(8,128)} %get-tuple-element.21), channel_id=1, source_target_pairs={{0,6},{1,3},{2,0},{3,5},{4,2},{5,7},{6,4},{7,1},{8,14},{9,11},{10,... | collective-permute-start | bytes 1179656 | tf_op jit(solution)/shard_map/ppermute | solution.py:276
  7.9 1.2 %collective-permute-start.2 = (f32[3,4,64,128]{3,2,1,0:T(8,128)}, f32[3,4,64,128]{3,2,1,0:T(8,128)S(1)}, u32[]{:S(2)}, u32[]{:S(2)}) collective-permute-start(f32[3,4,64,128]{3,2,1,0:T(8,128)} %get-tuple-element.20), channel_id=1, source_target_pairs={{0,7},{1,2},{2,1},{3,4},{4,3},{5,6},{6,5},{7,0},{8,15},{9,10},{10,... | collective-permute-start | bytes 1179656 | tf_op jit(solution)/shard_map/ppermute | solution.py:276
  9.1 0.0 collective-permute-start
  9.1 8.7 %collective-permute-done.1.straight = f32[3,4,64,128]{3,2,1,0:T(8,128)S(1)} collective-permute-done((f32[3,4,64,128]{3,2,1,0:T(8,128)}, f32[3,4,64,128]{3,2,1,0:T(8,128)S(1)}, u32[]{:S(2)}, u32[]{:S(2)}) %collective-permute-start.1) | collective-permute-done | bytes 393248 | tf_op jit(solution)/shard_map/ppermute | solution.py:276
  17.7 0.0 collective-permute-start.4
  17.7 9.0 %collective-permute-done.2.across = f32[3,4,64,128]{3,2,1,0:T(8,128)S(1)} collective-permute-done((f32[3,4,64,128]{3,2,1,0:T(8,128)}, f32[3,4,64,128]{3,2,1,0:T(8,128)S(1)}, u32[]{:S(2)}, u32[]{:S(2)}) %collective-permute-start.2) | collective-permute-done | bytes 393248 | tf_op jit(solution)/shard_map/ppermute | solution.py:276
  26.7 0.0 collective-permute-start.5
  26.7 1.4 %collective-permute-done.swap = f32[3,4,64,128]{3,2,1,0:T(8,128)S(1)} collective-permute-done((f32[3,4,64,128]{3,2,1,0:T(8,128)}, f32[3,4,64,128]{3,2,1,0:T(8,128)S(1)}, u32[]{:S(2)}, u32[]{:S(2)}) %collective-permute-start) | collective-permute-done | bytes 393248 | tf_op jit(solution)/shard_map/ppermute | solution.py:276
  28.1 0.0 collective-permute-start.3
  28.1 0.0 collective-permute-done.4.g_straight
  28.2 0.3 collective-permute-done.5.g_across
  28.4 1.4 %collective-permute-done.3.g_swap = f32[3,4,64,128]{3,2,1,0:T(8,128)S(1)} collective-permute-done((f32[3,4,64,128]{3,2,1,0:T(8,128)S(1)}, f32[3,4,64,128]{3,2,1,0:T(8,128)S(1)}, u32[]{:S(2)}, u32[]{:S(2)}) %collective-permute-start.3) | collective-permute-done | bytes 393248 | tf_op jit(solution)/shard_map/ppermute | solution.py:276
  29.9 0.0 copy-done
  29.9 0.0 copy-done.1
  29.9 0.0 copy-done.2
  29.9 4.5 %shard_map.51 = (f32[2,16,64,128]{3,2,1,0:T(8,128)S(1)}, f32[2,8,64,128]{3,2,1,0:T(8,128)S(1)}, f32[2,4,64,128]{3,2,1,0:T(8,128)S(1)}, f32[2,4,64,128]{3,2,1,0:T...) custom-call(s32[4]{0:T(128)S(1)} %copy-done.2, f32[4,4,64,128]{3,2,1,0:T(8,128)S(1)} %copy-done.1, ...), custom_call_target="tpu_custom_call" | custom-call | flops 8000000 | bytes 8000000 | tf_op jit(solution)/shard_map/pallas_call | solution.py:249
  34.4 0.2 collective-permute-start.6
  34.6 1.2 %collective-permute-done.6 = f32[4,64,128]{2,1,0:T(8,128)S(1)} collective-permute-done((f32[4,64,128]{2,1,0:T(8,128)S(1)}, f32[4,64,128]{2,1,0:T(8,128)S(1)}, u32[]{:S(2)}, u32[]{:S(2)}) %collective-permute-start.6) | collective-permute-done | bytes 131104 | tf_op jit(solution)/shard_map/ppermute | solution.py:276
  35.8 1.3 %collective-permute-start.9 = (f32[4,64,128]{2,1,0:T(8,128)S(1)}, f32[4,64,128]{2,1,0:T(8,128)S(1)}, u32[]{:S(2)}, u32[]{:S(2)}) collective-permute-start(f32[4,64,128]{2,1,0:T(8,128)S(1)} %mul.12), channel_id=1, source_target_pairs={{0,17},{1,16},{2,19},{3,18},{4,21},{5,20},{6,23},{7,22},{8,25},{9,... | collective-permute-start | bytes 393224 | tf_op jit(solution)/shard_map/ppermute | solution.py:276
  37.1 0.5 collective-permute-start.8
  37.7 1.7 %collective-permute-start.7 = (f32[4,64,128]{2,1,0:T(8,128)S(1)}, f32[4,64,128]{2,1,0:T(8,128)S(1)}, u32[]{:S(2)}, u32[]{:S(2)}) collective-permute-start(f32[4,64,128]{2,1,0:T(8,128)S(1)} %mul.12), channel_id=1, source_target_pairs={{0,1},{1,0},{2,3},{3,2},{4,5},{5,4},{6,7},{7,6},{8,9},{9,8},{10,11... | collective-permute-start | bytes 393224 | tf_op jit(solution)/shard_map/ppermute | solution.py:276
  39.4 0.0 collective-permute-start.10
  39.4 3.8 %collective-permute-start.11 = (f32[2,4,64,128]{3,2,1,0:T(8,128)S(1)}, f32[2,4,64,128]{3,2,1,0:T(8,128)S(1)}, u32[]{:S(2)}, u32[]{:S(2)}) collective-permute-start(f32[2,4,64,128]{3,2,1,0:T(8,128)S(1)} %get-tuple-element.27.two_low), channel_id=1, source_target_pairs={{0,6},{1,7},{2,0},{3,1},{4,2},{5,3},{6,4},{7,5},{8,14},{9,15},{10,... | collective-permute-start | bytes 786440 | tf_op jit(solution)/shard_map/ppermute | solution.py:276
  43.2 0.0 collective-permute-done.9
  43.2 0.8 %collective-permute-done.8 = f32[4,64,128]{2,1,0:T(8,128)S(1)} collective-permute-done((f32[4,64,128]{2,1,0:T(8,128)S(1)}, f32[4,64,128]{2,1,0:T(8,128)S(1)}, u32[]{:S(2)}, u32[]{:S(2)}) %collective-permute-start.8) | collective-permute-done | bytes 131104 | tf_op jit(solution)/shard_map/ppermute | solution.py:276
  44.0 1.1 %collective-permute-done.7 = f32[4,64,128]{2,1,0:T(8,128)S(1)} collective-permute-done((f32[4,64,128]{2,1,0:T(8,128)S(1)}, f32[4,64,128]{2,1,0:T(8,128)S(1)}, u32[]{:S(2)}, u32[]{:S(2)}) %collective-permute-start.7) | collective-permute-done | bytes 131104 | tf_op jit(solution)/shard_map/ppermute | solution.py:276
  45.2 2.6 %collective-permute-start.13 = (f32[4,64,128]{2,1,0:T(8,128)S(1)}, f32[4,64,128]{2,1,0:T(8,128)S(1)}, u32[]{:S(2)}, u32[]{:S(2)}) collective-permute-start(f32[4,64,128]{2,1,0:T(8,128)S(1)} %multiply_multiply_fusion.j_mine), channel_id=1, source_target_pairs={{0,6},{1,7},{2,0},{3,1},{4,2},{5,3},{6,4},{7,5},{8,10},{9,11},{10,... | collective-permute-start | bytes 393224 | tf_op jit(solution)/shard_map/ppermute | solution.py:276
  47.8 2.7 %collective-permute-done.10.two_left = f32[2,4,64,128]{3,2,1,0:T(8,128)S(1)} collective-permute-done((f32[2,4,64,128]{3,2,1,0:T(8,128)S(1)}, f32[2,4,64,128]{3,2,1,0:T(8,128)S(1)}, u32[]{:S(2)}, u32[]{:S(2)}) %collective-permute-start.10) | collective-permute-done | bytes 262176 | tf_op jit(solution)/shard_map/ppermute | solution.py:276
  50.4 2.1 %collective-permute-done.11.two_right = f32[2,4,64,128]{3,2,1,0:T(8,128)S(1)} collective-permute-done((f32[2,4,64,128]{3,2,1,0:T(8,128)S(1)}, f32[2,4,64,128]{3,2,1,0:T(8,128)S(1)}, u32[]{:S(2)}, u32[]{:S(2)}) %collective-permute-start.11) | collective-permute-done | bytes 262176 | tf_op jit(solution)/shard_map/ppermute | solution.py:276
  52.5 0.0 collective-permute-start.12
  52.5 2.6 %collective-permute-done.13.j_halo = f32[4,64,128]{2,1,0:T(8,128)S(1)} collective-permute-done((f32[4,64,128]{2,1,0:T(8,128)S(1)}, f32[4,64,128]{2,1,0:T(8,128)S(1)}, u32[]{:S(2)}, u32[]{:S(2)}) %collective-permute-start.13) | collective-permute-done | bytes 131104 | tf_op jit(solution)/shard_map/ppermute | solution.py:276
  55.2 0.1 collective-permute-start.14
  55.3 0.0 collective-permute-done.12.j_other
  55.3 1.2 %collective-permute-done.14.j_halo_other = f32[4,64,128]{2,1,0:T(8,128)S(1)} collective-permute-done((f32[4,64,128]{2,1,0:T(8,128)S(1)}, f32[4,64,128]{2,1,0:T(8,128)S(1)}, u32[]{:S(2)}, u32[]{:S(2)}) %collective-permute-start.14) | collective-permute-done | bytes 131104 | tf_op jit(solution)/shard_map/ppermute | solution.py:276
  56.5 4.6 %shard_map.52 = (f32[2,2,2,4,16,128]{5,4,3,2,1,0:T(8,128)S(1)}, f32[2,2,2,4,16,128]{5,4,3,2,1,0:T(8,128)S(1)}, f32[8,128]{1,0:T(8,128)S(1)}) custom-call(s32[4]{0:T(128)S(1)} %copy-done.2, f32[2,16,64,128]{3,2,1,0:T(8,128)S(1)} %get-tuple-element.22.u_ref, f32[2,8,64,128]{3,2,1,0:T(8,128)S(1)} %get-tuple-element.23.one_ref, ...), custom_call_target="tpu_custom_call" | custom-call | flops 8000000 | bytes 8000000 | tf_op jit(solution)/shard_map/pallas_call | solution.py:249
  61.1 0.2 collective-permute-start.16
  61.3 1.4 %collective-permute-done.16.received = f32[2,2,2,4,16,128]{5,4,3,2,1,0:T(8,128)S(1)} collective-permute-done((f32[2,2,2,4,16,128]{5,4,3,2,1,0:T(8,128)S(1)}, f32[2,2,2,4,16,128]{5,4,3,2,1,0:T(8,128)S(1)}, u32[]{:S(2)}, u32[]{:S(2)}) %collective-permute-start.16) | collective-permute-done | bytes 262176 | tf_op jit(solution)/shard_map/ppermute | solution.py:276
  62.7 0.4 collective-permute-start.17
  63.1 1.5 %collective-permute-start.18 = (f32[2,4,16,128]{3,2,1,0:T(8,128)S(1)}, f32[2,4,16,128]{3,2,1,0:T(8,128)S(1)}, u32[]{:S(2)}, u32[]{:S(2)}) collective-permute-start(f32[2,4,16,128]{3,2,1,0:T(8,128)S(1)} %get-tuple-element.36), channel_id=1, source_target_pairs={{0,16},{1,17},{2,18},{3,19},{4,20},{5,21},{6,22},{7,23},{8,24},{9,... | collective-permute-start | bytes 196616 | tf_op jit(solution)/shard_map/ppermute | solution.py:276
  64.6 1.7 %collective-permute-start.19 = (f32[2,4,16,128]{3,2,1,0:T(8,128)S(1)}, f32[2,4,16,128]{3,2,1,0:T(8,128)S(1)}, u32[]{:S(2)}, u32[]{:S(2)}) collective-permute-start(f32[2,4,16,128]{3,2,1,0:T(8,128)S(1)} %get-tuple-element.37), channel_id=1, source_target_pairs={{0,17},{1,16},{2,19},{3,18},{4,21},{5,20},{6,23},{7,22},{8,25},{9,... | collective-permute-start | bytes 196616 | tf_op jit(solution)/shard_map/ppermute | solution.py:276
  66.3 2.6 %collective-permute-start.15 = (f32[8,128]{1,0:T(8,128)S(1)}, f32[8,128]{1,0:T(8,128)S(1)}, u32[]{:S(2)}, u32[]{:S(2)}) collective-permute-start(f32[8,128]{1,0:T(8,128)S(1)} %get-tuple-element.31), channel_id=1, source_target_pairs={{0,4},{1,5},{2,6},{3,7},{4,0},{5,1},{6,2},{7,3},{8,12},{9,13},{10,... | collective-permute-start | bytes 12296 | tf_op jit(solution)/shard_map/ppermute | solution.py:276
  68.9 1.9 %collective-permute-done.15 = f32[8,128]{1,0:T(8,128)S(1)} collective-permute-done((f32[8,128]{1,0:T(8,128)S(1)}, f32[8,128]{1,0:T(8,128)S(1)}, u32[]{:S(2)}, u32[]{:S(2)}) %collective-permute-start.15) | collective-permute-done | bytes 4128 | tf_op jit(solution)/shard_map/ppermute | solution.py:276
  70.8 0.0 collective-permute-done.17.refs_0_
  70.8 0.0 collective-permute-done.18.refs_1_
  70.8 0.0 collective-permute-done.19.refs_2_
  70.8 0.8 %shard_map.54 = (f32[2,4,16,128]{3,2,1,0:T(8,128)}, f32[2,4,16,128]{3,2,1,0:T(8,128)}) custom-call(f32[2,4,64,128]{3,2,1,0:T(8,128)S(1)} %copy-done, f32[8,128]{1,0:T(8,128)S(1)} %add.3.total, f32[2,4,16,128]{3,2,1,0:T(8,128)S(1)} %get-tuple-element.34.own, f32[2,4,16,128]{3,2,1,0:T(8,128)S(1)} %collective-permute-done.17.refs_0_, ...), custom_call_target="tpu_custom_call" | custom-call | flops 1000000 | bytes 1000000 | tf_op jit(solution)/shard_map/pallas_call | solution.py:249
  (4 shorter events, 0.1 us)
Async XLA Ops:
  0.6 29.2 %copy-start = (f32[2,4,64,128]{3,2,1,0:T(8,128)S(1)}, f32[2,4,64,128]{3,2,1,0:T(8,128)}, u32[]{:S(2)}) copy-start(f32[2,4,64,128]{3,2,1,0:T(8,128)} %fields.5) | copy-start | bytes 786436
  0.6 29.2 %copy-start.1 = (f32[4,4,64,128]{3,2,1,0:T(8,128)S(1)}, f32[4,4,64,128]{3,2,1,0:T(8,128)}, u32[]{:S(2)}) copy-start(f32[4,4,64,128]{3,2,1,0:T(8,128)} %starts.3) | copy-start | bytes 1572868
  2.8 27.1 %copy-start.2 = (s32[4]{0:T(128)S(1)}, s32[4]{0:T(128)}, u32[]{:S(2)}) copy-start(s32[4]{0:T(128)} %labels.3) | copy-start | bytes 52
  2.8 14.9 %collective-permute-start.1 = (f32[3,4,64,128]{3,2,1,0:T(8,128)}, f32[3,4,64,128]{3,2,1,0:T(8,128)S(1)}, u32[]{:S(2)}, u32[]{:S(2)}) collective-permute-start(f32[3,4,64,128]{3,2,1,0:T(8,128)} %get-tuple-element.21), channel_id=1, source_target_pairs={{0,6},{1,3},{2,0},{3,5},{4,2},{5,7},{6,4},{7,1},{8,14},{9,11},{10,... | collective-permute-start | bytes 1179656 | tf_op jit(solution)/shard_map/ppermute | solution.py:276
  7.9 18.8 %collective-permute-start.2 = (f32[3,4,64,128]{3,2,1,0:T(8,128)}, f32[3,4,64,128]{3,2,1,0:T(8,128)S(1)}, u32[]{:S(2)}, u32[]{:S(2)}) collective-permute-start(f32[3,4,64,128]{3,2,1,0:T(8,128)} %get-tuple-element.20), channel_id=1, source_target_pairs={{0,7},{1,2},{2,1},{3,4},{4,3},{5,6},{6,5},{7,0},{8,15},{9,10},{10,... | collective-permute-start | bytes 1179656 | tf_op jit(solution)/shard_map/ppermute | solution.py:276
  9.1 19.1 %collective-permute-start = (f32[3,4,64,128]{3,2,1,0:T(8,128)}, f32[3,4,64,128]{3,2,1,0:T(8,128)S(1)}, u32[]{:S(2)}, u32[]{:S(2)}) collective-permute-start(f32[3,4,64,128]{3,2,1,0:T(8,128)} %get-tuple-element.20), channel_id=1, source_target_pairs={{0,1},{1,0},{2,3},{3,2},{4,5},{5,4},{6,7},{7,6},{8,9},{9,8},{10,11... | collective-permute-start | bytes 1179656 | tf_op jit(solution)/shard_map/ppermute | solution.py:276
  17.7 10.4 %collective-permute-start.4 = (f32[3,4,64,128]{3,2,1,0:T(8,128)S(1)}, f32[3,4,64,128]{3,2,1,0:T(8,128)S(1)}, u32[]{:S(2)}, u32[]{:S(2)}) collective-permute-start(f32[3,4,64,128]{3,2,1,0:T(8,128)S(1)} %collective-permute-done.1.straight), channel_id=1, source_target_pairs={{0,8},{1,9},{2,10},{3,11},{4,12},{5,13},{6,14},{7,15},{8,0},{9,1},... | collective-permute-start | bytes 1179656 | tf_op jit(solution)/shard_map/ppermute | solution.py:276
  26.7 1.7 %collective-permute-start.5 = (f32[3,4,64,128]{3,2,1,0:T(8,128)S(1)}, f32[3,4,64,128]{3,2,1,0:T(8,128)S(1)}, u32[]{:S(2)}, u32[]{:S(2)}) collective-permute-start(f32[3,4,64,128]{3,2,1,0:T(8,128)S(1)} %collective-permute-done.2.across), channel_id=1, source_target_pairs={{0,8},{1,9},{2,10},{3,11},{4,12},{5,13},{6,14},{7,15},{8,0},{9,1},... | collective-permute-start | bytes 1179656 | tf_op jit(solution)/shard_map/ppermute | solution.py:276
  28.1 1.7 %collective-permute-start.3 = (f32[3,4,64,128]{3,2,1,0:T(8,128)S(1)}, f32[3,4,64,128]{3,2,1,0:T(8,128)S(1)}, u32[]{:S(2)}, u32[]{:S(2)}) collective-permute-start(f32[3,4,64,128]{3,2,1,0:T(8,128)S(1)} %collective-permute-done.swap), channel_id=1, source_target_pairs={{0,8},{1,9},{2,10},{3,11},{4,12},{5,13},{6,14},{7,15},{8,0},{9,1},... | collective-permute-start | bytes 1179656 | tf_op jit(solution)/shard_map/ppermute | solution.py:276
  34.4 1.4 %collective-permute-start.6 = (f32[4,64,128]{2,1,0:T(8,128)S(1)}, f32[4,64,128]{2,1,0:T(8,128)S(1)}, u32[]{:S(2)}, u32[]{:S(2)}) collective-permute-start(f32[4,64,128]{2,1,0:T(8,128)S(1)} %get-tuple-element.25), channel_id=1, source_target_pairs={{0,8},{1,9},{2,10},{3,11},{4,12},{5,13},{6,14},{7,15},{8,0},{9,1},... | collective-permute-start | bytes 393224 | tf_op jit(solution)/shard_map/ppermute | solution.py:276
  35.8 7.4 %collective-permute-start.9 = (f32[4,64,128]{2,1,0:T(8,128)S(1)}, f32[4,64,128]{2,1,0:T(8,128)S(1)}, u32[]{:S(2)}, u32[]{:S(2)}) collective-permute-start(f32[4,64,128]{2,1,0:T(8,128)S(1)} %mul.12), channel_id=1, source_target_pairs={{0,17},{1,16},{2,19},{3,18},{4,21},{5,20},{6,23},{7,22},{8,25},{9,... | collective-permute-start | bytes 393224 | tf_op jit(solution)/shard_map/ppermute | solution.py:276
  37.1 6.9 %collective-permute-start.8 = (f32[4,64,128]{2,1,0:T(8,128)S(1)}, f32[4,64,128]{2,1,0:T(8,128)S(1)}, u32[]{:S(2)}, u32[]{:S(2)}) collective-permute-start(f32[4,64,128]{2,1,0:T(8,128)S(1)} %mul.12), channel_id=1, source_target_pairs={{0,16},{1,17},{2,18},{3,19},{4,20},{5,21},{6,22},{7,23},{8,24},{9,... | collective-permute-start | bytes 393224 | tf_op jit(solution)/shard_map/ppermute | solution.py:276
  37.7 7.5 %collective-permute-start.7 = (f32[4,64,128]{2,1,0:T(8,128)S(1)}, f32[4,64,128]{2,1,0:T(8,128)S(1)}, u32[]{:S(2)}, u32[]{:S(2)}) collective-permute-start(f32[4,64,128]{2,1,0:T(8,128)S(1)} %mul.12), channel_id=1, source_target_pairs={{0,1},{1,0},{2,3},{3,2},{4,5},{5,4},{6,7},{7,6},{8,9},{9,8},{10,11... | collective-permute-start | bytes 393224 | tf_op jit(solution)/shard_map/ppermute | solution.py:276
  39.4 11.0 %collective-permute-start.10 = (f32[2,4,64,128]{3,2,1,0:T(8,128)S(1)}, f32[2,4,64,128]{3,2,1,0:T(8,128)S(1)}, u32[]{:S(2)}, u32[]{:S(2)}) collective-permute-start(f32[2,4,64,128]{3,2,1,0:T(8,128)S(1)} %get-tuple-element.26.two_high), channel_id=1, source_target_pairs={{0,2},{1,3},{2,4},{3,5},{4,6},{5,7},{6,0},{7,1},{8,10},{9,11},{10,... | collective-permute-start | bytes 786440 | tf_op jit(solution)/shard_map/ppermute | solution.py:276
  39.4 13.1 %collective-permute-start.11 = (f32[2,4,64,128]{3,2,1,0:T(8,128)S(1)}, f32[2,4,64,128]{3,2,1,0:T(8,128)S(1)}, u32[]{:S(2)}, u32[]{:S(2)}) collective-permute-start(f32[2,4,64,128]{3,2,1,0:T(8,128)S(1)} %get-tuple-element.27.two_low), channel_id=1, source_target_pairs={{0,6},{1,7},{2,0},{3,1},{4,2},{5,3},{6,4},{7,5},{8,14},{9,15},{10,... | collective-permute-start | bytes 786440 | tf_op jit(solution)/shard_map/ppermute | solution.py:276
  45.2 10.0 %collective-permute-start.13 = (f32[4,64,128]{2,1,0:T(8,128)S(1)}, f32[4,64,128]{2,1,0:T(8,128)S(1)}, u32[]{:S(2)}, u32[]{:S(2)}) collective-permute-start(f32[4,64,128]{2,1,0:T(8,128)S(1)} %multiply_multiply_fusion.j_mine), channel_id=1, source_target_pairs={{0,6},{1,7},{2,0},{3,1},{4,2},{5,3},{6,4},{7,5},{8,10},{9,11},{10,... | collective-permute-start | bytes 393224 | tf_op jit(solution)/shard_map/ppermute | solution.py:276
  52.5 2.8 %collective-permute-start.12 = (f32[4,64,128]{2,1,0:T(8,128)S(1)}, f32[4,64,128]{2,1,0:T(8,128)S(1)}, u32[]{:S(2)}, u32[]{:S(2)}) collective-permute-start(f32[4,64,128]{2,1,0:T(8,128)S(1)} %multiply_multiply_fusion.j_mine), channel_id=1, source_target_pairs={{0,8},{1,9},{2,10},{3,11},{4,12},{5,13},{6,14},{7,15},{8,0},{9,1},... | collective-permute-start | bytes 393224 | tf_op jit(solution)/shard_map/ppermute | solution.py:276
  55.2 1.3 %collective-permute-start.14 = (f32[4,64,128]{2,1,0:T(8,128)S(1)}, f32[4,64,128]{2,1,0:T(8,128)S(1)}, u32[]{:S(2)}, u32[]{:S(2)}) collective-permute-start(f32[4,64,128]{2,1,0:T(8,128)S(1)} %collective-permute-done.13.j_halo), channel_id=1, source_target_pairs={{0,8},{1,9},{2,10},{3,11},{4,12},{5,13},{6,14},{7,15},{8,0},{9,1},... | collective-permute-start | bytes 393224 | tf_op jit(solution)/shard_map/ppermute | solution.py:276
  61.1 1.6 %collective-permute-start.16 = (f32[2,2,2,4,16,128]{5,4,3,2,1,0:T(8,128)S(1)}, f32[2,2,2,4,16,128]{5,4,3,2,1,0:T(8,128)S(1)}, u32[]{:S(2)}, u32[]{:S(2)}) collective-permute-start(f32[2,2,2,4,16,128]{5,4,3,2,1,0:T(8,128)S(1)} %get-tuple-element.33), channel_id=1, source_target_pairs={{0,8},{1,9},{2,10},{3,11},{4,12},{5,13},{6,14},{7,15},{8,0},{9,1},... | collective-permute-start | bytes 786440 | tf_op jit(solution)/shard_map/ppermute | solution.py:276
  62.7 8.1 %collective-permute-start.17 = (f32[2,4,16,128]{3,2,1,0:T(8,128)S(1)}, f32[2,4,16,128]{3,2,1,0:T(8,128)S(1)}, u32[]{:S(2)}, u32[]{:S(2)}) collective-permute-start(f32[2,4,16,128]{3,2,1,0:T(8,128)S(1)} %get-tuple-element.35), channel_id=1, source_target_pairs={{0,1},{1,0},{2,3},{3,2},{4,5},{5,4},{6,7},{7,6},{8,9},{9,8},{10,11... | collective-permute-start | bytes 196616 | tf_op jit(solution)/shard_map/ppermute | solution.py:276
  63.1 7.7 %collective-permute-start.18 = (f32[2,4,16,128]{3,2,1,0:T(8,128)S(1)}, f32[2,4,16,128]{3,2,1,0:T(8,128)S(1)}, u32[]{:S(2)}, u32[]{:S(2)}) collective-permute-start(f32[2,4,16,128]{3,2,1,0:T(8,128)S(1)} %get-tuple-element.36), channel_id=1, source_target_pairs={{0,16},{1,17},{2,18},{3,19},{4,20},{5,21},{6,22},{7,23},{8,24},{9,... | collective-permute-start | bytes 196616 | tf_op jit(solution)/shard_map/ppermute | solution.py:276
  64.6 6.2 %collective-permute-start.19 = (f32[2,4,16,128]{3,2,1,0:T(8,128)S(1)}, f32[2,4,16,128]{3,2,1,0:T(8,128)S(1)}, u32[]{:S(2)}, u32[]{:S(2)}) collective-permute-start(f32[2,4,16,128]{3,2,1,0:T(8,128)S(1)} %get-tuple-element.37), channel_id=1, source_target_pairs={{0,17},{1,16},{2,19},{3,18},{4,21},{5,20},{6,23},{7,22},{8,25},{9,... | collective-permute-start | bytes 196616 | tf_op jit(solution)/shard_map/ppermute | solution.py:276
  66.3 4.5 %collective-permute-start.15 = (f32[8,128]{1,0:T(8,128)S(1)}, f32[8,128]{1,0:T(8,128)S(1)}, u32[]{:S(2)}, u32[]{:S(2)}) collective-permute-start(f32[8,128]{1,0:T(8,128)S(1)} %get-tuple-element.31), channel_id=1, source_target_pairs={{0,4},{1,5},{2,6},{3,7},{4,0},{5,1},{6,2},{7,3},{8,12},{9,13},{10,... | collective-permute-start | bytes 12296 | tf_op jit(solution)/shard_map/ppermute | solution.py:276

commit v3 on v2

--- a/solution.py
+++ b/solution.py
@@ -55,33 +55,47 @@
     lax.fori_loop(first + 2, last - 2, outer, None, unroll=4)
 
 
-def pack_kernel(starts, fields, own_ref, other_ref, sems):
+def pack_kernel(starts, fields, field_ref, other_ref, own_ref, sems):
     arms = starts.shape[0] // 2
     side = lax.rem(lax.axis_index("space"), 2)
     core = lax.rem(lax.axis_index("arm"), 2)
-    copies = []
-    for k, (out_ref, at) in enumerate(((other_ref, 1 - side), (own_ref, side))):
-        copies.append(
-            pltpu.make_async_copy(starts.at[pl.ds(at * arms, arms)], out_ref.at[pl.ds(0, arms)], sems.at[2 * k])
-        )
-        copies.append(pltpu.make_async_copy(fields.at[core], out_ref.at[arms], sems.at[2 * k + 1]))
+    copies = [
+        pltpu.make_async_copy(fields.at[core], field_ref, sems.at[0]),
+        pltpu.make_async_copy(starts.at[pl.ds((1 - side) * arms, arms)], other_ref, sems.at[1]),
+        pltpu.make_async_copy(starts.at[pl.ds(side * arms, arms)], own_ref, sems.at[2]),
+    ]
     for copy in copies:
         copy.start()
     for copy in copies:
         copy.wait()
 
 
+def places(block):
+    side = lax.rem(lax.axis_index("space"), 2)
+    return block + side * block, 2 * block - side * block, 3 * block * (1 - side), 3 * block * side
+
+
+def window_kernel(starts, across, out_ref):
+    arms = across.shape[0]
+    side = lax.rem(lax.axis_index("space"), 2)
+    for j in range(arms):
+        out_ref[j] = starts[side * arms + j]
+        out_ref[arms + j] = across[j]
+
+
 def forward_kernel(
-    labels, starts, fields, swap, straight, across, g_swap, g_straight, g_across,
+    labels, window, swap, straight, fields, f_straight, g_straight, piece, piece_core, piece_chip, piece_both,
     u_ref, one_ref, low_ref, high_ref, keep_ref, send_ref,
     q_ref, p_ref, t_ref, s_ref, product_ref,
 ):
-    block = starts.shape[1]
-    arms = starts.shape[0] // 2
+    block = fields.shape[1]
+    arms = swap.shape[0]
     side = lax.rem(lax.axis_index("space"), 2)
     core = lax.rem(lax.axis_index("arm"), 2)
-    own_at, swap_at = block + side * block, 2 * block - side * block
-    straight_at, across_at = 3 * block * (1 - side), 3 * block * side
+    own_at, swap_at, straight_at, across_at = places(block)
+    chip = lax.div(lax.axis_index("arm"), 2)
+    here_at = swap_at + chip * (across_at - swap_at)
+    there_at = across_at + chip * (swap_at - across_at)
 
     def gain(field):
         return jnp.exp(field * (-contour_step / 4))
@@ -89,18 +103,17 @@
     def fill(i, _):
         for kind in range(2):
             u_ref[kind, own_at + i] = gain(fields[kind, i])
-        for at, mine, other in (
-            (swap_at, swap, g_swap),
-            (straight_at, straight, g_straight),
-            (across_at, across, g_across),
-        ):
-            u_ref[core, at + i] = gain(mine[arms, i])
-            u_ref[1 - core, at + i] = gain(other[arms, i])
-        for j in range(arms):
-            q_ref[j, own_at + i] = starts[side * arms + j, i]
+        u_ref[core, here_at + i] = gain(piece[i])
+        u_ref[1 - core, here_at + i] = gain(piece_core[i])
+        u_ref[core, there_at + i] = gain(piece_chip[i])
+        u_ref[1 - core, there_at + i] = gain(piece_both[i])
+        u_ref[core, straight_at + i] = gain(f_straight[i])
+        u_ref[1 - core, straight_at + i] = gain(g_straight[i])
+        for j in range(arms):
+            q_ref[j, own_at + i] = window[j, i]
+            q_ref[j, across_at + i] = window[arms + j, i]
             q_ref[j, swap_at + i] = swap[j, i]
             q_ref[j, straight_at + i] = straight[j, i]
-            q_ref[j, across_at + i] = across[j, i]
 
     lax.fori_loop(0, block, fill, None)
     kinds = [labels[side * arms + j] for j in range(arms)]
@@ -263,6 +276,8 @@
     held, block, rows, columns = starts.shape
     arms = held // 2
     owned = rows // arm_size
+    if chips != 2 or held % 2 or space_size % 2:
+        raise ValueError("unsupported mesh")
     side = lax.rem(lax.axis_index("space"), 2)
     core = lax.rem(lax.axis_index("arm"), 2)
 
@@ -287,40 +302,50 @@
     def to_across(value):
         return send(value, lambda x, c, p, h: (x, c, p + 2 * h - 1, 1 - h))
 
-    message = f32((arms + 1, block, rows, columns))
-    own_set, other_set = pl.pallas_call(
+    field_own, other_set, own_set = pl.pallas_call(
         pack_kernel,
-        out_shape=(message, message),
+        out_shape=(
+            f32((block, rows, columns)),
+            f32((arms, block, rows, columns)),
+            f32((arms, block, rows, columns)),
+        ),
         in_specs=[pl.BlockSpec(memory_space=pl.ANY)] * 2,
-        out_specs=[pl.BlockSpec(memory_space=pltpu.VMEM)] * 2,
-        scratch_shapes=[pltpu.SemaphoreType.DMA((4,))],
+        out_specs=[pl.BlockSpec(memory_space=pltpu.VMEM)] * 3,
+        scratch_shapes=[pltpu.SemaphoreType.DMA((3,))],
     )(starts, fields)
+    field_got = send(field_own, lambda x, c, p, h: (x, c, p + 2 * h - 1 if x else p, 1 - h))
     across = to_across(other_set)
     swap = to_side(other_set)
     straight = to_straight(own_set)
-    got = [swap, straight, across]
-    got_more = [to_core(value) for value in got]
+    pieces = [
+        field_got,
+        to_core(field_got),
+        send(field_got, lambda x, c, p, h: (1 - x, c, p, h)),
+        send(field_got, lambda x, c, p, h: (1 - x, 1 - c, p, h)),
+    ]
+    field_straight = to_straight(field_own)
+    straight_more = to_core(field_straight)
 
     wide = vmem((arms, 4 * block, rows, columns))
     whole = (arms, 2 * block, rows, columns)
     part = (arms, block, rows, columns)
     one = (block, rows, columns)
+    window = call(window_kernel, f32((2 * arms, block, rows, columns)), [], 0, starts, across)
     factor, step_one, low, high, keep, give = call(
         forward_kernel,
         (f32((2, 4 * block, rows, columns)), f32(whole), f32(part), f32(part), f32(one), f32(one)),
         [wide, wide, wide, wide, vmem((2,) + one)],
         1,
-        labels, starts, fields, *got, *got_more,
+        labels, window, swap, straight, fields, field_straight, straight_more, *pieces,
         cost=8_000_000,
     )
     right = send(low, lambda x, c, p, h: (x, c, p - 1, h))
     left = send(high, lambda x, c, p, h: (x, c, p + 1, h))
     mine = keep * to_core(give)
+    mine = mine * to_side(mine)
     junction = mine
-    for step, flip in other_chips(chips):
-        junction = junction * send(
-            mine, lambda x, c, p, h, step=step, flip=flip: (x + step, c, p, 1 - h if flip else h)
-        )
+    for step in range(1, chips):
+        junction = junction * send(mine, lambda x, c, p, h, step=step: (x + step, c, p, h))
     halo = send(junction, lambda x, c, p, h: (x, c, p + 2 * c - 1, h))
     held_junction, left, right = lax.optimization_barrier((junction, left, right))
     junction_other = to_core(held_junction)
@@ -342,13 +367,13 @@
             step *= 2
     else:
         total = lax.psum(total, "space") / 4.0
-    places = other_chips(chips)
+    to_places = other_chips(chips)
     own, *gives = call(
-        meet_kernel, (f32(parts[2:]),) * (1 + len(places)), [], 0, keep, to_core(give)
+        meet_kernel, (f32(parts[2:]),) * (1 + len(to_places)), [], 0, keep, to_core(give)
     )
     received = [
         send(value, lambda x, c, p, h, step=step, flip=flip: (x + step, c, p, 1 - h if flip else h))
-        for value, (step, flip) in zip(gives, places)
+        for value, (step, flip) in zip(gives, to_places)
     ]
     cell_count = block * space_size * rows * columns
     return call(

time: 71.8 us -> 67.3 us (0.937)
  waiting for transfers between devices: 35.9 us -> 19.3 us
  starting transfers between devices: 22.9 us -> 35.1 us
    ppermute x20 -> x22, waiting for transfers between devices: 35.9 us -> 19.3 us  [send(): return lax.ppermute(value, AXES, perm)]
    ppermute x20 -> x22, starting transfers between devices: 22.9 us -> 35.1 us  [send(): return lax.ppermute(value, AXES, perm)]
    pallas_call x4 -> x5, Pallas kernels: 9.92 us -> 9.95 us  [call(): pl.pallas_call(kernel, out_shape=out_shape, in_specs=specs, out_specs=jax...]
  transfers between devices with their start and end apart: 20 -> 22, of which waited for: 14 -> 9; matrix products, arithmetic and copies ran while one was open for 0% -> 0% of each run, Pallas kernels for 0% -> 0%
where the time goes in v3:
time: 67.3 us; the launch traced here: 67.2 us
  starting transfers between devices  35.1 us (52%)
  waiting for transfers between devices  19.3 us (29%)
  Pallas kernels  12 us (18%)
  between operations  0.74 us (1%)
    ppermute x22, starting transfers between devices, send(): return lax.ppermute(value, AXES, perm)  35.1 us
    ppermute x22, waiting for transfers between devices, send(): return lax.ppermute(value, AXES, perm)  19.3 us
    pallas_call x5, Pallas kernels, call(): pl.pallas_call(kernel, out_shape=out_shape, in_specs=specs, out_specs=jax...  9.95 us
    pallas_call x1, Pallas kernels, local(): pl.pallas_call(pack_kernel, out_shape=(f32((block, rows, columns)), f32((...  2.03 us
  transfers between devices with their start and end apart: 22, of which 9 were waited for; matrix products, arithmetic and copies ran while one was open for 0% of the time, Pallas kernels for 0%

profile of v3, /device:TPU:0, one launch (start us, length us, event | category | flops | bytes accessed | tf_op | source)
XLA Modules:
  0.0 67.2 jit_solution(16165754447553611584)
XLA Ops:
  0.6 0.0 copy-start.1
  0.6 2.0 %shard_map.50 = (f32[4,64,128]{2,1,0:T(8,128)}, f32[2,4,64,128]{3,2,1,0:T(8,128)}, f32[2,4,64,128]{3,2,1,0:T(8,128)}) custom-call(f32[4,4,64,128]{3,2,1,0:T(8,128)} %starts.3, f32[2,4,64,128]{3,2,1,0:T(8,128)} %fields.5), custom_call_target="tpu_custom_call" | custom-call | tf_op jit(solution)/shard_map/pallas_call | solution.py:305
  2.7 3.0 %collective-permute-start.5 = (f32[4,64,128]{2,1,0:T(8,128)}, f32[4,64,128]{2,1,0:T(8,128)S(1)}, u32[]{:S(2)}, u32[]{:S(2)}) collective-permute-start(f32[4,64,128]{2,1,0:T(8,128)} %get-tuple-element.23), channel_id=1, source_target_pairs={{0,1},{1,0},{2,3},{3,2},{4,5},{5,4},{6,7},{7,6},{8,9},{9,8},{10,11... | collective-permute-start | bytes 393224 | tf_op jit(solution)/shard_map/ppermute | solution.py:291
  5.7 3.5 %collective-permute-start = (f32[2,4,64,128]{3,2,1,0:T(8,128)}, f32[2,4,64,128]{3,2,1,0:T(8,128)S(1)}, u32[]{:S(2)}, u32[]{:S(2)}) collective-permute-start(f32[2,4,64,128]{3,2,1,0:T(8,128)} %get-tuple-element.21), channel_id=1, source_target_pairs={{0,7},{1,2},{2,1},{3,4},{4,3},{5,6},{6,5},{7,0},{8,15},{9,10},{10,... | collective-permute-start | bytes 786440 | tf_op jit(solution)/shard_map/ppermute | solution.py:291
  9.3 0.4 collective-permute-start.3
  9.7 4.7 %collective-permute-done.5.piece = f32[4,64,128]{2,1,0:T(8,128)S(1)} collective-permute-done((f32[4,64,128]{2,1,0:T(8,128)}, f32[4,64,128]{2,1,0:T(8,128)S(1)}, u32[]{:S(2)}, u32[]{:S(2)}) %collective-permute-start.5) | collective-permute-done | bytes 131104 | tf_op jit(solution)/shard_map/ppermute | solution.py:291
  14.4 0.0 collective-permute-start.8
  14.4 0.0 copy-start
  14.4 0.0 copy-start.2
  14.4 3.7 %collective-permute-start.2 = (f32[2,4,64,128]{3,2,1,0:T(8,128)}, f32[2,4,64,128]{3,2,1,0:T(8,128)S(1)}, u32[]{:S(2)}, u32[]{:S(2)}) collective-permute-start(f32[2,4,64,128]{3,2,1,0:T(8,128)} %get-tuple-element.22), channel_id=1, source_target_pairs={{0,6},{1,3},{2,0},{3,5},{4,2},{5,7},{6,4},{7,1},{8,14},{9,11},{10,... | collective-permute-start | bytes 786440 | tf_op jit(solution)/shard_map/ppermute | solution.py:291
  18.1 0.3 collective-permute-start.1
  18.4 0.0 collective-permute-done.3.f_straight
  18.4 4.4 %collective-permute-start.7 = (f32[4,64,128]{2,1,0:T(8,128)S(1)}, f32[4,64,128]{2,1,0:T(8,128)S(1)}, u32[]{:S(2)}, u32[]{:S(2)}) collective-permute-start(f32[4,64,128]{2,1,0:T(8,128)S(1)} %collective-permute-done.5.piece), channel_id=1, source_target_pairs={{0,16},{1,17},{2,18},{3,19},{4,20},{5,21},{6,22},{7,23},{8,24},{9,... | collective-permute-start | bytes 393224 | tf_op jit(solution)/shard_map/ppermute | solution.py:291
  22.8 0.0 collective-permute-done.8.piece_both
  22.8 0.0 collective-permute-start.6
  22.8 0.0 collective-permute-done.across
  22.8 0.5 collective-permute-start.4
  23.3 0.0 copy-done.1
  23.3 2.4 %collective-permute-done.7.piece_chip = f32[4,64,128]{2,1,0:T(8,128)S(1)} collective-permute-done((f32[4,64,128]{2,1,0:T(8,128)S(1)}, f32[4,64,128]{2,1,0:T(8,128)S(1)}, u32[]{:S(2)}, u32[]{:S(2)}) %collective-permute-start.7) | collective-permute-done | bytes 131104 | tf_op jit(solution)/shard_map/ppermute | solution.py:291
  25.7 0.0 collective-permute-done.6.piece_core
  25.7 0.0 collective-permute-done.4.g_straight
  25.7 0.0 collective-permute-done.2.straight
  25.7 0.0 collective-permute-done.1.swap
  25.7 0.0 copy-done
  25.8 0.0 copy-done.2
  25.8 4.5 %shard_map.52 = (f32[2,16,64,128]{3,2,1,0:T(8,128)S(1)}, f32[2,8,64,128]{3,2,1,0:T(8,128)S(1)}, f32[2,4,64,128]{3,2,1,0:T(8,128)S(1)}, f32[2,4,64,128]{3,2,1,0:T...) custom-call(s32[4]{0:T(128)S(1)} %copy-done.2, f32[4,4,64,128]{3,2,1,0:T(8,128)S(1)} %shard_map.51.window, ...), custom_call_target="tpu_custom_call" | custom-call | flops 8000000 | bytes 8000000 | tf_op jit(solution)/shard_map/pallas_call | solution.py:262
  30.3 0.1 collective-permute-start.9
  30.4 1.3 %collective-permute-done.9 = f32[4,64,128]{2,1,0:T(8,128)S(1)} collective-permute-done((f32[4,64,128]{2,1,0:T(8,128)S(1)}, f32[4,64,128]{2,1,0:T(8,128)S(1)}, u32[]{:S(2)}, u32[]{:S(2)}) %collective-permute-start.9) | collective-permute-done | bytes 131104 | tf_op jit(solution)/shard_map/ppermute | solution.py:291
  31.7 2.3 %collective-permute-start.10 = (f32[4,64,128]{2,1,0:T(8,128)S(1)}, f32[4,64,128]{2,1,0:T(8,128)S(1)}, u32[]{:S(2)}, u32[]{:S(2)}) collective-permute-start(f32[4,64,128]{2,1,0:T(8,128)S(1)} %mul.9), channel_id=1, source_target_pairs={{0,1},{1,0},{2,3},{3,2},{4,5},{5,4},{6,7},{7,6},{8,9},{9,8},{10,11... | collective-permute-start | bytes 393224 | tf_op jit(solution)/shard_map/ppermute | solution.py:291
  34.0 0.0 collective-permute-start.12
  34.0 3.8 %collective-permute-start.13 = (f32[2,4,64,128]{3,2,1,0:T(8,128)S(1)}, f32[2,4,64,128]{3,2,1,0:T(8,128)S(1)}, u32[]{:S(2)}, u32[]{:S(2)}) collective-permute-start(f32[2,4,64,128]{3,2,1,0:T(8,128)S(1)} %get-tuple-element.29.two_low), channel_id=1, source_target_pairs={{0,6},{1,7},{2,0},{3,1},{4,2},{5,3},{6,4},{7,5},{8,14},{9,15},{10,... | collective-permute-start | bytes 786440 | tf_op jit(solution)/shard_map/ppermute | solution.py:291
  37.8 0.0 collective-permute-done.10
  37.8 2.1 %collective-permute-start.11 = (f32[4,64,128]{2,1,0:T(8,128)S(1)}, f32[4,64,128]{2,1,0:T(8,128)S(1)}, u32[]{:S(2)}, u32[]{:S(2)}) collective-permute-start(f32[4,64,128]{2,1,0:T(8,128)S(1)} %mul.10), channel_id=1, source_target_pairs={{0,16},{1,17},{2,18},{3,19},{4,20},{5,21},{6,22},{7,23},{8,24},{9,... | collective-permute-start | bytes 393224 | tf_op jit(solution)/shard_map/ppermute | solution.py:291
  39.9 3.3 %collective-permute-done.11 = f32[4,64,128]{2,1,0:T(8,128)S(1)} collective-permute-done((f32[4,64,128]{2,1,0:T(8,128)S(1)}, f32[4,64,128]{2,1,0:T(8,128)S(1)}, u32[]{:S(2)}, u32[]{:S(2)}) %collective-permute-start.11) | collective-permute-done | bytes 131104 | tf_op jit(solution)/shard_map/ppermute | solution.py:291
  43.2 3.4 %collective-permute-start.15 = (f32[4,64,128]{2,1,0:T(8,128)S(1)}, f32[4,64,128]{2,1,0:T(8,128)S(1)}, u32[]{:S(2)}, u32[]{:S(2)}) collective-permute-start(f32[4,64,128]{2,1,0:T(8,128)S(1)} %mul.11.j_mine), channel_id=1, source_target_pairs={{0,6},{1,7},{2,0},{3,1},{4,2},{5,3},{6,4},{7,5},{8,10},{9,11},{10,... | collective-permute-start | bytes 393224 | tf_op jit(solution)/shard_map/ppermute | solution.py:291
  46.7 0.0 collective-permute-done.12.two_left
  46.7 1.0 %collective-permute-done.13.two_right = f32[2,4,64,128]{3,2,1,0:T(8,128)S(1)} collective-permute-done((f32[2,4,64,128]{3,2,1,0:T(8,128)S(1)}, f32[2,4,64,128]{3,2,1,0:T(8,128)S(1)}, u32[]{:S(2)}, u32[]{:S(2)}) %collective-permute-start.13) | collective-permute-done | bytes 262176 | tf_op jit(solution)/shard_map/ppermute | solution.py:291
  47.7 0.0 collective-permute-start.14
  47.7 2.0 %collective-permute-done.15.j_halo = f32[4,64,128]{2,1,0:T(8,128)S(1)} collective-permute-done((f32[4,64,128]{2,1,0:T(8,128)S(1)}, f32[4,64,128]{2,1,0:T(8,128)S(1)}, u32[]{:S(2)}, u32[]{:S(2)}) %collective-permute-start.15) | collective-permute-done | bytes 131104 | tf_op jit(solution)/shard_map/ppermute | solution.py:291
  49.7 1.4 %collective-permute-start.16 = (f32[4,64,128]{2,1,0:T(8,128)S(1)}, f32[4,64,128]{2,1,0:T(8,128)S(1)}, u32[]{:S(2)}, u32[]{:S(2)}) collective-permute-start(f32[4,64,128]{2,1,0:T(8,128)S(1)} %collective-permute-done.15.j_halo), channel_id=1, source_target_pairs={{0,8},{1,9},{2,10},{3,11},{4,12},{5,13},{6,14},{7,15},{8,0},{9,1},... | collective-permute-start | bytes 393224 | tf_op jit(solution)/shard_map/ppermute | solution.py:291
  51.1 0.0 collective-permute-done.14.j_other
  51.1 1.0 %collective-permute-done.16.j_halo_other = f32[4,64,128]{2,1,0:T(8,128)S(1)} collective-permute-done((f32[4,64,128]{2,1,0:T(8,128)S(1)}, f32[4,64,128]{2,1,0:T(8,128)S(1)}, u32[]{:S(2)}, u32[]{:S(2)}) %collective-permute-start.16) | collective-permute-done | bytes 131104 | tf_op jit(solution)/shard_map/ppermute | solution.py:291
  52.1 4.6 %shard_map.53 = (f32[2,2,2,4,16,128]{5,4,3,2,1,0:T(8,128)S(1)}, f32[2,2,2,4,16,128]{5,4,3,2,1,0:T(8,128)S(1)}, f32[8,128]{1,0:T(8,128)S(1)}) custom-call(s32[4]{0:T(128)S(1)} %copy-done.2, f32[2,16,64,128]{3,2,1,0:T(8,128)S(1)} %get-tuple-element.24.u_ref, f32[2,8,64,128]{3,2,1,0:T(8,128)S(1)} %get-tuple-element.25.one_ref, ...), custom_call_target="tpu_custom_call" | custom-call | flops 8000000 | bytes 8000000 | tf_op jit(solution)/shard_map/pallas_call | solution.py:262
  56.6 0.4 collective-permute-start.18
  57.1 1.2 %collective-permute-done.18.received = f32[2,2,2,4,16,128]{5,4,3,2,1,0:T(8,128)S(1)} collective-permute-done((f32[2,2,2,4,16,128]{5,4,3,2,1,0:T(8,128)S(1)}, f32[2,2,2,4,16,128]{5,4,3,2,1,0:T(8,128)S(1)}, u32[]{:S(2)}, u32[]{:S(2)}) %collective-permute-start.18) | collective-permute-done | bytes 262176 | tf_op jit(solution)/shard_map/ppermute | solution.py:291
  58.3 0.8 %collective-permute-start.19 = (f32[2,4,16,128]{3,2,1,0:T(8,128)S(1)}, f32[2,4,16,128]{3,2,1,0:T(8,128)S(1)}, u32[]{:S(2)}, u32[]{:S(2)}) collective-permute-start(f32[2,4,16,128]{3,2,1,0:T(8,128)S(1)} %get-tuple-element.37), channel_id=1, source_target_pairs={{0,1},{1,0},{2,3},{3,2},{4,5},{5,4},{6,7},{7,6},{8,9},{9,8},{10,11... | collective-permute-start | bytes 196616 | tf_op jit(solution)/shard_map/ppermute | solution.py:291
  59.1 2.0 %collective-permute-start.20 = (f32[2,4,16,128]{3,2,1,0:T(8,128)S(1)}, f32[2,4,16,128]{3,2,1,0:T(8,128)S(1)}, u32[]{:S(2)}, u32[]{:S(2)}) collective-permute-start(f32[2,4,16,128]{3,2,1,0:T(8,128)S(1)} %get-tuple-element.38), channel_id=1, source_target_pairs={{0,16},{1,17},{2,18},{3,19},{4,20},{5,21},{6,22},{7,23},{8,24},{9,... | collective-permute-start | bytes 196616 | tf_op jit(solution)/shard_map/ppermute | solution.py:291
  61.1 0.7 %collective-permute-start.21 = (f32[2,4,16,128]{3,2,1,0:T(8,128)S(1)}, f32[2,4,16,128]{3,2,1,0:T(8,128)S(1)}, u32[]{:S(2)}, u32[]{:S(2)}) collective-permute-start(f32[2,4,16,128]{3,2,1,0:T(8,128)S(1)} %get-tuple-element.39), channel_id=1, source_target_pairs={{0,17},{1,16},{2,19},{3,18},{4,21},{5,20},{6,23},{7,22},{8,25},{9,... | collective-permute-start | bytes 196616 | tf_op jit(solution)/shard_map/ppermute | solution.py:291
  61.8 2.2 %collective-permute-start.17 = (f32[8,128]{1,0:T(8,128)S(1)}, f32[8,128]{1,0:T(8,128)S(1)}, u32[]{:S(2)}, u32[]{:S(2)}) collective-permute-start(f32[8,128]{1,0:T(8,128)S(1)} %get-tuple-element.33), channel_id=1, source_target_pairs={{0,4},{1,5},{2,6},{3,7},{4,0},{5,1},{6,2},{7,3},{8,12},{9,13},{10,... | collective-permute-start | bytes 12296 | tf_op jit(solution)/shard_map/ppermute | solution.py:291
  64.0 2.3 %collective-permute-done.17 = f32[8,128]{1,0:T(8,128)S(1)} collective-permute-done((f32[8,128]{1,0:T(8,128)S(1)}, f32[8,128]{1,0:T(8,128)S(1)}, u32[]{:S(2)}, u32[]{:S(2)}) %collective-permute-start.17) | collective-permute-done | bytes 4128 | tf_op jit(solution)/shard_map/ppermute | solution.py:291
  66.4 0.0 collective-permute-done.19.refs_0_
  66.4 0.0 collective-permute-done.20.refs_1_
  66.4 0.0 collective-permute-done.21.refs_2_
  66.4 0.8 %shard_map.55 = (f32[2,4,16,128]{3,2,1,0:T(8,128)}, f32[2,4,16,128]{3,2,1,0:T(8,128)}) custom-call(f32[2,4,64,128]{3,2,1,0:T(8,128)S(1)} %copy-done, f32[8,128]{1,0:T(8,128)S(1)} %add.3.total, f32[2,4,16,128]{3,2,1,0:T(8,128)S(1)} %get-tuple-element.36.own, f32[2,4,16,128]{3,2,1,0:T(8,128)S(1)} %collective-permute-done.19.refs_0_, ...), custom_call_target="tpu_custom_call" | custom-call | flops 1000000 | bytes 1000000 | tf_op jit(solution)/shard_map/pallas_call | solution.py:262
  (6 shorter events, 0.1 us)
Async XLA Ops:
  0.6 22.7 %copy-start.1 = (f32[4,4,64,128]{3,2,1,0:T(8,128)S(1)}, f32[4,4,64,128]{3,2,1,0:T(8,128)}, u32[]{:S(2)}) copy-start(f32[4,4,64,128]{3,2,1,0:T(8,128)} %starts.3) | copy-start | bytes 1572868
  2.7 11.7 %collective-permute-start.5 = (f32[4,64,128]{2,1,0:T(8,128)}, f32[4,64,128]{2,1,0:T(8,128)S(1)}, u32[]{:S(2)}, u32[]{:S(2)}) collective-permute-start(f32[4,64,128]{2,1,0:T(8,128)} %get-tuple-element.23), channel_id=1, source_target_pairs={{0,1},{1,0},{2,3},{3,2},{4,5},{5,4},{6,7},{7,6},{8,9},{9,8},{10,11... | collective-permute-start | bytes 393224 | tf_op jit(solution)/shard_map/ppermute | solution.py:291
  5.7 17.1 %collective-permute-start = (f32[2,4,64,128]{3,2,1,0:T(8,128)}, f32[2,4,64,128]{3,2,1,0:T(8,128)S(1)}, u32[]{:S(2)}, u32[]{:S(2)}) collective-permute-start(f32[2,4,64,128]{3,2,1,0:T(8,128)} %get-tuple-element.21), channel_id=1, source_target_pairs={{0,7},{1,2},{2,1},{3,4},{4,3},{5,6},{6,5},{7,0},{8,15},{9,10},{10,... | collective-permute-start | bytes 786440 | tf_op jit(solution)/shard_map/ppermute | solution.py:291
  9.3 9.2 %collective-permute-start.3 = (f32[4,64,128]{2,1,0:T(8,128)}, f32[4,64,128]{2,1,0:T(8,128)S(1)}, u32[]{:S(2)}, u32[]{:S(2)}) collective-permute-start(f32[4,64,128]{2,1,0:T(8,128)} %get-tuple-element.23), channel_id=1, source_target_pairs={{0,6},{1,3},{2,0},{3,5},{4,2},{5,7},{6,4},{7,1},{8,14},{9,11},{10,... | collective-permute-start | bytes 393224 | tf_op jit(solution)/shard_map/ppermute | solution.py:291
  14.4 8.4 %collective-permute-start.8 = (f32[4,64,128]{2,1,0:T(8,128)S(1)}, f32[4,64,128]{2,1,0:T(8,128)S(1)}, u32[]{:S(2)}, u32[]{:S(2)}) collective-permute-start(f32[4,64,128]{2,1,0:T(8,128)S(1)} %collective-permute-done.5.piece), channel_id=1, source_target_pairs={{0,24},{1,25},{2,26},{3,27},{4,28},{5,29},{6,30},{7,31},{8,16},{9,... | collective-permute-start | bytes 393224 | tf_op jit(solution)/shard_map/ppermute | solution.py:291
  14.4 11.3 %copy-start = (f32[2,4,64,128]{3,2,1,0:T(8,128)S(1)}, f32[2,4,64,128]{3,2,1,0:T(8,128)}, u32[]{:S(2)}) copy-start(f32[2,4,64,128]{3,2,1,0:T(8,128)} %fields.5) | copy-start | bytes 786436
  14.4 11.4 %copy-start.2 = (s32[4]{0:T(128)S(1)}, s32[4]{0:T(128)}, u32[]{:S(2)}) copy-start(s32[4]{0:T(128)} %labels.3) | copy-start | bytes 52
  14.4 11.3 %collective-permute-start.2 = (f32[2,4,64,128]{3,2,1,0:T(8,128)}, f32[2,4,64,128]{3,2,1,0:T(8,128)S(1)}, u32[]{:S(2)}, u32[]{:S(2)}) collective-permute-start(f32[2,4,64,128]{3,2,1,0:T(8,128)} %get-tuple-element.22), channel_id=1, source_target_pairs={{0,6},{1,3},{2,0},{3,5},{4,2},{5,7},{6,4},{7,1},{8,14},{9,11},{10,... | collective-permute-start | bytes 786440 | tf_op jit(solution)/shard_map/ppermute | solution.py:291
  18.1 7.6 %collective-permute-start.1 = (f32[2,4,64,128]{3,2,1,0:T(8,128)}, f32[2,4,64,128]{3,2,1,0:T(8,128)S(1)}, u32[]{:S(2)}, u32[]{:S(2)}) collective-permute-start(f32[2,4,64,128]{3,2,1,0:T(8,128)} %get-tuple-element.21), channel_id=1, source_target_pairs={{0,1},{1,0},{2,3},{3,2},{4,5},{5,4},{6,7},{7,6},{8,9},{9,8},{10,11... | collective-permute-start | bytes 786440 | tf_op jit(solution)/shard_map/ppermute | solution.py:291
  18.4 7.3 %collective-permute-start.7 = (f32[4,64,128]{2,1,0:T(8,128)S(1)}, f32[4,64,128]{2,1,0:T(8,128)S(1)}, u32[]{:S(2)}, u32[]{:S(2)}) collective-permute-start(f32[4,64,128]{2,1,0:T(8,128)S(1)} %collective-permute-done.5.piece), channel_id=1, source_target_pairs={{0,16},{1,17},{2,18},{3,19},{4,20},{5,21},{6,22},{7,23},{8,24},{9,... | collective-permute-start | bytes 393224 | tf_op jit(solution)/shard_map/ppermute | solution.py:291
  22.8 2.9 %collective-permute-start.6 = (f32[4,64,128]{2,1,0:T(8,128)S(1)}, f32[4,64,128]{2,1,0:T(8,128)S(1)}, u32[]{:S(2)}, u32[]{:S(2)}) collective-permute-start(f32[4,64,128]{2,1,0:T(8,128)S(1)} %collective-permute-done.5.piece), channel_id=1, source_target_pairs={{0,8},{1,9},{2,10},{3,11},{4,12},{5,13},{6,14},{7,15},{8,0},{9,1},... | collective-permute-start | bytes 393224 | tf_op jit(solution)/shard_map/ppermute | solution.py:291
  22.8 2.9 %collective-permute-start.4 = (f32[4,64,128]{2,1,0:T(8,128)S(1)}, f32[4,64,128]{2,1,0:T(8,128)S(1)}, u32[]{:S(2)}, u32[]{:S(2)}) collective-permute-start(f32[4,64,128]{2,1,0:T(8,128)S(1)} %collective-permute-done.3.f_straight), channel_id=1, source_target_pairs={{0,8},{1,9},{2,10},{3,11},{4,12},{5,13},{6,14},{7,15},{8,0},{9,1},... | collective-permute-start | bytes 393224 | tf_op jit(solution)/shard_map/ppermute | solution.py:291
  30.3 1.4 %collective-permute-start.9 = (f32[4,64,128]{2,1,0:T(8,128)S(1)}, f32[4,64,128]{2,1,0:T(8,128)S(1)}, u32[]{:S(2)}, u32[]{:S(2)}) collective-permute-start(f32[4,64,128]{2,1,0:T(8,128)S(1)} %get-tuple-element.27), channel_id=1, source_target_pairs={{0,8},{1,9},{2,10},{3,11},{4,12},{5,13},{6,14},{7,15},{8,0},{9,1},... | collective-permute-start | bytes 393224 | tf_op jit(solution)/shard_map/ppermute | solution.py:291
  31.7 6.1 %collective-permute-start.10 = (f32[4,64,128]{2,1,0:T(8,128)S(1)}, f32[4,64,128]{2,1,0:T(8,128)S(1)}, u32[]{:S(2)}, u32[]{:S(2)}) collective-permute-start(f32[4,64,128]{2,1,0:T(8,128)S(1)} %mul.9), channel_id=1, source_target_pairs={{0,1},{1,0},{2,3},{3,2},{4,5},{5,4},{6,7},{7,6},{8,9},{9,8},{10,11... | collective-permute-start | bytes 393224 | tf_op jit(solution)/shard_map/ppermute | solution.py:291
  34.0 12.7 %collective-permute-start.12 = (f32[2,4,64,128]{3,2,1,0:T(8,128)S(1)}, f32[2,4,64,128]{3,2,1,0:T(8,128)S(1)}, u32[]{:S(2)}, u32[]{:S(2)}) collective-permute-start(f32[2,4,64,128]{3,2,1,0:T(8,128)S(1)} %get-tuple-element.28.two_high), channel_id=1, source_target_pairs={{0,2},{1,3},{2,4},{3,5},{4,6},{5,7},{6,0},{7,1},{8,10},{9,11},{10,... | collective-permute-start | bytes 786440 | tf_op jit(solution)/shard_map/ppermute | solution.py:291
  34.0 13.7 %collective-permute-start.13 = (f32[2,4,64,128]{3,2,1,0:T(8,128)S(1)}, f32[2,4,64,128]{3,2,1,0:T(8,128)S(1)}, u32[]{:S(2)}, u32[]{:S(2)}) collective-permute-start(f32[2,4,64,128]{3,2,1,0:T(8,128)S(1)} %get-tuple-element.29.two_low), channel_id=1, source_target_pairs={{0,6},{1,7},{2,0},{3,1},{4,2},{5,3},{6,4},{7,5},{8,14},{9,15},{10,... | collective-permute-start | bytes 786440 | tf_op jit(solution)/shard_map/ppermute | solution.py:291
  37.8 5.4 %collective-permute-start.11 = (f32[4,64,128]{2,1,0:T(8,128)S(1)}, f32[4,64,128]{2,1,0:T(8,128)S(1)}, u32[]{:S(2)}, u32[]{:S(2)}) collective-permute-start(f32[4,64,128]{2,1,0:T(8,128)S(1)} %mul.10), channel_id=1, source_target_pairs={{0,16},{1,17},{2,18},{3,19},{4,20},{5,21},{6,22},{7,23},{8,24},{9,... | collective-permute-start | bytes 393224 | tf_op jit(solution)/shard_map/ppermute | solution.py:291
  43.2 6.5 %collective-permute-start.15 = (f32[4,64,128]{2,1,0:T(8,128)S(1)}, f32[4,64,128]{2,1,0:T(8,128)S(1)}, u32[]{:S(2)}, u32[]{:S(2)}) collective-permute-start(f32[4,64,128]{2,1,0:T(8,128)S(1)} %mul.11.j_mine), channel_id=1, source_target_pairs={{0,6},{1,7},{2,0},{3,1},{4,2},{5,3},{6,4},{7,5},{8,10},{9,11},{10,... | collective-permute-start | bytes 393224 | tf_op jit(solution)/shard_map/ppermute | solution.py:291
  47.7 3.4 %collective-permute-start.14 = (f32[4,64,128]{2,1,0:T(8,128)S(1)}, f32[4,64,128]{2,1,0:T(8,128)S(1)}, u32[]{:S(2)}, u32[]{:S(2)}) collective-permute-start(f32[4,64,128]{2,1,0:T(8,128)S(1)} %mul.11.j_mine), channel_id=1, source_target_pairs={{0,8},{1,9},{2,10},{3,11},{4,12},{5,13},{6,14},{7,15},{8,0},{9,1},... | collective-permute-start | bytes 393224 | tf_op jit(solution)/shard_map/ppermute | solution.py:291
  49.7 2.4 %collective-permute-start.16 = (f32[4,64,128]{2,1,0:T(8,128)S(1)}, f32[4,64,128]{2,1,0:T(8,128)S(1)}, u32[]{:S(2)}, u32[]{:S(2)}) collective-permute-start(f32[4,64,128]{2,1,0:T(8,128)S(1)} %collective-permute-done.15.j_halo), channel_id=1, source_target_pairs={{0,8},{1,9},{2,10},{3,11},{4,12},{5,13},{6,14},{7,15},{8,0},{9,1},... | collective-permute-start | bytes 393224 | tf_op jit(solution)/shard_map/ppermute | solution.py:291
  56.6 1.6 %collective-permute-start.18 = (f32[2,2,2,4,16,128]{5,4,3,2,1,0:T(8,128)S(1)}, f32[2,2,2,4,16,128]{5,4,3,2,1,0:T(8,128)S(1)}, u32[]{:S(2)}, u32[]{:S(2)}) collective-permute-start(f32[2,2,2,4,16,128]{5,4,3,2,1,0:T(8,128)S(1)} %get-tuple-element.35), channel_id=1, source_target_pairs={{0,8},{1,9},{2,10},{3,11},{4,12},{5,13},{6,14},{7,15},{8,0},{9,1},... | collective-permute-start | bytes 786440 | tf_op jit(solution)/shard_map/ppermute | solution.py:291
  58.3 8.1 %collective-permute-start.19 = (f32[2,4,16,128]{3,2,1,0:T(8,128)S(1)}, f32[2,4,16,128]{3,2,1,0:T(8,128)S(1)}, u32[]{:S(2)}, u32[]{:S(2)}) collective-permute-start(f32[2,4,16,128]{3,2,1,0:T(8,128)S(1)} %get-tuple-element.37), channel_id=1, source_target_pairs={{0,1},{1,0},{2,3},{3,2},{4,5},{5,4},{6,7},{7,6},{8,9},{9,8},{10,11... | collective-permute-start | bytes 196616 | tf_op jit(solution)/shard_map/ppermute | solution.py:291
  59.1 7.3 %collective-permute-start.20 = (f32[2,4,16,128]{3,2,1,0:T(8,128)S(1)}, f32[2,4,16,128]{3,2,1,0:T(8,128)S(1)}, u32[]{:S(2)}, u32[]{:S(2)}) collective-permute-start(f32[2,4,16,128]{3,2,1,0:T(8,128)S(1)} %get-tuple-element.38), channel_id=1, source_target_pairs={{0,16},{1,17},{2,18},{3,19},{4,20},{5,21},{6,22},{7,23},{8,24},{9,... | collective-permute-start | bytes 196616 | tf_op jit(solution)/shard_map/ppermute | solution.py:291
  61.1 5.3 %collective-permute-start.21 = (f32[2,4,16,128]{3,2,1,0:T(8,128)S(1)}, f32[2,4,16,128]{3,2,1,0:T(8,128)S(1)}, u32[]{:S(2)}, u32[]{:S(2)}) collective-permute-start(f32[2,4,16,128]{3,2,1,0:T(8,128)S(1)} %get-tuple-element.39), channel_id=1, source_target_pairs={{0,17},{1,16},{2,19},{3,18},{4,21},{5,20},{6,23},{7,22},{8,25},{9,... | collective-permute-start | bytes 196616 | tf_op jit(solution)/shard_map/ppermute | solution.py:291
  61.8 4.5 %collective-permute-start.17 = (f32[8,128]{1,0:T(8,128)S(1)}, f32[8,128]{1,0:T(8,128)S(1)}, u32[]{:S(2)}, u32[]{:S(2)}) collective-permute-start(f32[8,128]{1,0:T(8,128)S(1)} %get-tuple-element.33), channel_id=1, source_target_pairs={{0,4},{1,5},{2,6},{3,7},{4,0},{5,1},{6,2},{7,3},{8,12},{9,13},{10,... | collective-permute-start | bytes 12296 | tf_op jit(solution)/shard_map/ppermute | solution.py:291

commit v4 on v3

--- a/solution.py
+++ b/solution.py
@@ -22,52 +22,80 @@
     return total + (pltpu.roll(plane, 1, 1) + pltpu.roll(plane, columns - 1, 1))
 
 
-def contour(first, last, arms, factor, values, store, p_ref, t_ref, s_ref):
+def wavefront(stages):
+    runs = [(first + 2 * k, last + 2 * k, 2 * k, work) for k, (first, last, work) in enumerate(stages)]
+    cuts = sorted({edge for first, last, _, _ in runs for edge in (first, last)})
+    for begin, end in zip(cuts, cuts[1:]):
+        active = [(lag, work) for first, last, lag, work in runs if first <= begin and end <= last]
+
+        def body(i, _, active=active):
+            for lag, work in reversed(active):
+                work(i - lag)
+
+        lax.fori_loop(begin, end, body, None)
+
+
+def two_steps(block, arms, factor, values, middle, store, scratch):
     half = coupling_full / 2
     centre_half, centre_full = 1.0 - 6.0 * half, 1.0 - 6.0 * coupling_full
 
-    def scale(i, _):
-        for j in range(arms):
-            u = factor(j, i)
-            p = u * values(j, i)
-            p_ref[j, i] = p
-            t_ref[j, i] = u * p
-
-    def inner(i, _):
+    def enter(j, i, value, p_ref, t_ref):
+        u = factor(j, i)
+        p = u * value
+        p_ref[j, i] = p
+        t_ref[j, i] = u * p
+
+    def inner(i, p_ref, s_ref):
         for j in range(arms):
             u = factor(j, i)
             p = p_ref[j, i]
             around = beside(p) + (p_ref[j, i - 1] + p_ref[j, i + 1])
             s_ref[j, i] = (u * u) * (centre_half * p + half * around)
 
-    def outer(i, _):
-        for j in range(arms):
-            u = factor(j, i)
-            s, t = s_ref[j, i], t_ref[j, i]
-            s_around = beside(s) + (s_ref[j, i - 1] + s_ref[j, i + 1])
-            t_around = beside(t) + (t_ref[j, i - 1] + t_ref[j, i + 1])
-            halves = (4.0 / 3.0 * centre_half) * s + (4.0 / 3.0 * half) * s_around
-            whole = (centre_full / 3.0) * t + (coupling_full / 3.0) * t_around
-            store(j, i, u * (halves - u * whole))
-
-    lax.fori_loop(first, last, scale, None, unroll=4)
-    lax.fori_loop(first + 1, last - 1, inner, None, unroll=4)
-    lax.fori_loop(first + 2, last - 2, outer, None, unroll=4)
-
-
-def pack_kernel(starts, fields, field_ref, other_ref, own_ref, sems):
+    def outer(j, i, t_ref, s_ref):
+        u = factor(j, i)
+        s, t = s_ref[j, i], t_ref[j, i]
+        s_around = beside(s) + (s_ref[j, i - 1] + s_ref[j, i + 1])
+        t_around = beside(t) + (t_ref[j, i - 1] + t_ref[j, i + 1])
+        halves = (4.0 / 3.0 * centre_half) * s + (4.0 / 3.0 * half) * s_around
+        whole = (centre_full / 3.0) * t + (coupling_full / 3.0) * t_around
+        return u * (halves - u * whole)
+
+    p_one, t_one, s_one, p_two, t_two, s_two = scratch
+
+    def start(i):
+        for j in range(arms):
+            enter(j, i, values(j, i), p_one, t_one)
+
+    def between(i):
+        for j in range(arms):
+            value = outer(j, i, t_one, s_one)
+            middle(j, i, value)
+            enter(j, i, value, p_two, t_two)
+
+    def finish(i):
+        for j in range(arms):
+            store(j, i, outer(j, i, t_two, s_two))
+
+    first, last = block - 2 * reach, 3 * block + 2 * reach
+    wavefront(
+        [
+            (first, last, start),
+            (first + 1, last - 1, lambda i: inner(i, p_one, s_one)),
+            (first + 2, last - 2, between),
+            (first + 3, last - 3, lambda i: inner(i, p_two, s_two)),
+            (first + 4, last - 4, finish),
+        ]
+    )
+
+
+def pack_kernel(starts, fields, field_ref, other_ref, own_ref):
     arms = starts.shape[0] // 2
     side = lax.rem(lax.axis_index("space"), 2)
-    core = lax.rem(lax.axis_index("arm"), 2)
-    copies = [
-        pltpu.make_async_copy(fields.at[core], field_ref, sems.at[0]),
-        pltpu.make_async_copy(starts.at[pl.ds((1 - side) * arms, arms)], other_ref, sems.at[1]),
-        pltpu.make_async_copy(starts.at[pl.ds(side * arms, arms)], own_ref, sems.at[2]),
-    ]
-    for copy in copies:
-        copy.start()
-    for copy in copies:
-        copy.wait()
+    field_ref[...] = fields[lax.rem(lax.axis_index("arm"), 2)]
+    for j in range(arms):
+        other_ref[j] = starts[(1 - side) * arms + j]
+        own_ref[j] = starts[side * arms + j]
 
 
 def places(block):
@@ -84,9 +112,9 @@
 
 
 def forward_kernel(
-    labels, window, swap, straight, fields, f_straight, g_straight, piece, piece_core, piece_chip, piece_both,
+    labels, window, swap, straight, fields, f_swap, g_swap, piece, piece_core, piece_chip, piece_both,
     u_ref, one_ref, low_ref, high_ref, keep_ref, send_ref,
-    q_ref, p_ref, t_ref, s_ref, product_ref,
+    q_ref, product_ref, *scratch,
 ):
     block = fields.shape[1]
     arms = swap.shape[0]
@@ -94,8 +122,8 @@
     core = lax.rem(lax.axis_index("arm"), 2)
     own_at, swap_at, straight_at, across_at = places(block)
     chip = lax.div(lax.axis_index("arm"), 2)
-    here_at = swap_at + chip * (across_at - swap_at)
-    there_at = across_at + chip * (swap_at - across_at)
+    here_at = straight_at + chip * (across_at - straight_at)
+    there_at = across_at + chip * (straight_at - across_at)
 
     def gain(field):
         return jnp.exp(field * (-contour_step / 4))
@@ -107,8 +135,8 @@
         u_ref[1 - core, here_at + i] = gain(piece_core[i])
         u_ref[core, there_at + i] = gain(piece_chip[i])
         u_ref[1 - core, there_at + i] = gain(piece_both[i])
-        u_ref[core, straight_at + i] = gain(f_straight[i])
-        u_ref[1 - core, straight_at + i] = gain(g_straight[i])
+        u_ref[core, swap_at + i] = gain(f_swap[i])
+        u_ref[1 - core, swap_at + i] = gain(g_swap[i])
         for j in range(arms):
             q_ref[j, own_at + i] = window[j, i]
             q_ref[j, across_at + i] = window[arms + j, i]
@@ -127,12 +155,13 @@
     def store(j, i, value):
         q_ref[j, i] = value
 
-    inner_at = block - 2 * reach
-    contour(inner_at, 4 * block - inner_at, arms, factor, values, store, p_ref, t_ref, s_ref)
+    def middle(j, i, value):
+        middle_ref[j, i] = value
+
+    *scratch, middle_ref = scratch
+    two_steps(block, arms, factor, values, middle, store, scratch)
     for j in range(arms):
-        one_ref[j] = q_ref[j, block : 3 * block]
-    inner_at = block - reach
-    contour(inner_at, 4 * block - inner_at, arms, factor, values, store, p_ref, t_ref, s_ref)
+        one_ref[j] = middle_ref[j, block : 3 * block]
 
     def finish(i, _):
         low, high = q_ref[0, block + i], q_ref[0, 2 * block + i]
@@ -151,15 +180,13 @@
 def backward_kernel(
     labels, u_ref, one_ref, two_left, two_low, two_high, two_right,
     j_mine, j_other, j_halo, j_halo_other,
-    keep_ref, send_ref, total_ref,
-    junction_ref, q_ref, p_ref, t_ref, s_ref, density_ref,
+    keep_ref, send_ref,
+    junction_ref, q_ref, density_ref, middle_ref, *scratch,
 ):
     arms, block = two_low.shape[0], two_low.shape[1]
     side = lax.rem(lax.axis_index("space"), 2)
     core = lax.rem(lax.axis_index("arm"), 2)
     kinds = [labels[side * arms + j] for j in range(arms)]
-
-    total_ref[...] = jnp.zeros_like(total_ref)
 
     def fill(i, _):
         junction_ref[block + core * block + i] = j_mine[i]
@@ -168,7 +195,6 @@
         junction_ref[3 * block * core + i] = j_halo_other[i]
         for place, two in enumerate((two_left, two_low, two_high, two_right)):
             whole = junction_ref[place * block + i]
-            total_ref[...] += jnp.sum(whole.reshape(-1, *total_ref.shape), axis=0)
             for j in range(arms):
                 q_ref[j, place * block + i] = whole / two[j, i]
 
@@ -183,13 +209,10 @@
     def store(j, i, value):
         q_ref[j, i] = value
 
-    inner_at = block - 2 * reach
-    contour(inner_at, 4 * block - inner_at, arms, factor, values, store, p_ref, t_ref, s_ref)
-    for j in range(arms):
-        one_ref_j = one_ref[j]
-        density_ref[j] = 0.5 * one_ref_j * q_ref[j, block : 3 * block]
-    inner_at = block - reach
-    contour(inner_at, 4 * block - inner_at, arms, factor, values, store, p_ref, t_ref, s_ref)
+    def middle(j, i, value):
+        middle_ref[j, i] = value
+
+    two_steps(block, arms, factor, values, middle, store, scratch)
 
     is_a = [(kind == 0).astype(jnp.float32) for kind in kinds]
 
@@ -197,11 +220,11 @@
         quarter = 0.25 * junction_ref[block + i]
         total_a = total_b = None
         for j in range(arms):
-            value = density_ref[j, i] + 0.25 * q_ref[j, block + i] + quarter
+            value = 0.5 * one_ref[j, i] * middle_ref[j, block + i] + 0.25 * q_ref[j, block + i] + quarter
             part_a, part_b = is_a[j] * value, (1.0 - is_a[j]) * value
             total_a = part_a if j == 0 else total_a + part_a
             total_b = part_b if j == 0 else total_b + part_b
-        s_ref[0, i], s_ref[1, i] = total_a, total_b
+        density_ref[0, i], density_ref[1, i] = total_a, total_b
 
     lax.fori_loop(0, 2 * block, segment, None)
     chips, owned = keep_ref.shape[0], keep_ref.shape[4]
@@ -212,10 +235,19 @@
             other = pl.ds(pl.multiple_of((2 * chip + 1 - core) * owned, 8), owned)
             for part in range(2):
                 for kind in range(2):
-                    keep_ref[chip, part, kind, i] = s_ref[kind, part * block + i, mine]
-                    send_ref[chip, part, kind, i] = s_ref[kind, part * block + i, other]
+                    keep_ref[chip, part, kind, i] = density_ref[kind, part * block + i, mine]
+                    send_ref[chip, part, kind, i] = density_ref[kind, part * block + i, other]
 
     lax.fori_loop(0, block, spread, None)
+
+
+def total_kernel(*refs):
+    *blocks, total_ref = refs
+    total = jnp.zeros_like(total_ref)
+    for block in blocks:
+        for i in range(block.shape[0]):
+            total = total + jnp.sum(block[i].reshape(-1, *total_ref.shape), axis=0)
+    total_ref[...] = total
 
 
 def meet_kernel(keep, received, own_ref, *out_refs):
@@ -302,18 +334,19 @@
     def to_across(value):
         return send(value, lambda x, c, p, h: (x, c, p + 2 * h - 1, 1 - h))
 
-    field_own, other_set, own_set = pl.pallas_call(
+    field_own, other_set, own_set = call(
         pack_kernel,
-        out_shape=(
+        (
             f32((block, rows, columns)),
             f32((arms, block, rows, columns)),
             f32((arms, block, rows, columns)),
         ),
-        in_specs=[pl.BlockSpec(memory_space=pl.ANY)] * 2,
-        out_specs=[pl.BlockSpec(memory_space=pltpu.VMEM)] * 3,
-        scratch_shapes=[pltpu.SemaphoreType.DMA((3,))],
-    )(starts, fields)
-    field_got = send(field_own, lambda x, c, p, h: (x, c, p + 2 * h - 1 if x else p, 1 - h))
+        [],
+        0,
+        starts,
+        fields,
+    )
+    field_got = send(field_own, lambda x, c, p, h: (x, c, p + 2 * h - 1, 1 - h if x else h))
     across = to_across(other_set)
     swap = to_side(other_set)
     straight = to_straight(own_set)
@@ -323,8 +356,8 @@
         send(field_got, lambda x, c, p, h: (1 - x, c, p, h)),
         send(field_got, lambda x, c, p, h: (1 - x, 1 - c, p, h)),
     ]
-    field_straight = to_straight(field_own)
-    straight_more = to_core(field_straight)
+    field_swap = to_side(field_own)
+    swap_more = to_core(field_swap)
 
     wide = vmem((arms, 4 * block, rows, columns))
     whole = (arms, 2 * block, rows, columns)
@@ -334,9 +367,9 @@
     factor, step_one, low, high, keep, give = call(
         forward_kernel,
         (f32((2, 4 * block, rows, columns)), f32(whole), f32(part), f32(part), f32(one), f32(one)),
-        [wide, wide, wide, wide, vmem((2,) + one)],
+        [wide, vmem((2,) + one)] + [wide] * 7,
         1,
-        labels, window, swap, straight, fields, field_straight, straight_more, *pieces,
+        labels, window, swap, straight, fields, field_swap, swap_more, *pieces,
         cost=8_000_000,
     )
     right = send(low, lambda x, c, p, h: (x, c, p - 1, h))
@@ -351,15 +384,7 @@
     junction_other = to_core(held_junction)
     halo_other = to_core(halo)
 
-    parts = (chips, 2, 2, block, owned, columns)
-    keep, give, total = call(
-        backward_kernel,
-        (f32(parts), f32(parts), f32((8, columns))),
-        [vmem((4 * block, rows, columns)), wide, wide, wide, wide, vmem(whole)],
-        1,
-        labels, factor, step_one, left, low, high, right, junction, junction_other, halo, halo_other,
-        cost=8_000_000,
-    )
+    total = call(total_kernel, f32((8, columns)), [], 0, junction, junction_other, halo, halo_other, cost=1)
     if pairs & (pairs - 1) == 0:
         step = 2
         while step < pairs:
@@ -367,6 +392,15 @@
             step *= 2
     else:
         total = lax.psum(total, "space") / 4.0
+    parts = (chips, 2, 2, block, owned, columns)
+    keep, give = call(
+        backward_kernel,
+        (f32(parts), f32(parts)),
+        [vmem((4 * block, rows, columns)), wide, vmem((2,) + whole[1:])] + [wide] * 7,
+        1,
+        labels, factor, step_one, left, low, high, right, junction, junction_other, halo, halo_other,
+        cost=8_000_000,
+    )
     to_places = other_chips(chips)
     own, *gives = call(
         meet_kernel, (f32(parts[2:]),) * (1 + len(to_places)), [], 0, keep, to_core(give)

time: 67.3 us -> 66.9 us (level)
  Pallas kernels: 12 us -> 9.84 us
  local copies, waits for them, and re-layouts: 0.01 us -> 1.99 us
  starting transfers between devices: 35.1 us -> 33.2 us
  waiting for transfers between devices: 19.3 us -> 20.8 us
    pallas_call x1 -> x0, Pallas kernels: 2.03 us -> none  [local(): pl.pallas_call(pack_kernel, out_shape=(f32((block, rows, columns)), f32((...]
    unnamed x6 -> x8, local copies, waits for them, and re-layouts: 0.01 us -> 1.99 us
    ppermute x22, starting transfers between devices: 35.1 us -> 33.2 us  [send(): return lax.ppermute(value, AXES, perm)]
    ppermute x22, waiting for transfers between devices: 19.3 us -> 20.8 us  [send(): return lax.ppermute(value, AXES, perm)]
    pallas_call x5 -> x7, Pallas kernels: 9.95 us -> 9.84 us  [call(): pl.pallas_call(kernel, out_shape=out_shape, in_specs=specs, out_specs=jax...]
  transfers between devices with their start and end apart: 22 -> 22, of which waited for: 9 -> 11; matrix products, arithmetic and copies ran while one was open for 0% -> 0% of each run, Pallas kernels for 0% -> 0%
where the time goes in v4:
time: 66.9 us; the launch traced here: 66.7 us
  starting transfers between devices  33.2 us (50%)
  waiting for transfers between devices  20.8 us (31%)
  Pallas kernels  9.84 us (15%)
  local copies, waits for them, and re-layouts  1.99 us (3%)
  between operations  0.74 us (1%)
    ppermute x22, starting transfers between devices, send(): return lax.ppermute(value, AXES, perm)  33.2 us
    ppermute x22, waiting for transfers between devices, send(): return lax.ppermute(value, AXES, perm)  20.8 us
    pallas_call x7, Pallas kernels, call(): pl.pallas_call(kernel, out_shape=out_shape, in_specs=specs, out_specs=jax...  9.84 us
    unnamed x8, local copies, waits for them, and re-layouts  1.99 us
  transfers between devices with their start and end apart: 22, of which 11 were waited for; matrix products, arithmetic and copies ran while one was open for 0% of the time, Pallas kernels for 0%

profile of v4, /device:TPU:0, one launch (start us, length us, event | category | flops | bytes accessed | tf_op | source)
XLA Modules:
  0.0 66.7 jit_solution(16528632187109235618)
XLA Ops:
  0.6 0.0 copy-start
  0.6 0.9 %copy-done = f32[2,4,64,128]{3,2,1,0:T(8,128)S(1)} copy-done((f32[2,4,64,128]{3,2,1,0:T(8,128)S(1)}, f32[2,4,64,128]{3,2,1,0:T(8,128)}, u32[]{:S(2)}) %copy-start) | copy-done | bytes 262168
  1.6 0.0 copy-start.2
  1.6 1.0 %copy-done.2 = f32[4,4,64,128]{3,2,1,0:T(8,128)S(1)} copy-done((f32[4,4,64,128]{3,2,1,0:T(8,128)S(1)}, f32[4,4,64,128]{3,2,1,0:T(8,128)}, u32[]{:S(2)}) %copy-start.2) | copy-done | bytes 524312
  2.7 5.1 %collective-permute-start.5 = (f32[4,64,128]{2,1,0:T(8,128)S(1)}, f32[4,64,128]{2,1,0:T(8,128)S(1)}, u32[]{:S(2)}, u32[]{:S(2)}) collective-permute-start(f32[4,64,128]{2,1,0:T(8,128)S(1)} %get-tuple-element.22), channel_id=1, source_target_pairs={{0,6},{1,3},{2,0},{3,5},{4,2},{5,7},{6,4},{7,1},{8,14},{9,11},{10,... | collective-permute-start | bytes 393224 | tf_op jit(solution)/shard_map/ppermute | solution.py:323
  7.8 1.2 %collective-permute-start = (f32[2,4,64,128]{3,2,1,0:T(8,128)S(1)}, f32[2,4,64,128]{3,2,1,0:T(8,128)S(1)}, u32[]{:S(2)}, u32[]{:S(2)}) collective-permute-start(f32[2,4,64,128]{3,2,1,0:T(8,128)S(1)} %get-tuple-element.20), channel_id=1, source_target_pairs={{0,7},{1,2},{2,1},{3,4},{4,3},{5,6},{6,5},{7,0},{8,15},{9,10},{10,... | collective-permute-start | bytes 786440 | tf_op jit(solution)/shard_map/ppermute | solution.py:323
  9.0 0.0 collective-permute-start.3
  9.0 2.7 %collective-permute-done.5.piece = f32[4,64,128]{2,1,0:T(8,128)S(1)} collective-permute-done((f32[4,64,128]{2,1,0:T(8,128)S(1)}, f32[4,64,128]{2,1,0:T(8,128)S(1)}, u32[]{:S(2)}, u32[]{:S(2)}) %collective-permute-start.5) | collective-permute-done | bytes 131104 | tf_op jit(solution)/shard_map/ppermute | solution.py:323
  11.7 0.7 %collective-permute-start.8 = (f32[4,64,128]{2,1,0:T(8,128)S(1)}, f32[4,64,128]{2,1,0:T(8,128)S(1)}, u32[]{:S(2)}, u32[]{:S(2)}) collective-permute-start(f32[4,64,128]{2,1,0:T(8,128)S(1)} %collective-permute-done.5.piece), channel_id=1, source_target_pairs={{0,24},{1,25},{2,26},{3,27},{4,28},{5,29},{6,30},{7,31},{8,16},{9,... | collective-permute-start | bytes 393224 | tf_op jit(solution)/shard_map/ppermute | solution.py:323
  12.4 0.0 copy-start.1
  12.4 0.0 copy-start.3
  12.4 3.6 %collective-permute-start.2 = (f32[2,4,64,128]{3,2,1,0:T(8,128)S(1)}, f32[2,4,64,128]{3,2,1,0:T(8,128)S(1)}, u32[]{:S(2)}, u32[]{:S(2)}) collective-permute-start(f32[2,4,64,128]{3,2,1,0:T(8,128)S(1)} %get-tuple-element.21), channel_id=1, source_target_pairs={{0,6},{1,3},{2,0},{3,5},{4,2},{5,7},{6,4},{7,1},{8,14},{9,11},{10,... | collective-permute-start | bytes 786440 | tf_op jit(solution)/shard_map/ppermute | solution.py:323
  16.0 0.0 collective-permute-start.1
  16.0 3.9 %collective-permute-done.3.f_swap = f32[4,64,128]{2,1,0:T(8,128)S(1)} collective-permute-done((f32[4,64,128]{2,1,0:T(8,128)S(1)}, f32[4,64,128]{2,1,0:T(8,128)S(1)}, u32[]{:S(2)}, u32[]{:S(2)}) %collective-permute-start.3) | collective-permute-done | bytes 131104 | tf_op jit(solution)/shard_map/ppermute | solution.py:323
  19.9 2.4 %collective-permute-start.7 = (f32[4,64,128]{2,1,0:T(8,128)S(1)}, f32[4,64,128]{2,1,0:T(8,128)S(1)}, u32[]{:S(2)}, u32[]{:S(2)}) collective-permute-start(f32[4,64,128]{2,1,0:T(8,128)S(1)} %collective-permute-done.5.piece), channel_id=1, source_target_pairs={{0,16},{1,17},{2,18},{3,19},{4,20},{5,21},{6,22},{7,23},{8,24},{9,... | collective-permute-start | bytes 393224 | tf_op jit(solution)/shard_map/ppermute | solution.py:323
  22.4 0.0 collective-permute-done.8.piece_both
  22.4 0.0 collective-permute-start.6
  22.4 0.0 collective-permute-done.across
  22.4 0.5 collective-permute-start.4
  22.9 2.5 %collective-permute-done.7.piece_chip = f32[4,64,128]{2,1,0:T(8,128)S(1)} collective-permute-done((f32[4,64,128]{2,1,0:T(8,128)S(1)}, f32[4,64,128]{2,1,0:T(8,128)S(1)}, u32[]{:S(2)}, u32[]{:S(2)}) %collective-permute-start.7) | collective-permute-done | bytes 131104 | tf_op jit(solution)/shard_map/ppermute | solution.py:323
  25.4 0.0 collective-permute-done.6.piece_core
  25.4 0.0 collective-permute-done.4.g_swap
  25.4 0.0 collective-permute-done.2.straight
  25.4 0.0 collective-permute-done.1.swap
  25.4 0.0 copy-done.1
  25.4 0.0 copy-done.3
  25.4 4.4 %shard_map.52 = (f32[2,16,64,128]{3,2,1,0:T(8,128)S(1)}, f32[2,8,64,128]{3,2,1,0:T(8,128)S(1)}, f32[2,4,64,128]{3,2,1,0:T(8,128)S(1)}, f32[2,4,64,128]{3,2,1,0:T...) custom-call(s32[4]{0:T(128)S(1)} %copy-done.3, f32[4,4,64,128]{3,2,1,0:T(8,128)S(1)} %shard_map.51.window, ...), custom_call_target="tpu_custom_call" | custom-call | flops 8000000 | bytes 8000000 | tf_op jit(solution)/shard_map/pallas_call | solution.py:294
  29.9 0.1 collective-permute-start.9
  29.9 1.3 %collective-permute-done.9 = f32[4,64,128]{2,1,0:T(8,128)S(1)} collective-permute-done((f32[4,64,128]{2,1,0:T(8,128)S(1)}, f32[4,64,128]{2,1,0:T(8,128)S(1)}, u32[]{:S(2)}, u32[]{:S(2)}) %collective-permute-start.9) | collective-permute-done | bytes 131104 | tf_op jit(solution)/shard_map/ppermute | solution.py:323
  31.3 0.1 collective-permute-start.10
  31.4 1.6 %collective-permute-start.12 = (f32[2,4,64,128]{3,2,1,0:T(8,128)S(1)}, f32[2,4,64,128]{3,2,1,0:T(8,128)S(1)}, u32[]{:S(2)}, u32[]{:S(2)}) collective-permute-start(f32[2,4,64,128]{3,2,1,0:T(8,128)S(1)} %get-tuple-element.25.two_high), channel_id=1, source_target_pairs={{0,2},{1,3},{2,4},{3,5},{4,6},{5,7},{6,0},{7,1},{8,10},{9,11},{10,... | collective-permute-start | bytes 786440 | tf_op jit(solution)/shard_map/ppermute | solution.py:323
  33.0 3.8 %collective-permute-start.13 = (f32[2,4,64,128]{3,2,1,0:T(8,128)S(1)}, f32[2,4,64,128]{3,2,1,0:T(8,128)S(1)}, u32[]{:S(2)}, u32[]{:S(2)}) collective-permute-start(f32[2,4,64,128]{3,2,1,0:T(8,128)S(1)} %get-tuple-element.26.two_low), channel_id=1, source_target_pairs={{0,6},{1,7},{2,0},{3,1},{4,2},{5,3},{6,4},{7,5},{8,14},{9,15},{10,... | collective-permute-start | bytes 786440 | tf_op jit(solution)/shard_map/ppermute | solution.py:323
  36.8 0.1 collective-permute-done.10
  36.9 2.4 %collective-permute-start.11 = (f32[4,64,128]{2,1,0:T(8,128)S(1)}, f32[4,64,128]{2,1,0:T(8,128)S(1)}, u32[]{:S(2)}, u32[]{:S(2)}) collective-permute-start(f32[4,64,128]{2,1,0:T(8,128)S(1)} %mul.10), channel_id=1, source_target_pairs={{0,16},{1,17},{2,18},{3,19},{4,20},{5,21},{6,22},{7,23},{8,24},{9,... | collective-permute-start | bytes 393224 | tf_op jit(solution)/shard_map/ppermute | solution.py:323
  39.3 3.0 %collective-permute-done.11 = f32[4,64,128]{2,1,0:T(8,128)S(1)} collective-permute-done((f32[4,64,128]{2,1,0:T(8,128)S(1)}, f32[4,64,128]{2,1,0:T(8,128)S(1)}, u32[]{:S(2)}, u32[]{:S(2)}) %collective-permute-start.11) | collective-permute-done | bytes 131104 | tf_op jit(solution)/shard_map/ppermute | solution.py:323
  42.3 3.6 %collective-permute-start.15 = (f32[4,64,128]{2,1,0:T(8,128)S(1)}, f32[4,64,128]{2,1,0:T(8,128)S(1)}, u32[]{:S(2)}, u32[]{:S(2)}) collective-permute-start(f32[4,64,128]{2,1,0:T(8,128)S(1)} %mul.11.refs_0_.j_mine), channel_id=1, source_target_pairs={{0,6},{1,7},{2,0},{3,1},{4,2},{5,3},{6,4},{7,5},{8,10},{9,11},{10,... | collective-permute-start | bytes 393224 | tf_op jit(solution)/shard_map/ppermute | solution.py:323
  45.9 0.0 collective-permute-done.12.two_left
  45.9 0.4 collective-permute-done.13.two_right
  46.4 0.0 collective-permute-start.14
  46.4 2.1 %collective-permute-done.15.refs_2_.j_halo = f32[4,64,128]{2,1,0:T(8,128)S(1)} collective-permute-done((f32[4,64,128]{2,1,0:T(8,128)S(1)}, f32[4,64,128]{2,1,0:T(8,128)S(1)}, u32[]{:S(2)}, u32[]{:S(2)}) %collective-permute-start.15) | collective-permute-done | bytes 131104 | tf_op jit(solution)/shard_map/ppermute | solution.py:323
  48.5 2.2 %collective-permute-start.16 = (f32[4,64,128]{2,1,0:T(8,128)S(1)}, f32[4,64,128]{2,1,0:T(8,128)S(1)}, u32[]{:S(2)}, u32[]{:S(2)}) collective-permute-start(f32[4,64,128]{2,1,0:T(8,128)S(1)} %collective-permute-done.15.refs_2_.j_halo), channel_id=1, source_target_pairs={{0,8},{1,9},{2,10},{3,11},{4,12},{5,13},{6,14},{7,15},{8,0},{9,1},... | collective-permute-start | bytes 393224 | tf_op jit(solution)/shard_map/ppermute | solution.py:323
  50.6 0.0 collective-permute-done.14.refs_1_.j_other
  50.6 1.0 %collective-permute-done.16.refs_3_.j_halo_other = f32[4,64,128]{2,1,0:T(8,128)S(1)} collective-permute-done((f32[4,64,128]{2,1,0:T(8,128)S(1)}, f32[4,64,128]{2,1,0:T(8,128)S(1)}, u32[]{:S(2)}, u32[]{:S(2)}) %collective-permute-start.16) | collective-permute-done | bytes 131104 | tf_op jit(solution)/shard_map/ppermute | solution.py:323
  51.6 4.5 %shard_map.54 = (f32[2,2,2,4,16,128]{5,4,3,2,1,0:T(8,128)S(1)}, f32[2,2,2,4,16,128]{5,4,3,2,1,0:T(8,128)S(1)}) custom-call(s32[4]{0:T(128)S(1)} %copy-done.3, f32[2,16,64,128]{3,2,1,0:T(8,128)S(1)} %get-tuple-element.28.u_ref, f32[2,8,64,128]{3,2,1,0:T(8,128)S(1)} %get-tuple-element.29.one_ref, f32[2,4,64,128]{3,2,1,0:T(8,128)S(1)} %collective-permute-done.12.two_left, ...), custom_call_target="tpu_custom_call" | custom-call | flops 8000000 | bytes 8000000 | tf_op jit(solution)/shard_map/pallas_call | solution.py:294
  56.1 0.4 collective-permute-start.18
  56.5 1.2 %collective-permute-done.18.received = f32[2,2,2,4,16,128]{5,4,3,2,1,0:T(8,128)S(1)} collective-permute-done((f32[2,2,2,4,16,128]{5,4,3,2,1,0:T(8,128)S(1)}, f32[2,2,2,4,16,128]{5,4,3,2,1,0:T(8,128)S(1)}, u32[]{:S(2)}, u32[]{:S(2)}) %collective-permute-start.18) | collective-permute-done | bytes 262176 | tf_op jit(solution)/shard_map/ppermute | solution.py:323
  57.7 0.3 collective-permute-start.19
  58.1 1.9 %collective-permute-start.20 = (f32[2,4,16,128]{3,2,1,0:T(8,128)S(1)}, f32[2,4,16,128]{3,2,1,0:T(8,128)S(1)}, u32[]{:S(2)}, u32[]{:S(2)}) collective-permute-start(f32[2,4,16,128]{3,2,1,0:T(8,128)S(1)} %get-tuple-element.36), channel_id=1, source_target_pairs={{0,16},{1,17},{2,18},{3,19},{4,20},{5,21},{6,22},{7,23},{8,24},{9,... | collective-permute-start | bytes 196616 | tf_op jit(solution)/shard_map/ppermute | solution.py:323
  59.9 1.4 %collective-permute-start.21 = (f32[2,4,16,128]{3,2,1,0:T(8,128)S(1)}, f32[2,4,16,128]{3,2,1,0:T(8,128)S(1)}, u32[]{:S(2)}, u32[]{:S(2)}) collective-permute-start(f32[2,4,16,128]{3,2,1,0:T(8,128)S(1)} %get-tuple-element.37), channel_id=1, source_target_pairs={{0,17},{1,16},{2,19},{3,18},{4,21},{5,20},{6,23},{7,22},{8,25},{9,... | collective-permute-start | bytes 196616 | tf_op jit(solution)/shard_map/ppermute | solution.py:323
  61.3 2.0 %collective-permute-start.17 = (f32[8,128]{1,0:T(8,128)S(1)}, f32[8,128]{1,0:T(8,128)S(1)}, u32[]{:S(2)}, u32[]{:S(2)}) collective-permute-start(f32[8,128]{1,0:T(8,128)S(1)} %shard_map.53), channel_id=1, source_target_pairs={{0,4},{1,5},{2,6},{3,7},{4,0},{5,1},{6,2},{7,3},{8,12},{9,13},{10,... | collective-permute-start | bytes 12296 | tf_op jit(solution)/shard_map/ppermute | solution.py:323
  63.3 2.6 %collective-permute-done.17 = f32[8,128]{1,0:T(8,128)S(1)} collective-permute-done((f32[8,128]{1,0:T(8,128)S(1)}, f32[8,128]{1,0:T(8,128)S(1)}, u32[]{:S(2)}, u32[]{:S(2)}) %collective-permute-start.17) | collective-permute-done | bytes 4128 | tf_op jit(solution)/shard_map/ppermute | solution.py:323
  65.9 0.0 collective-permute-done.19.refs_0_
  65.9 0.0 collective-permute-done.20.refs_1_
  65.9 0.0 collective-permute-done.21.refs_2_
  65.9 0.8 %shard_map.56 = (f32[2,4,16,128]{3,2,1,0:T(8,128)}, f32[2,4,16,128]{3,2,1,0:T(8,128)}) custom-call(f32[2,4,64,128]{3,2,1,0:T(8,128)S(1)} %copy-done.1, f32[8,128]{1,0:T(8,128)S(1)} %add.3.total, f32[2,4,16,128]{3,2,1,0:T(8,128)S(1)} %get-tuple-element.34.own, f32[2,4,16,128]{3,2,1,0:T(8,128)S(1)} %collective-permute-done.19.refs_0_, ...), custom_call_target="tpu_custom_call" | custom-call | flops 1000000 | bytes 1000000 | tf_op jit(solution)/shard_map/pallas_call | solution.py:294
  (8 shorter events, 0.2 us)
Async XLA Ops:
  0.6 1.0 %copy-start = (f32[2,4,64,128]{3,2,1,0:T(8,128)S(1)}, f32[2,4,64,128]{3,2,1,0:T(8,128)}, u32[]{:S(2)}) copy-start(f32[2,4,64,128]{3,2,1,0:T(8,128)} %fields.5) | copy-start | bytes 786436
  1.6 1.0 %copy-start.2 = (f32[4,4,64,128]{3,2,1,0:T(8,128)S(1)}, f32[4,4,64,128]{3,2,1,0:T(8,128)}, u32[]{:S(2)}) copy-start(f32[4,4,64,128]{3,2,1,0:T(8,128)} %starts.3) | copy-start | bytes 1572868
  2.7 9.0 %collective-permute-start.5 = (f32[4,64,128]{2,1,0:T(8,128)S(1)}, f32[4,64,128]{2,1,0:T(8,128)S(1)}, u32[]{:S(2)}, u32[]{:S(2)}) collective-permute-start(f32[4,64,128]{2,1,0:T(8,128)S(1)} %get-tuple-element.22), channel_id=1, source_target_pairs={{0,6},{1,3},{2,0},{3,5},{4,2},{5,7},{6,4},{7,1},{8,14},{9,11},{10,... | collective-permute-start | bytes 393224 | tf_op jit(solution)/shard_map/ppermute | solution.py:323
  7.8 14.6 %collective-permute-start = (f32[2,4,64,128]{3,2,1,0:T(8,128)S(1)}, f32[2,4,64,128]{3,2,1,0:T(8,128)S(1)}, u32[]{:S(2)}, u32[]{:S(2)}) collective-permute-start(f32[2,4,64,128]{3,2,1,0:T(8,128)S(1)} %get-tuple-element.20), channel_id=1, source_target_pairs={{0,7},{1,2},{2,1},{3,4},{4,3},{5,6},{6,5},{7,0},{8,15},{9,10},{10,... | collective-permute-start | bytes 786440 | tf_op jit(solution)/shard_map/ppermute | solution.py:323
  9.0 11.0 %collective-permute-start.3 = (f32[4,64,128]{2,1,0:T(8,128)S(1)}, f32[4,64,128]{2,1,0:T(8,128)S(1)}, u32[]{:S(2)}, u32[]{:S(2)}) collective-permute-start(f32[4,64,128]{2,1,0:T(8,128)S(1)} %get-tuple-element.22), channel_id=1, source_target_pairs={{0,1},{1,0},{2,3},{3,2},{4,5},{5,4},{6,7},{7,6},{8,9},{9,8},{10,11... | collective-permute-start | bytes 393224 | tf_op jit(solution)/shard_map/ppermute | solution.py:323
  11.7 10.7 %collective-permute-start.8 = (f32[4,64,128]{2,1,0:T(8,128)S(1)}, f32[4,64,128]{2,1,0:T(8,128)S(1)}, u32[]{:S(2)}, u32[]{:S(2)}) collective-permute-start(f32[4,64,128]{2,1,0:T(8,128)S(1)} %collective-permute-done.5.piece), channel_id=1, source_target_pairs={{0,24},{1,25},{2,26},{3,27},{4,28},{5,29},{6,30},{7,31},{8,16},{9,... | collective-permute-start | bytes 393224 | tf_op jit(solution)/shard_map/ppermute | solution.py:323
  12.4 13.0 %copy-start.1 = (f32[2,4,64,128]{3,2,1,0:T(8,128)S(1)}, f32[2,4,64,128]{3,2,1,0:T(8,128)}, u32[]{:S(2)}) copy-start(f32[2,4,64,128]{3,2,1,0:T(8,128)} %fields.5) | copy-start | bytes 786436
  12.4 13.0 %copy-start.3 = (s32[4]{0:T(128)S(1)}, s32[4]{0:T(128)}, u32[]{:S(2)}) copy-start(s32[4]{0:T(128)} %labels.3) | copy-start | bytes 52
  12.4 13.0 %collective-permute-start.2 = (f32[2,4,64,128]{3,2,1,0:T(8,128)S(1)}, f32[2,4,64,128]{3,2,1,0:T(8,128)S(1)}, u32[]{:S(2)}, u32[]{:S(2)}) collective-permute-start(f32[2,4,64,128]{3,2,1,0:T(8,128)S(1)} %get-tuple-element.21), channel_id=1, source_target_pairs={{0,6},{1,3},{2,0},{3,5},{4,2},{5,7},{6,4},{7,1},{8,14},{9,11},{10,... | collective-permute-start | bytes 786440 | tf_op jit(solution)/shard_map/ppermute | solution.py:323
  16.0 9.4 %collective-permute-start.1 = (f32[2,4,64,128]{3,2,1,0:T(8,128)S(1)}, f32[2,4,64,128]{3,2,1,0:T(8,128)S(1)}, u32[]{:S(2)}, u32[]{:S(2)}) collective-permute-start(f32[2,4,64,128]{3,2,1,0:T(8,128)S(1)} %get-tuple-element.20), channel_id=1, source_target_pairs={{0,1},{1,0},{2,3},{3,2},{4,5},{5,4},{6,7},{7,6},{8,9},{9,8},{10,11... | collective-permute-start | bytes 786440 | tf_op jit(solution)/shard_map/ppermute | solution.py:323
  19.9 5.5 %collective-permute-start.7 = (f32[4,64,128]{2,1,0:T(8,128)S(1)}, f32[4,64,128]{2,1,0:T(8,128)S(1)}, u32[]{:S(2)}, u32[]{:S(2)}) collective-permute-start(f32[4,64,128]{2,1,0:T(8,128)S(1)} %collective-permute-done.5.piece), channel_id=1, source_target_pairs={{0,16},{1,17},{2,18},{3,19},{4,20},{5,21},{6,22},{7,23},{8,24},{9,... | collective-permute-start | bytes 393224 | tf_op jit(solution)/shard_map/ppermute | solution.py:323
  22.4 3.0 %collective-permute-start.6 = (f32[4,64,128]{2,1,0:T(8,128)S(1)}, f32[4,64,128]{2,1,0:T(8,128)S(1)}, u32[]{:S(2)}, u32[]{:S(2)}) collective-permute-start(f32[4,64,128]{2,1,0:T(8,128)S(1)} %collective-permute-done.5.piece), channel_id=1, source_target_pairs={{0,8},{1,9},{2,10},{3,11},{4,12},{5,13},{6,14},{7,15},{8,0},{9,1},... | collective-permute-start | bytes 393224 | tf_op jit(solution)/shard_map/ppermute | solution.py:323
  22.4 3.0 %collective-permute-start.4 = (f32[4,64,128]{2,1,0:T(8,128)S(1)}, f32[4,64,128]{2,1,0:T(8,128)S(1)}, u32[]{:S(2)}, u32[]{:S(2)}) collective-permute-start(f32[4,64,128]{2,1,0:T(8,128)S(1)} %collective-permute-done.3.f_swap), channel_id=1, source_target_pairs={{0,8},{1,9},{2,10},{3,11},{4,12},{5,13},{6,14},{7,15},{8,0},{9,1},... | collective-permute-start | bytes 393224 | tf_op jit(solution)/shard_map/ppermute | solution.py:323
  29.9 1.4 %collective-permute-start.9 = (f32[4,64,128]{2,1,0:T(8,128)S(1)}, f32[4,64,128]{2,1,0:T(8,128)S(1)}, u32[]{:S(2)}, u32[]{:S(2)}) collective-permute-start(f32[4,64,128]{2,1,0:T(8,128)S(1)} %get-tuple-element.24), channel_id=1, source_target_pairs={{0,8},{1,9},{2,10},{3,11},{4,12},{5,13},{6,14},{7,15},{8,0},{9,1},... | collective-permute-start | bytes 393224 | tf_op jit(solution)/shard_map/ppermute | solution.py:323
  31.3 5.6 %collective-permute-start.10 = (f32[4,64,128]{2,1,0:T(8,128)S(1)}, f32[4,64,128]{2,1,0:T(8,128)S(1)}, u32[]{:S(2)}, u32[]{:S(2)}) collective-permute-start(f32[4,64,128]{2,1,0:T(8,128)S(1)} %mul.9), channel_id=1, source_target_pairs={{0,1},{1,0},{2,3},{3,2},{4,5},{5,4},{6,7},{7,6},{8,9},{9,8},{10,11... | collective-permute-start | bytes 393224 | tf_op jit(solution)/shard_map/ppermute | solution.py:323
  31.4 14.6 %collective-permute-start.12 = (f32[2,4,64,128]{3,2,1,0:T(8,128)S(1)}, f32[2,4,64,128]{3,2,1,0:T(8,128)S(1)}, u32[]{:S(2)}, u32[]{:S(2)}) collective-permute-start(f32[2,4,64,128]{3,2,1,0:T(8,128)S(1)} %get-tuple-element.25.two_high), channel_id=1, source_target_pairs={{0,2},{1,3},{2,4},{3,5},{4,6},{5,7},{6,0},{7,1},{8,10},{9,11},{10,... | collective-permute-start | bytes 786440 | tf_op jit(solution)/shard_map/ppermute | solution.py:323
  33.0 13.4 %collective-permute-start.13 = (f32[2,4,64,128]{3,2,1,0:T(8,128)S(1)}, f32[2,4,64,128]{3,2,1,0:T(8,128)S(1)}, u32[]{:S(2)}, u32[]{:S(2)}) collective-permute-start(f32[2,4,64,128]{3,2,1,0:T(8,128)S(1)} %get-tuple-element.26.two_low), channel_id=1, source_target_pairs={{0,6},{1,7},{2,0},{3,1},{4,2},{5,3},{6,4},{7,5},{8,14},{9,15},{10,... | collective-permute-start | bytes 786440 | tf_op jit(solution)/shard_map/ppermute | solution.py:323
  36.9 5.4 %collective-permute-start.11 = (f32[4,64,128]{2,1,0:T(8,128)S(1)}, f32[4,64,128]{2,1,0:T(8,128)S(1)}, u32[]{:S(2)}, u32[]{:S(2)}) collective-permute-start(f32[4,64,128]{2,1,0:T(8,128)S(1)} %mul.10), channel_id=1, source_target_pairs={{0,16},{1,17},{2,18},{3,19},{4,20},{5,21},{6,22},{7,23},{8,24},{9,... | collective-permute-start | bytes 393224 | tf_op jit(solution)/shard_map/ppermute | solution.py:323
  42.3 6.2 %collective-permute-start.15 = (f32[4,64,128]{2,1,0:T(8,128)S(1)}, f32[4,64,128]{2,1,0:T(8,128)S(1)}, u32[]{:S(2)}, u32[]{:S(2)}) collective-permute-start(f32[4,64,128]{2,1,0:T(8,128)S(1)} %mul.11.refs_0_.j_mine), channel_id=1, source_target_pairs={{0,6},{1,7},{2,0},{3,1},{4,2},{5,3},{6,4},{7,5},{8,10},{9,11},{10,... | collective-permute-start | bytes 393224 | tf_op jit(solution)/shard_map/ppermute | solution.py:323
  46.4 4.2 %collective-permute-start.14 = (f32[4,64,128]{2,1,0:T(8,128)S(1)}, f32[4,64,128]{2,1,0:T(8,128)S(1)}, u32[]{:S(2)}, u32[]{:S(2)}) collective-permute-start(f32[4,64,128]{2,1,0:T(8,128)S(1)} %mul.11.refs_0_.j_mine), channel_id=1, source_target_pairs={{0,8},{1,9},{2,10},{3,11},{4,12},{5,13},{6,14},{7,15},{8,0},{9,1},... | collective-permute-start | bytes 393224 | tf_op jit(solution)/shard_map/ppermute | solution.py:323
  48.5 3.1 %collective-permute-start.16 = (f32[4,64,128]{2,1,0:T(8,128)S(1)}, f32[4,64,128]{2,1,0:T(8,128)S(1)}, u32[]{:S(2)}, u32[]{:S(2)}) collective-permute-start(f32[4,64,128]{2,1,0:T(8,128)S(1)} %collective-permute-done.15.refs_2_.j_halo), channel_id=1, source_target_pairs={{0,8},{1,9},{2,10},{3,11},{4,12},{5,13},{6,14},{7,15},{8,0},{9,1},... | collective-permute-start | bytes 393224 | tf_op jit(solution)/shard_map/ppermute | solution.py:323
  56.1 1.6 %collective-permute-start.18 = (f32[2,2,2,4,16,128]{5,4,3,2,1,0:T(8,128)S(1)}, f32[2,2,2,4,16,128]{5,4,3,2,1,0:T(8,128)S(1)}, u32[]{:S(2)}, u32[]{:S(2)}) collective-permute-start(f32[2,2,2,4,16,128]{5,4,3,2,1,0:T(8,128)S(1)} %get-tuple-element.33), channel_id=1, source_target_pairs={{0,8},{1,9},{2,10},{3,11},{4,12},{5,13},{6,14},{7,15},{8,0},{9,1},... | collective-permute-start | bytes 786440 | tf_op jit(solution)/shard_map/ppermute | solution.py:323
  57.7 8.2 %collective-permute-start.19 = (f32[2,4,16,128]{3,2,1,0:T(8,128)S(1)}, f32[2,4,16,128]{3,2,1,0:T(8,128)S(1)}, u32[]{:S(2)}, u32[]{:S(2)}) collective-permute-start(f32[2,4,16,128]{3,2,1,0:T(8,128)S(1)} %get-tuple-element.35), channel_id=1, source_target_pairs={{0,1},{1,0},{2,3},{3,2},{4,5},{5,4},{6,7},{7,6},{8,9},{9,8},{10,11... | collective-permute-start | bytes 196616 | tf_op jit(solution)/shard_map/ppermute | solution.py:323
  58.1 7.8 %collective-permute-start.20 = (f32[2,4,16,128]{3,2,1,0:T(8,128)S(1)}, f32[2,4,16,128]{3,2,1,0:T(8,128)S(1)}, u32[]{:S(2)}, u32[]{:S(2)}) collective-permute-start(f32[2,4,16,128]{3,2,1,0:T(8,128)S(1)} %get-tuple-element.36), channel_id=1, source_target_pairs={{0,16},{1,17},{2,18},{3,19},{4,20},{5,21},{6,22},{7,23},{8,24},{9,... | collective-permute-start | bytes 196616 | tf_op jit(solution)/shard_map/ppermute | solution.py:323
  59.9 6.0 %collective-permute-start.21 = (f32[2,4,16,128]{3,2,1,0:T(8,128)S(1)}, f32[2,4,16,128]{3,2,1,0:T(8,128)S(1)}, u32[]{:S(2)}, u32[]{:S(2)}) collective-permute-start(f32[2,4,16,128]{3,2,1,0:T(8,128)S(1)} %get-tuple-element.37), channel_id=1, source_target_pairs={{0,17},{1,16},{2,19},{3,18},{4,21},{5,20},{6,23},{7,22},{8,25},{9,... | collective-permute-start | bytes 196616 | tf_op jit(solution)/shard_map/ppermute | solution.py:323
  61.3 4.6 %collective-permute-start.17 = (f32[8,128]{1,0:T(8,128)S(1)}, f32[8,128]{1,0:T(8,128)S(1)}, u32[]{:S(2)}, u32[]{:S(2)}) collective-permute-start(f32[8,128]{1,0:T(8,128)S(1)} %shard_map.53), channel_id=1, source_target_pairs={{0,4},{1,5},{2,6},{3,7},{4,0},{5,1},{6,2},{7,3},{8,12},{9,13},{10,... | collective-permute-start | bytes 12296 | tf_op jit(solution)/shard_map/ppermute | solution.py:323

commit v5 on v4

--- a/solution.py
+++ b/solution.py
@@ -239,6 +239,19 @@
                     send_ref[chip, part, kind, i] = density_ref[kind, part * block + i, other]
 
     lax.fori_loop(0, block, spread, None)
+
+
+def product_kernel(one, other, *out_refs):
+    planes = one.shape[0] // len(out_refs)
+    for k, out_ref in enumerate(out_refs):
+        part = slice(k * planes, (k + 1) * planes)
+        out_ref[...] = one[part] * other[part]
+
+
+def join_kernel(upper, upper_other, lower, lower_other, out_ref):
+    planes = upper.shape[0]
+    out_ref[:planes] = upper[...] * upper_other[...]
+    out_ref[planes:] = lower[...] * lower_other[...]
 
 
 def total_kernel(*refs):
@@ -308,7 +321,7 @@
     held, block, rows, columns = starts.shape
     arms = held // 2
     owned = rows // arm_size
-    if chips != 2 or held % 2 or space_size % 2:
+    if chips != 2 or held % 2 or space_size % 2 or block % 2:
         raise ValueError("unsupported mesh")
     side = lax.rem(lax.axis_index("space"), 2)
     core = lax.rem(lax.axis_index("arm"), 2)
@@ -327,6 +340,9 @@
 
     def to_side(value):
         return send(value, lambda x, c, p, h: (x, c, p, 1 - h))
+
+    def to_chip(value):
+        return send(value, lambda x, c, p, h: (x + 1, c, p, h))
 
     def to_straight(value):
         return send(value, lambda x, c, p, h: (x, c, p + 2 * h - 1, h))
@@ -350,12 +366,8 @@
     across = to_across(other_set)
     swap = to_side(other_set)
     straight = to_straight(own_set)
-    pieces = [
-        field_got,
-        to_core(field_got),
-        send(field_got, lambda x, c, p, h: (1 - x, c, p, h)),
-        send(field_got, lambda x, c, p, h: (1 - x, 1 - c, p, h)),
-    ]
+    field_both = send(field_got, lambda x, c, p, h: (1 - x, 1 - c, p, h))
+    pieces = [field_got, to_core(field_got), to_core(field_both), field_both]
     field_swap = to_side(field_own)
     swap_more = to_core(field_swap)
 
@@ -374,11 +386,11 @@
     )
     right = send(low, lambda x, c, p, h: (x, c, p - 1, h))
     left = send(high, lambda x, c, p, h: (x, c, p + 1, h))
-    mine = keep * to_core(give)
-    mine = mine * to_side(mine)
-    junction = mine
-    for step in range(1, chips):
-        junction = junction * send(mine, lambda x, c, p, h, step=step: (x + step, c, p, h))
+    half = f32((block // 2, rows, columns))
+    upper, lower = call(product_kernel, (half, half), [], 0, keep, to_core(give))
+    upper = call(product_kernel, (half,), [], 0, upper, to_side(upper))[0]
+    lower = call(product_kernel, (half,), [], 0, lower, to_chip(lower))[0]
+    junction = call(join_kernel, f32(one), [], 0, upper, to_chip(upper), lower, to_side(lower))
     halo = send(junction, lambda x, c, p, h: (x, c, p + 2 * c - 1, h))
     held_junction, left, right = lax.optimization_barrier((junction, left, right))
     junction_other = to_core(held_junction)

time: 66.9 us -> 66.8 us (level)
  starting transfers between devices: 33.2 us -> 28.5 us
  waiting for transfers between devices: 20.8 us -> 25.5 us
    ppermute x22 -> x24, starting transfers between devices: 33.2 us -> 28.5 us  [send(): return lax.ppermute(value, AXES, perm)]
    ppermute x22 -> x24, waiting for transfers between devices: 20.8 us -> 25.5 us  [send(): return lax.ppermute(value, AXES, perm)]
    pallas_call x7 -> x11, Pallas kernels: 9.84 us -> 9.9 us  [call(): pl.pallas_call(kernel, out_shape=out_shape, in_specs=specs, out_specs=jax...]
  transfers between devices with their start and end apart: 22 -> 24, of which waited for: 11 -> 14; matrix products, arithmetic and copies ran while one was open for 0% -> 0% of each run, Pallas kernels for 0% -> 0%
where the time goes in v5:
time: 66.8 us; the launch traced here: 66.6 us
  starting transfers between devices  28.5 us (43%)
  waiting for transfers between devices  25.5 us (38%)
  Pallas kernels  9.9 us (15%)
  local copies, waits for them, and re-layouts  1.99 us (3%)
  between operations  0.76 us (1%)
    ppermute x24, starting transfers between devices, send(): return lax.ppermute(value, AXES, perm)  28.5 us
    ppermute x24, waiting for transfers between devices, send(): return lax.ppermute(value, AXES, perm)  25.5 us
    pallas_call x11, Pallas kernels, call(): pl.pallas_call(kernel, out_shape=out_shape, in_specs=specs, out_specs=jax...  9.9 us
    unnamed x8, local copies, waits for them, and re-layouts  1.99 us
  transfers between devices with their start and end apart: 24, of which 14 were waited for; matrix products, arithmetic and copies ran while one was open for 0% of the time, Pallas kernels for 0%

profile of v5, /device:TPU:0, one launch (start us, length us, event | category | flops | bytes accessed | tf_op | source)
XLA Modules:
  0.0 66.6 jit_solution(1658499234087828894)
XLA Ops:
  0.6 0.0 copy-start
  0.6 0.9 %copy-done = f32[2,4,64,128]{3,2,1,0:T(8,128)S(1)} copy-done((f32[2,4,64,128]{3,2,1,0:T(8,128)S(1)}, f32[2,4,64,128]{3,2,1,0:T(8,128)}, u32[]{:S(2)}) %copy-start) | copy-done | bytes 262168
  1.6 0.0 copy-start.2
  1.6 1.0 %copy-done.2 = f32[4,4,64,128]{3,2,1,0:T(8,128)S(1)} copy-done((f32[4,4,64,128]{3,2,1,0:T(8,128)S(1)}, f32[4,4,64,128]{3,2,1,0:T(8,128)}, u32[]{:S(2)}) %copy-start.2) | copy-done | bytes 524312
  2.7 5.1 %collective-permute-start.5 = (f32[4,64,128]{2,1,0:T(8,128)S(1)}, f32[4,64,128]{2,1,0:T(8,128)S(1)}, u32[]{:S(2)}, u32[]{:S(2)}) collective-permute-start(f32[4,64,128]{2,1,0:T(8,128)S(1)} %get-tuple-element.24), channel_id=1, source_target_pairs={{0,6},{1,3},{2,0},{3,5},{4,2},{5,7},{6,4},{7,1},{8,14},{9,11},{10,... | collective-permute-start | bytes 393224 | tf_op jit(solution)/shard_map/ppermute | solution.py:336
  7.8 1.2 %collective-permute-start = (f32[2,4,64,128]{3,2,1,0:T(8,128)S(1)}, f32[2,4,64,128]{3,2,1,0:T(8,128)S(1)}, u32[]{:S(2)}, u32[]{:S(2)}) collective-permute-start(f32[2,4,64,128]{3,2,1,0:T(8,128)S(1)} %get-tuple-element.22), channel_id=1, source_target_pairs={{0,7},{1,2},{2,1},{3,4},{4,3},{5,6},{6,5},{7,0},{8,15},{9,10},{10,... | collective-permute-start | bytes 786440 | tf_op jit(solution)/shard_map/ppermute | solution.py:336
  9.0 0.0 collective-permute-start.3
  9.0 2.7 %collective-permute-done.5.piece = f32[4,64,128]{2,1,0:T(8,128)S(1)} collective-permute-done((f32[4,64,128]{2,1,0:T(8,128)S(1)}, f32[4,64,128]{2,1,0:T(8,128)S(1)}, u32[]{:S(2)}, u32[]{:S(2)}) %collective-permute-start.5) | collective-permute-done | bytes 131104 | tf_op jit(solution)/shard_map/ppermute | solution.py:336
  11.7 0.7 %collective-permute-start.7 = (f32[4,64,128]{2,1,0:T(8,128)S(1)}, f32[4,64,128]{2,1,0:T(8,128)S(1)}, u32[]{:S(2)}, u32[]{:S(2)}) collective-permute-start(f32[4,64,128]{2,1,0:T(8,128)S(1)} %collective-permute-done.5.piece), channel_id=1, source_target_pairs={{0,24},{1,25},{2,26},{3,27},{4,28},{5,29},{6,30},{7,31},{8,16},{9,... | collective-permute-start | bytes 393224 | tf_op jit(solution)/shard_map/ppermute | solution.py:336
  12.4 0.0 copy-start.1
  12.4 0.0 copy-start.3
  12.4 3.6 %collective-permute-start.2 = (f32[2,4,64,128]{3,2,1,0:T(8,128)S(1)}, f32[2,4,64,128]{3,2,1,0:T(8,128)S(1)}, u32[]{:S(2)}, u32[]{:S(2)}) collective-permute-start(f32[2,4,64,128]{3,2,1,0:T(8,128)S(1)} %get-tuple-element.23), channel_id=1, source_target_pairs={{0,6},{1,3},{2,0},{3,5},{4,2},{5,7},{6,4},{7,1},{8,14},{9,11},{10,... | collective-permute-start | bytes 786440 | tf_op jit(solution)/shard_map/ppermute | solution.py:336
  16.0 0.0 collective-permute-start.1
  16.0 3.9 %collective-permute-done.3.f_swap = f32[4,64,128]{2,1,0:T(8,128)S(1)} collective-permute-done((f32[4,64,128]{2,1,0:T(8,128)S(1)}, f32[4,64,128]{2,1,0:T(8,128)S(1)}, u32[]{:S(2)}, u32[]{:S(2)}) %collective-permute-start.3) | collective-permute-done | bytes 131104 | tf_op jit(solution)/shard_map/ppermute | solution.py:336
  19.9 0.0 collective-permute-start.6
  19.9 0.0 collective-permute-done.7.piece_both
  19.9 0.5 collective-permute-start.4
  20.4 0.0 collective-permute-done.across
  20.4 0.1 collective-permute-start.8
  20.6 0.7 %collective-permute-done.6.piece_core = f32[4,64,128]{2,1,0:T(8,128)S(1)} collective-permute-done((f32[4,64,128]{2,1,0:T(8,128)S(1)}, f32[4,64,128]{2,1,0:T(8,128)S(1)}, u32[]{:S(2)}, u32[]{:S(2)}) %collective-permute-start.6) | collective-permute-done | bytes 131104 | tf_op jit(solution)/shard_map/ppermute | solution.py:336
  21.3 0.2 collective-permute-done.4.g_swap
  21.5 1.0 %collective-permute-done.2.straight = f32[2,4,64,128]{3,2,1,0:T(8,128)S(1)} collective-permute-done((f32[2,4,64,128]{3,2,1,0:T(8,128)S(1)}, f32[2,4,64,128]{3,2,1,0:T(8,128)S(1)}, u32[]{:S(2)}, u32[]{:S(2)}) %collective-permute-start.2) | collective-permute-done | bytes 262176 | tf_op jit(solution)/shard_map/ppermute | solution.py:336
  22.5 2.7 %collective-permute-done.1.swap = f32[2,4,64,128]{3,2,1,0:T(8,128)S(1)} collective-permute-done((f32[2,4,64,128]{3,2,1,0:T(8,128)S(1)}, f32[2,4,64,128]{3,2,1,0:T(8,128)S(1)}, u32[]{:S(2)}, u32[]{:S(2)}) %collective-permute-start.1) | collective-permute-done | bytes 262176 | tf_op jit(solution)/shard_map/ppermute | solution.py:336
  25.2 0.0 collective-permute-done.8.piece_chip
  25.2 0.0 copy-done.1
  25.2 0.0 copy-done.3
  25.2 4.4 %shard_map.52 = (f32[2,16,64,128]{3,2,1,0:T(8,128)S(1)}, f32[2,8,64,128]{3,2,1,0:T(8,128)S(1)}, f32[2,4,64,128]{3,2,1,0:T(8,128)S(1)}, f32[2,4,64,128]{3,2,1,0:T...) custom-call(s32[4]{0:T(128)S(1)} %copy-done.3, f32[4,4,64,128]{3,2,1,0:T(8,128)S(1)} %shard_map.51.window, ...), custom_call_target="tpu_custom_call" | custom-call | flops 8000000 | bytes 8000000 | tf_op jit(solution)/shard_map/pallas_call | solution.py:307
  29.6 0.1 collective-permute-start.9
  29.7 1.3 %collective-permute-done.9.other = f32[4,64,128]{2,1,0:T(8,128)S(1)} collective-permute-done((f32[4,64,128]{2,1,0:T(8,128)S(1)}, f32[4,64,128]{2,1,0:T(8,128)S(1)}, u32[]{:S(2)}, u32[]{:S(2)}) %collective-permute-start.9) | collective-permute-done | bytes 131104 | tf_op jit(solution)/shard_map/ppermute | solution.py:336
  31.0 0.1 collective-permute-start.10
  31.1 0.1 collective-permute-start.14
  31.2 3.7 %collective-permute-start.12 = (f32[2,64,128]{2,1,0:T(8,128)S(1)}, f32[2,64,128]{2,1,0:T(8,128)S(1)}, u32[]{:S(2)}, u32[]{:S(2)}) collective-permute-start(f32[2,64,128]{2,1,0:T(8,128)S(1)} %get-tuple-element.28.one), channel_id=1, source_target_pairs={{0,16},{1,17},{2,18},{3,19},{4,20},{5,21},{6,22},{7,23},{8,24},{9,... | collective-permute-start | bytes 196616 | tf_op jit(solution)/shard_map/ppermute | solution.py:336
  34.9 3.8 %collective-permute-start.15 = (f32[2,4,64,128]{3,2,1,0:T(8,128)S(1)}, f32[2,4,64,128]{3,2,1,0:T(8,128)S(1)}, u32[]{:S(2)}, u32[]{:S(2)}) collective-permute-start(f32[2,4,64,128]{3,2,1,0:T(8,128)S(1)} %get-tuple-element.30.two_low), channel_id=1, source_target_pairs={{0,6},{1,7},{2,0},{3,1},{4,2},{5,3},{6,4},{7,5},{8,14},{9,15},{10,... | collective-permute-start | bytes 786440 | tf_op jit(solution)/shard_map/ppermute | solution.py:336
  38.7 0.0 collective-permute-done.10.other
  38.7 0.1 collective-permute-start.11
  38.8 0.0 collective-permute-done.12.other
  38.8 0.9 %collective-permute-start.13 = (f32[2,64,128]{2,1,0:T(8,128)S(1)}, f32[2,64,128]{2,1,0:T(8,128)S(1)}, u32[]{:S(2)}, u32[]{:S(2)}) collective-permute-start(f32[2,64,128]{2,1,0:T(8,128)S(1)} %shard_map.55.lower), channel_id=1, source_target_pairs={{0,1},{1,0},{2,3},{3,2},{4,5},{5,4},{6,7},{7,6},{8,9},{9,8},{10,11... | collective-permute-start | bytes 196616 | tf_op jit(solution)/shard_map/ppermute | solution.py:336
  39.7 3.3 %collective-permute-done.11.upper_other = f32[2,64,128]{2,1,0:T(8,128)S(1)} collective-permute-done((f32[2,64,128]{2,1,0:T(8,128)S(1)}, f32[2,64,128]{2,1,0:T(8,128)S(1)}, u32[]{:S(2)}, u32[]{:S(2)}) %collective-permute-start.11) | collective-permute-done | bytes 65568 | tf_op jit(solution)/shard_map/ppermute | solution.py:336
  43.0 0.1 collective-permute-done.13.lower_other
  43.2 2.4 %collective-permute-start.17 = (f32[4,64,128]{2,1,0:T(8,128)S(1)}, f32[4,64,128]{2,1,0:T(8,128)S(1)}, u32[]{:S(2)}, u32[]{:S(2)}) collective-permute-start(f32[4,64,128]{2,1,0:T(8,128)S(1)} %shard_map.56.refs_0_.j_mine), channel_id=1, source_target_pairs={{0,6},{1,7},{2,0},{3,1},{4,2},{5,3},{6,4},{7,5},{8,10},{9,11},{10,... | collective-permute-start | bytes 393224 | tf_op jit(solution)/shard_map/ppermute | solution.py:336
  45.6 0.0 collective-permute-done.14.two_left
  45.6 2.1 %collective-permute-done.15.two_right = f32[2,4,64,128]{3,2,1,0:T(8,128)S(1)} collective-permute-done((f32[2,4,64,128]{3,2,1,0:T(8,128)S(1)}, f32[2,4,64,128]{3,2,1,0:T(8,128)S(1)}, u32[]{:S(2)}, u32[]{:S(2)}) %collective-permute-start.15) | collective-permute-done | bytes 262176 | tf_op jit(solution)/shard_map/ppermute | solution.py:336
  47.7 0.0 collective-permute-start.16
  47.7 2.0 %collective-permute-done.17.refs_2_.j_halo = f32[4,64,128]{2,1,0:T(8,128)S(1)} collective-permute-done((f32[4,64,128]{2,1,0:T(8,128)S(1)}, f32[4,64,128]{2,1,0:T(8,128)S(1)}, u32[]{:S(2)}, u32[]{:S(2)}) %collective-permute-start.17) | collective-permute-done | bytes 131104 | tf_op jit(solution)/shard_map/ppermute | solution.py:336
  49.7 0.0 collective-permute-start.18
  49.7 0.0 collective-permute-done.16.refs_1_.j_other
  49.7 1.3 %collective-permute-done.18.refs_3_.j_halo_other = f32[4,64,128]{2,1,0:T(8,128)S(1)} collective-permute-done((f32[4,64,128]{2,1,0:T(8,128)S(1)}, f32[4,64,128]{2,1,0:T(8,128)S(1)}, u32[]{:S(2)}, u32[]{:S(2)}) %collective-permute-start.18) | collective-permute-done | bytes 131104 | tf_op jit(solution)/shard_map/ppermute | solution.py:336
  51.1 4.5 %shard_map.58 = (f32[2,2,2,4,16,128]{5,4,3,2,1,0:T(8,128)S(1)}, f32[2,2,2,4,16,128]{5,4,3,2,1,0:T(8,128)S(1)}) custom-call(s32[4]{0:T(128)S(1)} %copy-done.3, f32[2,16,64,128]{3,2,1,0:T(8,128)S(1)} %get-tuple-element.32.u_ref, f32[2,8,64,128]{3,2,1,0:T(8,128)S(1)} %get-tuple-element.33.one_ref, f32[2,4,64,128]{3,2,1,0:T(8,128)S(1)} %collective-permute-done.14.two_left, ...), custom_call_target="tpu_custom_call" | custom-call | flops 8000000 | bytes 8000000 | tf_op jit(solution)/shard_map/pallas_call | solution.py:307
  55.6 0.2 collective-permute-start.20
  55.8 1.4 %collective-permute-done.20.received = f32[2,2,2,4,16,128]{5,4,3,2,1,0:T(8,128)S(1)} collective-permute-done((f32[2,2,2,4,16,128]{5,4,3,2,1,0:T(8,128)S(1)}, f32[2,2,2,4,16,128]{5,4,3,2,1,0:T(8,128)S(1)}, u32[]{:S(2)}, u32[]{:S(2)}) %collective-permute-start.20) | collective-permute-done | bytes 262176 | tf_op jit(solution)/shard_map/ppermute | solution.py:336
  57.2 1.7 %collective-permute-start.21 = (f32[2,4,16,128]{3,2,1,0:T(8,128)S(1)}, f32[2,4,16,128]{3,2,1,0:T(8,128)S(1)}, u32[]{:S(2)}, u32[]{:S(2)}) collective-permute-start(f32[2,4,16,128]{3,2,1,0:T(8,128)S(1)} %get-tuple-element.39), channel_id=1, source_target_pairs={{0,1},{1,0},{2,3},{3,2},{4,5},{5,4},{6,7},{7,6},{8,9},{9,8},{10,11... | collective-permute-start | bytes 196616 | tf_op jit(solution)/shard_map/ppermute | solution.py:336
  59.0 1.0 %collective-permute-start.22 = (f32[2,4,16,128]{3,2,1,0:T(8,128)S(1)}, f32[2,4,16,128]{3,2,1,0:T(8,128)S(1)}, u32[]{:S(2)}, u32[]{:S(2)}) collective-permute-start(f32[2,4,16,128]{3,2,1,0:T(8,128)S(1)} %get-tuple-element.40), channel_id=1, source_target_pairs={{0,16},{1,17},{2,18},{3,19},{4,20},{5,21},{6,22},{7,23},{8,24},{9,... | collective-permute-start | bytes 196616 | tf_op jit(solution)/shard_map/ppermute | solution.py:336
  60.0 1.2 %collective-permute-start.23 = (f32[2,4,16,128]{3,2,1,0:T(8,128)S(1)}, f32[2,4,16,128]{3,2,1,0:T(8,128)S(1)}, u32[]{:S(2)}, u32[]{:S(2)}) collective-permute-start(f32[2,4,16,128]{3,2,1,0:T(8,128)S(1)} %get-tuple-element.41), channel_id=1, source_target_pairs={{0,17},{1,16},{2,19},{3,18},{4,21},{5,20},{6,23},{7,22},{8,25},{9,... | collective-permute-start | bytes 196616 | tf_op jit(solution)/shard_map/ppermute | solution.py:336
  61.2 2.0 %collective-permute-start.19 = (f32[8,128]{1,0:T(8,128)S(1)}, f32[8,128]{1,0:T(8,128)S(1)}, u32[]{:S(2)}, u32[]{:S(2)}) collective-permute-start(f32[8,128]{1,0:T(8,128)S(1)} %shard_map.57), channel_id=1, source_target_pairs={{0,4},{1,5},{2,6},{3,7},{4,0},{5,1},{6,2},{7,3},{8,12},{9,13},{10,... | collective-permute-start | bytes 12296 | tf_op jit(solution)/shard_map/ppermute | solution.py:336
  63.2 2.6 %collective-permute-done.19 = f32[8,128]{1,0:T(8,128)S(1)} collective-permute-done((f32[8,128]{1,0:T(8,128)S(1)}, f32[8,128]{1,0:T(8,128)S(1)}, u32[]{:S(2)}, u32[]{:S(2)}) %collective-permute-start.19) | collective-permute-done | bytes 4128 | tf_op jit(solution)/shard_map/ppermute | solution.py:336
  65.8 0.0 collective-permute-done.21.refs_0_
  65.8 0.0 collective-permute-done.22.refs_1_
  65.8 0.0 collective-permute-done.23.refs_2_
  65.8 0.8 %shard_map.60 = (f32[2,4,16,128]{3,2,1,0:T(8,128)}, f32[2,4,16,128]{3,2,1,0:T(8,128)}) custom-call(f32[2,4,64,128]{3,2,1,0:T(8,128)S(1)} %copy-done.1, f32[8,128]{1,0:T(8,128)S(1)} %add.3.total, f32[2,4,16,128]{3,2,1,0:T(8,128)S(1)} %get-tuple-element.38.own, f32[2,4,16,128]{3,2,1,0:T(8,128)S(1)} %collective-permute-done.21.refs_0_, ...), custom_call_target="tpu_custom_call" | custom-call | flops 1000000 | bytes 1000000 | tf_op jit(solution)/shard_map/pallas_call | solution.py:307
  (9 shorter events, 0.2 us)
Async XLA Ops:
  0.6 1.0 %copy-start = (f32[2,4,64,128]{3,2,1,0:T(8,128)S(1)}, f32[2,4,64,128]{3,2,1,0:T(8,128)}, u32[]{:S(2)}) copy-start(f32[2,4,64,128]{3,2,1,0:T(8,128)} %fields.5) | copy-start | bytes 786436
  1.6 1.0 %copy-start.2 = (f32[4,4,64,128]{3,2,1,0:T(8,128)S(1)}, f32[4,4,64,128]{3,2,1,0:T(8,128)}, u32[]{:S(2)}) copy-start(f32[4,4,64,128]{3,2,1,0:T(8,128)} %starts.3) | copy-start | bytes 1572868
  2.7 9.0 %collective-permute-start.5 = (f32[4,64,128]{2,1,0:T(8,128)S(1)}, f32[4,64,128]{2,1,0:T(8,128)S(1)}, u32[]{:S(2)}, u32[]{:S(2)}) collective-permute-start(f32[4,64,128]{2,1,0:T(8,128)S(1)} %get-tuple-element.24), channel_id=1, source_target_pairs={{0,6},{1,3},{2,0},{3,5},{4,2},{5,7},{6,4},{7,1},{8,14},{9,11},{10,... | collective-permute-start | bytes 393224 | tf_op jit(solution)/shard_map/ppermute | solution.py:336
  7.8 12.7 %collective-permute-start = (f32[2,4,64,128]{3,2,1,0:T(8,128)S(1)}, f32[2,4,64,128]{3,2,1,0:T(8,128)S(1)}, u32[]{:S(2)}, u32[]{:S(2)}) collective-permute-start(f32[2,4,64,128]{3,2,1,0:T(8,128)S(1)} %get-tuple-element.22), channel_id=1, source_target_pairs={{0,7},{1,2},{2,1},{3,4},{4,3},{5,6},{6,5},{7,0},{8,15},{9,10},{10,... | collective-permute-start | bytes 786440 | tf_op jit(solution)/shard_map/ppermute | solution.py:336
  9.0 11.0 %collective-permute-start.3 = (f32[4,64,128]{2,1,0:T(8,128)S(1)}, f32[4,64,128]{2,1,0:T(8,128)S(1)}, u32[]{:S(2)}, u32[]{:S(2)}) collective-permute-start(f32[4,64,128]{2,1,0:T(8,128)S(1)} %get-tuple-element.24), channel_id=1, source_target_pairs={{0,1},{1,0},{2,3},{3,2},{4,5},{5,4},{6,7},{7,6},{8,9},{9,8},{10,11... | collective-permute-start | bytes 393224 | tf_op jit(solution)/shard_map/ppermute | solution.py:336
  11.7 8.3 %collective-permute-start.7 = (f32[4,64,128]{2,1,0:T(8,128)S(1)}, f32[4,64,128]{2,1,0:T(8,128)S(1)}, u32[]{:S(2)}, u32[]{:S(2)}) collective-permute-start(f32[4,64,128]{2,1,0:T(8,128)S(1)} %collective-permute-done.5.piece), channel_id=1, source_target_pairs={{0,24},{1,25},{2,26},{3,27},{4,28},{5,29},{6,30},{7,31},{8,16},{9,... | collective-permute-start | bytes 393224 | tf_op jit(solution)/shard_map/ppermute | solution.py:336
  12.4 12.7 %copy-start.1 = (f32[2,4,64,128]{3,2,1,0:T(8,128)S(1)}, f32[2,4,64,128]{3,2,1,0:T(8,128)}, u32[]{:S(2)}) copy-start(f32[2,4,64,128]{3,2,1,0:T(8,128)} %fields.5) | copy-start | bytes 786436
  12.4 12.7 %copy-start.3 = (s32[4]{0:T(128)S(1)}, s32[4]{0:T(128)}, u32[]{:S(2)}) copy-start(s32[4]{0:T(128)} %labels.3) | copy-start | bytes 52
  12.4 10.1 %collective-permute-start.2 = (f32[2,4,64,128]{3,2,1,0:T(8,128)S(1)}, f32[2,4,64,128]{3,2,1,0:T(8,128)S(1)}, u32[]{:S(2)}, u32[]{:S(2)}) collective-permute-start(f32[2,4,64,128]{3,2,1,0:T(8,128)S(1)} %get-tuple-element.23), channel_id=1, source_target_pairs={{0,6},{1,3},{2,0},{3,5},{4,2},{5,7},{6,4},{7,1},{8,14},{9,11},{10,... | collective-permute-start | bytes 786440 | tf_op jit(solution)/shard_map/ppermute | solution.py:336
  16.0 9.1 %collective-permute-start.1 = (f32[2,4,64,128]{3,2,1,0:T(8,128)S(1)}, f32[2,4,64,128]{3,2,1,0:T(8,128)S(1)}, u32[]{:S(2)}, u32[]{:S(2)}) collective-permute-start(f32[2,4,64,128]{3,2,1,0:T(8,128)S(1)} %get-tuple-element.22), channel_id=1, source_target_pairs={{0,1},{1,0},{2,3},{3,2},{4,5},{5,4},{6,7},{7,6},{8,9},{9,8},{10,11... | collective-permute-start | bytes 786440 | tf_op jit(solution)/shard_map/ppermute | solution.py:336
  19.9 1.3 %collective-permute-start.6 = (f32[4,64,128]{2,1,0:T(8,128)S(1)}, f32[4,64,128]{2,1,0:T(8,128)S(1)}, u32[]{:S(2)}, u32[]{:S(2)}) collective-permute-start(f32[4,64,128]{2,1,0:T(8,128)S(1)} %collective-permute-done.5.piece), channel_id=1, source_target_pairs={{0,8},{1,9},{2,10},{3,11},{4,12},{5,13},{6,14},{7,15},{8,0},{9,1},... | collective-permute-start | bytes 393224 | tf_op jit(solution)/shard_map/ppermute | solution.py:336
  19.9 1.5 %collective-permute-start.4 = (f32[4,64,128]{2,1,0:T(8,128)S(1)}, f32[4,64,128]{2,1,0:T(8,128)S(1)}, u32[]{:S(2)}, u32[]{:S(2)}) collective-permute-start(f32[4,64,128]{2,1,0:T(8,128)S(1)} %collective-permute-done.3.f_swap), channel_id=1, source_target_pairs={{0,8},{1,9},{2,10},{3,11},{4,12},{5,13},{6,14},{7,15},{8,0},{9,1},... | collective-permute-start | bytes 393224 | tf_op jit(solution)/shard_map/ppermute | solution.py:336
  20.4 4.7 %collective-permute-start.8 = (f32[4,64,128]{2,1,0:T(8,128)S(1)}, f32[4,64,128]{2,1,0:T(8,128)S(1)}, u32[]{:S(2)}, u32[]{:S(2)}) collective-permute-start(f32[4,64,128]{2,1,0:T(8,128)S(1)} %collective-permute-done.7.piece_both), channel_id=1, source_target_pairs={{0,8},{1,9},{2,10},{3,11},{4,12},{5,13},{6,14},{7,15},{8,0},{9,1},... | collective-permute-start | bytes 393224 | tf_op jit(solution)/shard_map/ppermute | solution.py:336
  29.6 1.4 %collective-permute-start.9 = (f32[4,64,128]{2,1,0:T(8,128)S(1)}, f32[4,64,128]{2,1,0:T(8,128)S(1)}, u32[]{:S(2)}, u32[]{:S(2)}) collective-permute-start(f32[4,64,128]{2,1,0:T(8,128)S(1)} %get-tuple-element.26), channel_id=1, source_target_pairs={{0,8},{1,9},{2,10},{3,11},{4,12},{5,13},{6,14},{7,15},{8,0},{9,1},... | collective-permute-start | bytes 393224 | tf_op jit(solution)/shard_map/ppermute | solution.py:336
  31.0 7.7 %collective-permute-start.10 = (f32[2,64,128]{2,1,0:T(8,128)S(1)}, f32[2,64,128]{2,1,0:T(8,128)S(1)}, u32[]{:S(2)}, u32[]{:S(2)}) collective-permute-start(f32[2,64,128]{2,1,0:T(8,128)S(1)} %get-tuple-element.27.one), channel_id=1, source_target_pairs={{0,1},{1,0},{2,3},{3,2},{4,5},{5,4},{6,7},{7,6},{8,9},{9,8},{10,11... | collective-permute-start | bytes 196616 | tf_op jit(solution)/shard_map/ppermute | solution.py:336
  31.1 14.5 %collective-permute-start.14 = (f32[2,4,64,128]{3,2,1,0:T(8,128)S(1)}, f32[2,4,64,128]{3,2,1,0:T(8,128)S(1)}, u32[]{:S(2)}, u32[]{:S(2)}) collective-permute-start(f32[2,4,64,128]{3,2,1,0:T(8,128)S(1)} %get-tuple-element.29.two_high), channel_id=1, source_target_pairs={{0,2},{1,3},{2,4},{3,5},{4,6},{5,7},{6,0},{7,1},{8,10},{9,11},{10,... | collective-permute-start | bytes 786440 | tf_op jit(solution)/shard_map/ppermute | solution.py:336
  31.2 7.6 %collective-permute-start.12 = (f32[2,64,128]{2,1,0:T(8,128)S(1)}, f32[2,64,128]{2,1,0:T(8,128)S(1)}, u32[]{:S(2)}, u32[]{:S(2)}) collective-permute-start(f32[2,64,128]{2,1,0:T(8,128)S(1)} %get-tuple-element.28.one), channel_id=1, source_target_pairs={{0,16},{1,17},{2,18},{3,19},{4,20},{5,21},{6,22},{7,23},{8,24},{9,... | collective-permute-start | bytes 196616 | tf_op jit(solution)/shard_map/ppermute | solution.py:336
  34.9 12.8 %collective-permute-start.15 = (f32[2,4,64,128]{3,2,1,0:T(8,128)S(1)}, f32[2,4,64,128]{3,2,1,0:T(8,128)S(1)}, u32[]{:S(2)}, u32[]{:S(2)}) collective-permute-start(f32[2,4,64,128]{3,2,1,0:T(8,128)S(1)} %get-tuple-element.30.two_low), channel_id=1, source_target_pairs={{0,6},{1,7},{2,0},{3,1},{4,2},{5,3},{6,4},{7,5},{8,14},{9,15},{10,... | collective-permute-start | bytes 786440 | tf_op jit(solution)/shard_map/ppermute | solution.py:336
  38.7 4.3 %collective-permute-start.11 = (f32[2,64,128]{2,1,0:T(8,128)S(1)}, f32[2,64,128]{2,1,0:T(8,128)S(1)}, u32[]{:S(2)}, u32[]{:S(2)}) collective-permute-start(f32[2,64,128]{2,1,0:T(8,128)S(1)} %shard_map.54.upper), channel_id=1, source_target_pairs={{0,16},{1,17},{2,18},{3,19},{4,20},{5,21},{6,22},{7,23},{8,24},{9,... | collective-permute-start | bytes 196616 | tf_op jit(solution)/shard_map/ppermute | solution.py:336
  38.8 4.3 %collective-permute-start.13 = (f32[2,64,128]{2,1,0:T(8,128)S(1)}, f32[2,64,128]{2,1,0:T(8,128)S(1)}, u32[]{:S(2)}, u32[]{:S(2)}) collective-permute-start(f32[2,64,128]{2,1,0:T(8,128)S(1)} %shard_map.55.lower), channel_id=1, source_target_pairs={{0,1},{1,0},{2,3},{3,2},{4,5},{5,4},{6,7},{7,6},{8,9},{9,8},{10,11... | collective-permute-start | bytes 196616 | tf_op jit(solution)/shard_map/ppermute | solution.py:336
  43.2 6.6 %collective-permute-start.17 = (f32[4,64,128]{2,1,0:T(8,128)S(1)}, f32[4,64,128]{2,1,0:T(8,128)S(1)}, u32[]{:S(2)}, u32[]{:S(2)}) collective-permute-start(f32[4,64,128]{2,1,0:T(8,128)S(1)} %shard_map.56.refs_0_.j_mine), channel_id=1, source_target_pairs={{0,6},{1,7},{2,0},{3,1},{4,2},{5,3},{6,4},{7,5},{8,10},{9,11},{10,... | collective-permute-start | bytes 393224 | tf_op jit(solution)/shard_map/ppermute | solution.py:336
  47.7 2.0 %collective-permute-start.16 = (f32[4,64,128]{2,1,0:T(8,128)S(1)}, f32[4,64,128]{2,1,0:T(8,128)S(1)}, u32[]{:S(2)}, u32[]{:S(2)}) collective-permute-start(f32[4,64,128]{2,1,0:T(8,128)S(1)} %shard_map.56.refs_0_.j_mine), channel_id=1, source_target_pairs={{0,8},{1,9},{2,10},{3,11},{4,12},{5,13},{6,14},{7,15},{8,0},{9,1},... | collective-permute-start | bytes 393224 | tf_op jit(solution)/shard_map/ppermute | solution.py:336
  49.7 1.3 %collective-permute-start.18 = (f32[4,64,128]{2,1,0:T(8,128)S(1)}, f32[4,64,128]{2,1,0:T(8,128)S(1)}, u32[]{:S(2)}, u32[]{:S(2)}) collective-permute-start(f32[4,64,128]{2,1,0:T(8,128)S(1)} %collective-permute-done.17.refs_2_.j_halo), channel_id=1, source_target_pairs={{0,8},{1,9},{2,10},{3,11},{4,12},{5,13},{6,14},{7,15},{8,0},{9,1},... | collective-permute-start | bytes 393224 | tf_op jit(solution)/shard_map/ppermute | solution.py:336
  55.6 1.6 %collective-permute-start.20 = (f32[2,2,2,4,16,128]{5,4,3,2,1,0:T(8,128)S(1)}, f32[2,2,2,4,16,128]{5,4,3,2,1,0:T(8,128)S(1)}, u32[]{:S(2)}, u32[]{:S(2)}) collective-permute-start(f32[2,2,2,4,16,128]{5,4,3,2,1,0:T(8,128)S(1)} %get-tuple-element.37), channel_id=1, source_target_pairs={{0,8},{1,9},{2,10},{3,11},{4,12},{5,13},{6,14},{7,15},{8,0},{9,1},... | collective-permute-start | bytes 786440 | tf_op jit(solution)/shard_map/ppermute | solution.py:336
  57.2 8.6 %collective-permute-start.21 = (f32[2,4,16,128]{3,2,1,0:T(8,128)S(1)}, f32[2,4,16,128]{3,2,1,0:T(8,128)S(1)}, u32[]{:S(2)}, u32[]{:S(2)}) collective-permute-start(f32[2,4,16,128]{3,2,1,0:T(8,128)S(1)} %get-tuple-element.39), channel_id=1, source_target_pairs={{0,1},{1,0},{2,3},{3,2},{4,5},{5,4},{6,7},{7,6},{8,9},{9,8},{10,11... | collective-permute-start | bytes 196616 | tf_op jit(solution)/shard_map/ppermute | solution.py:336
  59.0 6.8 %collective-permute-start.22 = (f32[2,4,16,128]{3,2,1,0:T(8,128)S(1)}, f32[2,4,16,128]{3,2,1,0:T(8,128)S(1)}, u32[]{:S(2)}, u32[]{:S(2)}) collective-permute-start(f32[2,4,16,128]{3,2,1,0:T(8,128)S(1)} %get-tuple-element.40), channel_id=1, source_target_pairs={{0,16},{1,17},{2,18},{3,19},{4,20},{5,21},{6,22},{7,23},{8,24},{9,... | collective-permute-start | bytes 196616 | tf_op jit(solution)/shard_map/ppermute | solution.py:336
  60.0 5.8 %collective-permute-start.23 = (f32[2,4,16,128]{3,2,1,0:T(8,128)S(1)}, f32[2,4,16,128]{3,2,1,0:T(8,128)S(1)}, u32[]{:S(2)}, u32[]{:S(2)}) collective-permute-start(f32[2,4,16,128]{3,2,1,0:T(8,128)S(1)} %get-tuple-element.41), channel_id=1, source_target_pairs={{0,17},{1,16},{2,19},{3,18},{4,21},{5,20},{6,23},{7,22},{8,25},{9,... | collective-permute-start | bytes 196616 | tf_op jit(solution)/shard_map/ppermute | solution.py:336
  61.2 4.6 %collective-permute-start.19 = (f32[8,128]{1,0:T(8,128)S(1)}, f32[8,128]{1,0:T(8,128)S(1)}, u32[]{:S(2)}, u32[]{:S(2)}) collective-permute-start(f32[8,128]{1,0:T(8,128)S(1)} %shard_map.57), channel_id=1, source_target_pairs={{0,4},{1,5},{2,6},{3,7},{4,0},{5,1},{6,2},{7,3},{8,12},{9,13},{10,... | collective-permute-start | bytes 12296 | tf_op jit(solution)/shard_map/ppermute | solution.py:336

commit v6 on v5

--- a/solution.py
+++ b/solution.py
@@ -16,10 +16,8 @@
 AXES = ("arm", "space")
 
 
-def beside(plane):
-    rows, columns = plane.shape
-    total = pltpu.roll(plane, 1, 0) + pltpu.roll(plane, rows - 1, 0)
-    return total + (pltpu.roll(plane, 1, 1) + pltpu.roll(plane, columns - 1, 1))
+def shifts(plane, axis):
+    return pltpu.roll(plane, 1, axis), pltpu.roll(plane, plane.shape[axis] - 1, axis)
 
 
 def wavefront(stages):
@@ -35,7 +33,7 @@
         lax.fori_loop(begin, end, body, None)
 
 
-def two_steps(block, arms, factor, values, middle, store, scratch):
+def two_steps(block, arms, factor, factor_shifts, values, middle, store, scratch):
     half = coupling_full / 2
     centre_half, centre_full = 1.0 - 6.0 * half, 1.0 - 6.0 * coupling_full
 
@@ -45,23 +43,28 @@
         p_ref[j, i] = p
         t_ref[j, i] = u * p
 
-    def inner(i, p_ref, s_ref):
+    def inner(i, p_ref, s_ref, z_ref):
         for j in range(arms):
             u = factor(j, i)
             p = p_ref[j, i]
-            around = beside(p) + (p_ref[j, i - 1] + p_ref[j, i + 1])
+            (up, down), (left, right) = shifts(p, 0), shifts(p, 1)
+            u_left, u_right = factor_shifts(j, i)
+            z_ref[j, i] = u_left * left + u_right * right
+            around = (up + down) + (left + right) + (p_ref[j, i - 1] + p_ref[j, i + 1])
             s_ref[j, i] = (u * u) * (centre_half * p + half * around)
 
-    def outer(j, i, t_ref, s_ref):
+    def outer(j, i, t_ref, s_ref, z_ref):
         u = factor(j, i)
         s, t = s_ref[j, i], t_ref[j, i]
-        s_around = beside(s) + (s_ref[j, i - 1] + s_ref[j, i + 1])
-        t_around = beside(t) + (t_ref[j, i - 1] + t_ref[j, i + 1])
+        (up, down), (left, right) = shifts(s, 0), shifts(s, 1)
+        s_around = (up + down) + (left + right) + (s_ref[j, i - 1] + s_ref[j, i + 1])
+        up, down = shifts(t, 0)
+        t_around = (up + down) + z_ref[j, i] + (t_ref[j, i - 1] + t_ref[j, i + 1])
         halves = (4.0 / 3.0 * centre_half) * s + (4.0 / 3.0 * half) * s_around
         whole = (centre_full / 3.0) * t + (coupling_full / 3.0) * t_around
         return u * (halves - u * whole)
 
-    p_one, t_one, s_one, p_two, t_two, s_two = scratch
+    p_one, t_one, s_one, z_one, p_two, t_two, s_two, z_two = scratch
 
     def start(i):
         for j in range(arms):
@@ -69,21 +72,21 @@
 
     def between(i):
         for j in range(arms):
-            value = outer(j, i, t_one, s_one)
+            value = outer(j, i, t_one, s_one, z_one)
             middle(j, i, value)
             enter(j, i, value, p_two, t_two)
 
     def finish(i):
         for j in range(arms):
-            store(j, i, outer(j, i, t_two, s_two))
+            store(j, i, outer(j, i, t_two, s_two, z_two))
 
     first, last = block - 2 * reach, 3 * block + 2 * reach
     wavefront(
         [
             (first, last, start),
-            (first + 1, last - 1, lambda i: inner(i, p_one, s_one)),
+            (first + 1, last - 1, lambda i: inner(i, p_one, s_one, z_one)),
             (first + 2, last - 2, between),
-            (first + 3, last - 3, lambda i: inner(i, p_two, s_two)),
+            (first + 3, last - 3, lambda i: inner(i, p_two, s_two, z_two)),
             (first + 4, last - 4, finish),
         ]
     )
@@ -103,7 +106,7 @@
     return block + side * block, 2 * block - side * block, 3 * block * (1 - side), 3 * block * side
 
 
-def window_kernel(starts, across, out_ref):
+def window_kernel(labels, starts, across, out_ref):
     arms = across.shape[0]
     side = lax.rem(lax.axis_index("space"), 2)
     for j in range(arms):
@@ -111,14 +114,10 @@
         out_ref[arms + j] = across[j]
 
 
-def forward_kernel(
-    labels, window, swap, straight, fields, f_swap, g_swap, piece, piece_core, piece_chip, piece_both,
-    u_ref, one_ref, low_ref, high_ref, keep_ref, send_ref,
-    q_ref, product_ref, *scratch,
+def gain_kernel(
+    fields, f_swap, g_swap, piece, piece_core, piece_chip, piece_both, u_ref, u_left_ref, u_right_ref
 ):
     block = fields.shape[1]
-    arms = swap.shape[0]
-    side = lax.rem(lax.axis_index("space"), 2)
     core = lax.rem(lax.axis_index("arm"), 2)
     own_at, swap_at, straight_at, across_at = places(block)
     chip = lax.div(lax.axis_index("arm"), 2)
@@ -131,12 +130,34 @@
     def fill(i, _):
         for kind in range(2):
             u_ref[kind, own_at + i] = gain(fields[kind, i])
-        u_ref[core, here_at + i] = gain(piece[i])
-        u_ref[1 - core, here_at + i] = gain(piece_core[i])
-        u_ref[core, there_at + i] = gain(piece_chip[i])
-        u_ref[1 - core, there_at + i] = gain(piece_both[i])
-        u_ref[core, swap_at + i] = gain(f_swap[i])
-        u_ref[1 - core, swap_at + i] = gain(g_swap[i])
+        for at, mine, other in (
+            (swap_at, f_swap, g_swap),
+            (here_at, piece, piece_core),
+            (there_at, piece_chip, piece_both),
+        ):
+            u_ref[core, at + i] = gain(mine[i])
+            u_ref[1 - core, at + i] = gain(other[i])
+
+    lax.fori_loop(0, block, fill, None)
+
+    def shift(i, _):
+        for kind in range(2):
+            u_left_ref[kind, i], u_right_ref[kind, i] = shifts(u_ref[kind, i], 1)
+
+    lax.fori_loop(0, 4 * block, shift, None, unroll=2)
+
+
+def forward_kernel(
+    labels, window, swap, straight, u_ref, u_left_ref, u_right_ref,
+    one_ref, low_ref, high_ref, keep_ref, send_ref,
+    q_ref, product_ref, *scratch,
+):
+    arms, block = swap.shape[0], swap.shape[1]
+    side = lax.rem(lax.axis_index("space"), 2)
+    core = lax.rem(lax.axis_index("arm"), 2)
+    own_at, swap_at, straight_at, across_at = places(block)
+
+    def fill(i, _):
         for j in range(arms):
             q_ref[j, own_at + i] = window[j, i]
             q_ref[j, across_at + i] = window[arms + j, i]
@@ -149,6 +170,9 @@
     def factor(j, i):
         return u_ref[kinds[j], i]
 
+    def factor_shifts(j, i):
+        return u_left_ref[kinds[j], i], u_right_ref[kinds[j], i]
+
     def values(j, i):
         return q_ref[j, i]
 
@@ -159,7 +183,7 @@
         middle_ref[j, i] = value
 
     *scratch, middle_ref = scratch
-    two_steps(block, arms, factor, values, middle, store, scratch)
+    two_steps(block, arms, factor, factor_shifts, values, middle, store, scratch)
     for j in range(arms):
         one_ref[j] = middle_ref[j, block : 3 * block]
 
@@ -178,7 +202,7 @@
 
 
 def backward_kernel(
-    labels, u_ref, one_ref, two_left, two_low, two_high, two_right,
+    labels, u_ref, u_left_ref, u_right_ref, one_ref, two_left, two_low, two_high, two_right,
     j_mine, j_other, j_halo, j_halo_other,
     keep_ref, send_ref,
     junction_ref, q_ref, density_ref, middle_ref, *scratch,
@@ -203,6 +227,9 @@
     def factor(j, i):
         return u_ref[kinds[j], i]
 
+    def factor_shifts(j, i):
+        return u_left_ref[kinds[j], i], u_right_ref[kinds[j], i]
+
     def values(j, i):
         return q_ref[j, i]
 
@@ -212,7 +239,7 @@
     def middle(j, i, value):
         middle_ref[j, i] = value
 
-    two_steps(block, arms, factor, values, middle, store, scratch)
+    two_steps(block, arms, factor, factor_shifts, values, middle, store, scratch)
 
     is_a = [(kind == 0).astype(jnp.float32) for kind in kinds]
 
@@ -375,13 +402,15 @@
     whole = (arms, 2 * block, rows, columns)
     part = (arms, block, rows, columns)
     one = (block, rows, columns)
-    window = call(window_kernel, f32((2 * arms, block, rows, columns)), [], 0, starts, across)
-    factor, step_one, low, high, keep, give = call(
+    window = call(window_kernel, f32((2 * arms, block, rows, columns)), [], 1, labels, starts, across)
+    gains = f32((2, 4 * block, rows, columns))
+    factors = call(gain_kernel, (gains,) * 3, [], 0, fields, field_swap, swap_more, *pieces)
+    step_one, low, high, keep, give = call(
         forward_kernel,
-        (f32((2, 4 * block, rows, columns)), f32(whole), f32(part), f32(part), f32(one), f32(one)),
-        [wide, vmem((2,) + one)] + [wide] * 7,
+        (f32(whole), f32(part), f32(part), f32(one), f32(one)),
+        [wide, vmem((2,) + one)] + [wide] * 9,
         1,
-        labels, window, swap, straight, fields, field_swap, swap_more, *pieces,
+        labels, window, swap, straight, *factors,
         cost=8_000_000,
     )
     right = send(low, lambda x, c, p, h: (x, c, p - 1, h))
@@ -408,9 +437,9 @@
     keep, give = call(
         backward_kernel,
         (f32(parts), f32(parts)),
-        [vmem((4 * block, rows, columns)), wide, vmem((2,) + whole[1:])] + [wide] * 7,
+        [vmem((4 * block, rows, columns)), wide, vmem((2,) + whole[1:])] + [wide] * 9,
         1,
-        labels, factor, step_one, left, low, high, right, junction, junction_other, halo, halo_other,
+        labels, *factors, step_one, left, low, high, right, junction, junction_other, halo, halo_other,
         cost=8_000_000,
     )
     to_places = other_chips(chips)

time: 66.8 us -> 65.8 us (0.985)
  waiting for transfers between devices: 25.5 us -> 23.7 us
  Pallas kernels: 9.9 us -> 10.7 us
    ppermute x24, waiting for transfers between devices: 25.5 us -> 23.7 us  [send(): return lax.ppermute(value, AXES, perm)]
    pallas_call x11 -> x12, Pallas kernels: 9.9 us -> 10.7 us  [call(): pl.pallas_call(kernel, out_shape=out_shape, in_specs=specs, out_specs=jax...]
  transfers between devices with their start and end apart: 24 -> 24, of which waited for: 14 -> 14; matrix products, arithmetic and copies ran while one was open for 0% -> 0% of each run, Pallas kernels for 0% -> 3%
where the time goes in v6:
time: 65.8 us; the launch traced here: 65.6 us
  starting transfers between devices  28.4 us (43%)
  waiting for transfers between devices  23.7 us (36%)
  Pallas kernels  10.7 us (16%)
  local copies, waits for them, and re-layouts  1.99 us (3%)
  between operations  0.78 us (1%)
    ppermute x24, starting transfers between devices, send(): return lax.ppermute(value, AXES, perm)  28.4 us
    ppermute x24, waiting for transfers between devices, send(): return lax.ppermute(value, AXES, perm)  23.7 us
    pallas_call x12, Pallas kernels, call(): pl.pallas_call(kernel, out_shape=out_shape, in_specs=specs, out_specs=jax...  10.7 us
    unnamed x8, local copies, waits for them, and re-layouts  1.99 us
  transfers between devices with their start and end apart: 24, of which 14 were waited for; matrix products, arithmetic and copies ran while one was open for 0% of the time, Pallas kernels for 3%

profile of v6, /device:TPU:0, one launch (start us, length us, event | category | flops | bytes accessed | tf_op | source)
XLA Modules:
  0.0 65.6 jit_solution(17608345087256608884)
XLA Ops:
  0.6 0.0 copy-start
  0.6 0.9 %copy-done = f32[2,4,64,128]{3,2,1,0:T(8,128)S(1)} copy-done((f32[2,4,64,128]{3,2,1,0:T(8,128)S(1)}, f32[2,4,64,128]{3,2,1,0:T(8,128)}, u32[]{:S(2)}) %copy-start) | copy-done | bytes 262168
  1.6 0.0 copy-start.2
  1.6 1.0 %copy-done.2 = f32[4,4,64,128]{3,2,1,0:T(8,128)S(1)} copy-done((f32[4,4,64,128]{3,2,1,0:T(8,128)S(1)}, f32[4,4,64,128]{3,2,1,0:T(8,128)}, u32[]{:S(2)}) %copy-start.2) | copy-done | bytes 524312
  2.7 5.1 %collective-permute-start.5 = (f32[4,64,128]{2,1,0:T(8,128)S(1)}, f32[4,64,128]{2,1,0:T(8,128)S(1)}, u32[]{:S(2)}, u32[]{:S(2)}) collective-permute-start(f32[4,64,128]{2,1,0:T(8,128)S(1)} %get-tuple-element.26), channel_id=1, source_target_pairs={{0,6},{1,3},{2,0},{3,5},{4,2},{5,7},{6,4},{7,1},{8,14},{9,11},{10,... | collective-permute-start | bytes 393224 | tf_op jit(solution)/shard_map/ppermute | solution.py:363
  7.8 0.0 copy-start.3
  7.8 1.2 %collective-permute-start = (f32[2,4,64,128]{3,2,1,0:T(8,128)S(1)}, f32[2,4,64,128]{3,2,1,0:T(8,128)S(1)}, u32[]{:S(2)}, u32[]{:S(2)}) collective-permute-start(f32[2,4,64,128]{3,2,1,0:T(8,128)S(1)} %get-tuple-element.24), channel_id=1, source_target_pairs={{0,7},{1,2},{2,1},{3,4},{4,3},{5,6},{6,5},{7,0},{8,15},{9,10},{10,... | collective-permute-start | bytes 786440 | tf_op jit(solution)/shard_map/ppermute | solution.py:363
  9.0 0.0 collective-permute-start.3
  9.0 2.7 %collective-permute-done.5.piece = f32[4,64,128]{2,1,0:T(8,128)S(1)} collective-permute-done((f32[4,64,128]{2,1,0:T(8,128)S(1)}, f32[4,64,128]{2,1,0:T(8,128)S(1)}, u32[]{:S(2)}, u32[]{:S(2)}) %collective-permute-start.5) | collective-permute-done | bytes 131104 | tf_op jit(solution)/shard_map/ppermute | solution.py:363
  11.7 0.7 %collective-permute-start.7 = (f32[4,64,128]{2,1,0:T(8,128)S(1)}, f32[4,64,128]{2,1,0:T(8,128)S(1)}, u32[]{:S(2)}, u32[]{:S(2)}) collective-permute-start(f32[4,64,128]{2,1,0:T(8,128)S(1)} %collective-permute-done.5.piece), channel_id=1, source_target_pairs={{0,24},{1,25},{2,26},{3,27},{4,28},{5,29},{6,30},{7,31},{8,16},{9,... | collective-permute-start | bytes 393224 | tf_op jit(solution)/shard_map/ppermute | solution.py:363
  12.4 0.0 copy-start.1
  12.4 3.5 %collective-permute-start.2 = (f32[2,4,64,128]{3,2,1,0:T(8,128)S(1)}, f32[2,4,64,128]{3,2,1,0:T(8,128)S(1)}, u32[]{:S(2)}, u32[]{:S(2)}) collective-permute-start(f32[2,4,64,128]{3,2,1,0:T(8,128)S(1)} %get-tuple-element.25), channel_id=1, source_target_pairs={{0,6},{1,3},{2,0},{3,5},{4,2},{5,7},{6,4},{7,1},{8,14},{9,11},{10,... | collective-permute-start | bytes 786440 | tf_op jit(solution)/shard_map/ppermute | solution.py:363
  16.0 0.0 collective-permute-start.1
  16.0 4.0 %collective-permute-done.3.f_swap = f32[4,64,128]{2,1,0:T(8,128)S(1)} collective-permute-done((f32[4,64,128]{2,1,0:T(8,128)S(1)}, f32[4,64,128]{2,1,0:T(8,128)S(1)}, u32[]{:S(2)}, u32[]{:S(2)}) %collective-permute-start.3) | collective-permute-done | bytes 131104 | tf_op jit(solution)/shard_map/ppermute | solution.py:363
  19.9 0.0 collective-permute-start.6
  19.9 0.0 collective-permute-done.7.piece_both
  19.9 0.5 collective-permute-start.4
  20.4 0.0 collective-permute-done.across
  20.5 0.1 collective-permute-start.8
  20.5 0.0 copy-done.3
  20.5 0.6 shard_map.51.window
  21.1 0.2 collective-permute-done.6.piece_core
  21.3 0.2 collective-permute-done.4.g_swap
  21.5 0.3 collective-permute-done.8.piece_chip
  21.8 0.0 copy-done.1
  21.8 1.3 %shard_map.52 = (f32[2,16,64,128]{3,2,1,0:T(8,128)S(1)}, f32[2,16,64,128]{3,2,1,0:T(8,128)S(1)}, f32[2,16,64,128]{3,2,1,0:T(8,128)S(1)}) custom-call(f32[2,4,64,128]{3,2,1,0:T(8,128)S(1)} %copy-done.1, f32[4,64,128]{2,1,0:T(8,128)S(1)} %collective-permute-done.3.f_swap, f32[4,64,128]{2,1,0:T(8,128)S(1)} %collective-permute-done.4.g_swap, ...), custom_call_target="tpu_custom_call" | custom-call | flops 1000000 | bytes 1000000 | tf_op jit(solution)/shard_map/pallas_call | solution.py:334
  23.1 0.0 collective-permute-done.2.straight
  23.1 2.1 %collective-permute-done.1.swap = f32[2,4,64,128]{3,2,1,0:T(8,128)S(1)} collective-permute-done((f32[2,4,64,128]{3,2,1,0:T(8,128)S(1)}, f32[2,4,64,128]{3,2,1,0:T(8,128)S(1)}, u32[]{:S(2)}, u32[]{:S(2)}) %collective-permute-start.1) | collective-permute-done | bytes 262176 | tf_op jit(solution)/shard_map/ppermute | solution.py:363
  25.2 3.8 %shard_map.53 = (f32[2,8,64,128]{3,2,1,0:T(8,128)S(1)}, f32[2,4,64,128]{3,2,1,0:T(8,128)S(1)}, f32[2,4,64,128]{3,2,1,0:T(8,128)S(1)}, f32[4,64,128]{2,1,0:T(8,128)S(1)}, f32[4,64,128]{2,1,0:T(8,128)S(1)}) custom-call(s32[4]{0:T(128)S(1)} %copy-done.3, f32[4,4,64,128]{3,2,1,0:T(8,128)S(1)} %shard_map.51.window, ...), custom_call_target="tpu_custom_call" | custom-call | flops 8000000 | bytes 8000000 | tf_op jit(solution)/shard_map/pallas_call | solution.py:334
  29.0 0.1 collective-permute-start.9
  29.0 1.3 %collective-permute-done.9.other = f32[4,64,128]{2,1,0:T(8,128)S(1)} collective-permute-done((f32[4,64,128]{2,1,0:T(8,128)S(1)}, f32[4,64,128]{2,1,0:T(8,128)S(1)}, u32[]{:S(2)}, u32[]{:S(2)}) %collective-permute-start.9) | collective-permute-done | bytes 131104 | tf_op jit(solution)/shard_map/ppermute | solution.py:363
  30.4 0.1 collective-permute-start.10
  30.5 0.1 collective-permute-start.14
  30.5 3.7 %collective-permute-start.12 = (f32[2,64,128]{2,1,0:T(8,128)S(1)}, f32[2,64,128]{2,1,0:T(8,128)S(1)}, u32[]{:S(2)}, u32[]{:S(2)}) collective-permute-start(f32[2,64,128]{2,1,0:T(8,128)S(1)} %get-tuple-element.33.one), channel_id=1, source_target_pairs={{0,16},{1,17},{2,18},{3,19},{4,20},{5,21},{6,22},{7,23},{8,24},{9,... | collective-permute-start | bytes 196616 | tf_op jit(solution)/shard_map/ppermute | solution.py:363
  34.2 3.8 %collective-permute-start.15 = (f32[2,4,64,128]{3,2,1,0:T(8,128)S(1)}, f32[2,4,64,128]{3,2,1,0:T(8,128)S(1)}, u32[]{:S(2)}, u32[]{:S(2)}) collective-permute-start(f32[2,4,64,128]{3,2,1,0:T(8,128)S(1)} %get-tuple-element.35.two_low), channel_id=1, source_target_pairs={{0,6},{1,7},{2,0},{3,1},{4,2},{5,3},{6,4},{7,5},{8,14},{9,15},{10,... | collective-permute-start | bytes 786440 | tf_op jit(solution)/shard_map/ppermute | solution.py:363
  38.1 0.0 collective-permute-done.10.other
  38.1 0.1 collective-permute-start.11
  38.2 0.0 collective-permute-done.12.other
  38.2 0.9 %collective-permute-start.13 = (f32[2,64,128]{2,1,0:T(8,128)S(1)}, f32[2,64,128]{2,1,0:T(8,128)S(1)}, u32[]{:S(2)}, u32[]{:S(2)}) collective-permute-start(f32[2,64,128]{2,1,0:T(8,128)S(1)} %shard_map.56.lower), channel_id=1, source_target_pairs={{0,1},{1,0},{2,3},{3,2},{4,5},{5,4},{6,7},{7,6},{8,9},{9,8},{10,11... | collective-permute-start | bytes 196616 | tf_op jit(solution)/shard_map/ppermute | solution.py:363
  39.1 3.3 %collective-permute-done.11.upper_other = f32[2,64,128]{2,1,0:T(8,128)S(1)} collective-permute-done((f32[2,64,128]{2,1,0:T(8,128)S(1)}, f32[2,64,128]{2,1,0:T(8,128)S(1)}, u32[]{:S(2)}, u32[]{:S(2)}) %collective-permute-start.11) | collective-permute-done | bytes 65568 | tf_op jit(solution)/shard_map/ppermute | solution.py:363
  42.4 0.1 collective-permute-done.13.lower_other
  42.5 2.4 %collective-permute-start.17 = (f32[4,64,128]{2,1,0:T(8,128)S(1)}, f32[4,64,128]{2,1,0:T(8,128)S(1)}, u32[]{:S(2)}, u32[]{:S(2)}) collective-permute-start(f32[4,64,128]{2,1,0:T(8,128)S(1)} %shard_map.57.refs_0_.j_mine), channel_id=1, source_target_pairs={{0,6},{1,7},{2,0},{3,1},{4,2},{5,3},{6,4},{7,5},{8,10},{9,11},{10,... | collective-permute-start | bytes 393224 | tf_op jit(solution)/shard_map/ppermute | solution.py:363
  45.0 0.0 collective-permute-done.14.two_left
  45.0 2.1 %collective-permute-done.15.two_right = f32[2,4,64,128]{3,2,1,0:T(8,128)S(1)} collective-permute-done((f32[2,4,64,128]{3,2,1,0:T(8,128)S(1)}, f32[2,4,64,128]{3,2,1,0:T(8,128)S(1)}, u32[]{:S(2)}, u32[]{:S(2)}) %collective-permute-start.15) | collective-permute-done | bytes 262176 | tf_op jit(solution)/shard_map/ppermute | solution.py:363
  47.1 0.0 collective-permute-start.16
  47.1 2.0 %collective-permute-done.17.refs_2_.j_halo = f32[4,64,128]{2,1,0:T(8,128)S(1)} collective-permute-done((f32[4,64,128]{2,1,0:T(8,128)S(1)}, f32[4,64,128]{2,1,0:T(8,128)S(1)}, u32[]{:S(2)}, u32[]{:S(2)}) %collective-permute-start.17) | collective-permute-done | bytes 131104 | tf_op jit(solution)/shard_map/ppermute | solution.py:363
  49.1 0.0 collective-permute-start.18
  49.1 0.0 collective-permute-done.16.refs_1_.j_other
  49.1 1.3 %collective-permute-done.18.refs_3_.j_halo_other = f32[4,64,128]{2,1,0:T(8,128)S(1)} collective-permute-done((f32[4,64,128]{2,1,0:T(8,128)S(1)}, f32[4,64,128]{2,1,0:T(8,128)S(1)}, u32[]{:S(2)}, u32[]{:S(2)}) %collective-permute-start.18) | collective-permute-done | bytes 131104 | tf_op jit(solution)/shard_map/ppermute | solution.py:363
  50.5 4.1 %shard_map.59 = (f32[2,2,2,4,16,128]{5,4,3,2,1,0:T(8,128)S(1)}, f32[2,2,2,4,16,128]{5,4,3,2,1,0:T(8,128)S(1)}) custom-call(s32[4]{0:T(128)S(1)} %copy-done.3, f32[2,16,64,128]{3,2,1,0:T(8,128)S(1)} %get-tuple-element.27.u_ref, f32[2,16,64,128]{3,2,1,0:T(8,128)S(1)} %get-tuple-element.28.u_left_ref, f32[2,16,64,128]{3,2,1,0:T(8,128)S(1)} %get-tuple-element.29.u_right_ref, ...), custom_call_target="tpu_custom_call" | custom-call | flops 8000000 | bytes 8000000 | tf_op jit(solution)/shard_map/pallas_call | solution.py:334
  54.5 0.2 collective-permute-start.20
  54.7 1.4 %collective-permute-done.20.received = f32[2,2,2,4,16,128]{5,4,3,2,1,0:T(8,128)S(1)} collective-permute-done((f32[2,2,2,4,16,128]{5,4,3,2,1,0:T(8,128)S(1)}, f32[2,2,2,4,16,128]{5,4,3,2,1,0:T(8,128)S(1)}, u32[]{:S(2)}, u32[]{:S(2)}) %collective-permute-start.20) | collective-permute-done | bytes 262176 | tf_op jit(solution)/shard_map/ppermute | solution.py:363
  56.2 1.7 %collective-permute-start.21 = (f32[2,4,16,128]{3,2,1,0:T(8,128)S(1)}, f32[2,4,16,128]{3,2,1,0:T(8,128)S(1)}, u32[]{:S(2)}, u32[]{:S(2)}) collective-permute-start(f32[2,4,16,128]{3,2,1,0:T(8,128)S(1)} %get-tuple-element.43), channel_id=1, source_target_pairs={{0,1},{1,0},{2,3},{3,2},{4,5},{5,4},{6,7},{7,6},{8,9},{9,8},{10,11... | collective-permute-start | bytes 196616 | tf_op jit(solution)/shard_map/ppermute | solution.py:363
  57.9 1.0 %collective-permute-start.22 = (f32[2,4,16,128]{3,2,1,0:T(8,128)S(1)}, f32[2,4,16,128]{3,2,1,0:T(8,128)S(1)}, u32[]{:S(2)}, u32[]{:S(2)}) collective-permute-start(f32[2,4,16,128]{3,2,1,0:T(8,128)S(1)} %get-tuple-element.44), channel_id=1, source_target_pairs={{0,16},{1,17},{2,18},{3,19},{4,20},{5,21},{6,22},{7,23},{8,24},{9,... | collective-permute-start | bytes 196616 | tf_op jit(solution)/shard_map/ppermute | solution.py:363
  58.9 1.2 %collective-permute-start.23 = (f32[2,4,16,128]{3,2,1,0:T(8,128)S(1)}, f32[2,4,16,128]{3,2,1,0:T(8,128)S(1)}, u32[]{:S(2)}, u32[]{:S(2)}) collective-permute-start(f32[2,4,16,128]{3,2,1,0:T(8,128)S(1)} %get-tuple-element.45), channel_id=1, source_target_pairs={{0,17},{1,16},{2,19},{3,18},{4,21},{5,20},{6,23},{7,22},{8,25},{9,... | collective-permute-start | bytes 196616 | tf_op jit(solution)/shard_map/ppermute | solution.py:363
  60.2 2.0 %collective-permute-start.19 = (f32[8,128]{1,0:T(8,128)S(1)}, f32[8,128]{1,0:T(8,128)S(1)}, u32[]{:S(2)}, u32[]{:S(2)}) collective-permute-start(f32[8,128]{1,0:T(8,128)S(1)} %shard_map.58), channel_id=1, source_target_pairs={{0,4},{1,5},{2,6},{3,7},{4,0},{5,1},{6,2},{7,3},{8,12},{9,13},{10,... | collective-permute-start | bytes 12296 | tf_op jit(solution)/shard_map/ppermute | solution.py:363
  62.1 2.6 %collective-permute-done.19 = f32[8,128]{1,0:T(8,128)S(1)} collective-permute-done((f32[8,128]{1,0:T(8,128)S(1)}, f32[8,128]{1,0:T(8,128)S(1)}, u32[]{:S(2)}, u32[]{:S(2)}) %collective-permute-start.19) | collective-permute-done | bytes 4128 | tf_op jit(solution)/shard_map/ppermute | solution.py:363
  64.7 0.0 collective-permute-done.21.refs_0_
  64.7 0.0 collective-permute-done.22.refs_1_
  64.7 0.0 collective-permute-done.23.refs_2_
  64.8 0.8 %shard_map.61 = (f32[2,4,16,128]{3,2,1,0:T(8,128)}, f32[2,4,16,128]{3,2,1,0:T(8,128)}) custom-call(f32[2,4,64,128]{3,2,1,0:T(8,128)S(1)} %copy-done.1, f32[8,128]{1,0:T(8,128)S(1)} %add.3.total, f32[2,4,16,128]{3,2,1,0:T(8,128)S(1)} %get-tuple-element.42.own, f32[2,4,16,128]{3,2,1,0:T(8,128)S(1)} %collective-permute-done.21.refs_0_, ...), custom_call_target="tpu_custom_call" | custom-call | flops 1000000 | bytes 1000000 | tf_op jit(solution)/shard_map/pallas_call | solution.py:334
  (8 shorter events, 0.2 us)
Async XLA Ops:
  0.6 1.0 %copy-start = (f32[2,4,64,128]{3,2,1,0:T(8,128)S(1)}, f32[2,4,64,128]{3,2,1,0:T(8,128)}, u32[]{:S(2)}) copy-start(f32[2,4,64,128]{3,2,1,0:T(8,128)} %fields.5) | copy-start | bytes 786436
  1.6 1.0 %copy-start.2 = (f32[4,4,64,128]{3,2,1,0:T(8,128)S(1)}, f32[4,4,64,128]{3,2,1,0:T(8,128)}, u32[]{:S(2)}) copy-start(f32[4,4,64,128]{3,2,1,0:T(8,128)} %starts.3) | copy-start | bytes 1572868
  2.7 9.0 %collective-permute-start.5 = (f32[4,64,128]{2,1,0:T(8,128)S(1)}, f32[4,64,128]{2,1,0:T(8,128)S(1)}, u32[]{:S(2)}, u32[]{:S(2)}) collective-permute-start(f32[4,64,128]{2,1,0:T(8,128)S(1)} %get-tuple-element.26), channel_id=1, source_target_pairs={{0,6},{1,3},{2,0},{3,5},{4,2},{5,7},{6,4},{7,1},{8,14},{9,11},{10,... | collective-permute-start | bytes 393224 | tf_op jit(solution)/shard_map/ppermute | solution.py:363
  7.8 12.8 %copy-start.3 = (s32[4]{0:T(128)S(1)}, s32[4]{0:T(128)}, u32[]{:S(2)}) copy-start(s32[4]{0:T(128)} %labels.5) | copy-start | bytes 52
  7.8 12.7 %collective-permute-start = (f32[2,4,64,128]{3,2,1,0:T(8,128)S(1)}, f32[2,4,64,128]{3,2,1,0:T(8,128)S(1)}, u32[]{:S(2)}, u32[]{:S(2)}) collective-permute-start(f32[2,4,64,128]{3,2,1,0:T(8,128)S(1)} %get-tuple-element.24), channel_id=1, source_target_pairs={{0,7},{1,2},{2,1},{3,4},{4,3},{5,6},{6,5},{7,0},{8,15},{9,10},{10,... | collective-permute-start | bytes 786440 | tf_op jit(solution)/shard_map/ppermute | solution.py:363
  9.0 11.0 %collective-permute-start.3 = (f32[4,64,128]{2,1,0:T(8,128)S(1)}, f32[4,64,128]{2,1,0:T(8,128)S(1)}, u32[]{:S(2)}, u32[]{:S(2)}) collective-permute-start(f32[4,64,128]{2,1,0:T(8,128)S(1)} %get-tuple-element.26), channel_id=1, source_target_pairs={{0,1},{1,0},{2,3},{3,2},{4,5},{5,4},{6,7},{7,6},{8,9},{9,8},{10,11... | collective-permute-start | bytes 393224 | tf_op jit(solution)/shard_map/ppermute | solution.py:363
  11.7 8.3 %collective-permute-start.7 = (f32[4,64,128]{2,1,0:T(8,128)S(1)}, f32[4,64,128]{2,1,0:T(8,128)S(1)}, u32[]{:S(2)}, u32[]{:S(2)}) collective-permute-start(f32[4,64,128]{2,1,0:T(8,128)S(1)} %collective-permute-done.5.piece), channel_id=1, source_target_pairs={{0,24},{1,25},{2,26},{3,27},{4,28},{5,29},{6,30},{7,31},{8,16},{9,... | collective-permute-start | bytes 393224 | tf_op jit(solution)/shard_map/ppermute | solution.py:363
  12.4 9.4 %copy-start.1 = (f32[2,4,64,128]{3,2,1,0:T(8,128)S(1)}, f32[2,4,64,128]{3,2,1,0:T(8,128)}, u32[]{:S(2)}) copy-start(f32[2,4,64,128]{3,2,1,0:T(8,128)} %fields.5) | copy-start | bytes 786436
  12.4 10.7 %collective-permute-start.2 = (f32[2,4,64,128]{3,2,1,0:T(8,128)S(1)}, f32[2,4,64,128]{3,2,1,0:T(8,128)S(1)}, u32[]{:S(2)}, u32[]{:S(2)}) collective-permute-start(f32[2,4,64,128]{3,2,1,0:T(8,128)S(1)} %get-tuple-element.25), channel_id=1, source_target_pairs={{0,6},{1,3},{2,0},{3,5},{4,2},{5,7},{6,4},{7,1},{8,14},{9,11},{10,... | collective-permute-start | bytes 786440 | tf_op jit(solution)/shard_map/ppermute | solution.py:363
  16.0 9.2 %collective-permute-start.1 = (f32[2,4,64,128]{3,2,1,0:T(8,128)S(1)}, f32[2,4,64,128]{3,2,1,0:T(8,128)S(1)}, u32[]{:S(2)}, u32[]{:S(2)}) collective-permute-start(f32[2,4,64,128]{3,2,1,0:T(8,128)S(1)} %get-tuple-element.24), channel_id=1, source_target_pairs={{0,1},{1,0},{2,3},{3,2},{4,5},{5,4},{6,7},{7,6},{8,9},{9,8},{10,11... | collective-permute-start | bytes 786440 | tf_op jit(solution)/shard_map/ppermute | solution.py:363
  19.9 1.3 %collective-permute-start.6 = (f32[4,64,128]{2,1,0:T(8,128)S(1)}, f32[4,64,128]{2,1,0:T(8,128)S(1)}, u32[]{:S(2)}, u32[]{:S(2)}) collective-permute-start(f32[4,64,128]{2,1,0:T(8,128)S(1)} %collective-permute-done.5.piece), channel_id=1, source_target_pairs={{0,8},{1,9},{2,10},{3,11},{4,12},{5,13},{6,14},{7,15},{8,0},{9,1},... | collective-permute-start | bytes 393224 | tf_op jit(solution)/shard_map/ppermute | solution.py:363
  19.9 1.5 %collective-permute-start.4 = (f32[4,64,128]{2,1,0:T(8,128)S(1)}, f32[4,64,128]{2,1,0:T(8,128)S(1)}, u32[]{:S(2)}, u32[]{:S(2)}) collective-permute-start(f32[4,64,128]{2,1,0:T(8,128)S(1)} %collective-permute-done.3.f_swap), channel_id=1, source_target_pairs={{0,8},{1,9},{2,10},{3,11},{4,12},{5,13},{6,14},{7,15},{8,0},{9,1},... | collective-permute-start | bytes 393224 | tf_op jit(solution)/shard_map/ppermute | solution.py:363
  20.5 1.3 %collective-permute-start.8 = (f32[4,64,128]{2,1,0:T(8,128)S(1)}, f32[4,64,128]{2,1,0:T(8,128)S(1)}, u32[]{:S(2)}, u32[]{:S(2)}) collective-permute-start(f32[4,64,128]{2,1,0:T(8,128)S(1)} %collective-permute-done.7.piece_both), channel_id=1, source_target_pairs={{0,8},{1,9},{2,10},{3,11},{4,12},{5,13},{6,14},{7,15},{8,0},{9,1},... | collective-permute-start | bytes 393224 | tf_op jit(solution)/shard_map/ppermute | solution.py:363
  29.0 1.4 %collective-permute-start.9 = (f32[4,64,128]{2,1,0:T(8,128)S(1)}, f32[4,64,128]{2,1,0:T(8,128)S(1)}, u32[]{:S(2)}, u32[]{:S(2)}) collective-permute-start(f32[4,64,128]{2,1,0:T(8,128)S(1)} %get-tuple-element.31), channel_id=1, source_target_pairs={{0,8},{1,9},{2,10},{3,11},{4,12},{5,13},{6,14},{7,15},{8,0},{9,1},... | collective-permute-start | bytes 393224 | tf_op jit(solution)/shard_map/ppermute | solution.py:363
  30.4 7.7 %collective-permute-start.10 = (f32[2,64,128]{2,1,0:T(8,128)S(1)}, f32[2,64,128]{2,1,0:T(8,128)S(1)}, u32[]{:S(2)}, u32[]{:S(2)}) collective-permute-start(f32[2,64,128]{2,1,0:T(8,128)S(1)} %get-tuple-element.32.one), channel_id=1, source_target_pairs={{0,1},{1,0},{2,3},{3,2},{4,5},{5,4},{6,7},{7,6},{8,9},{9,8},{10,11... | collective-permute-start | bytes 196616 | tf_op jit(solution)/shard_map/ppermute | solution.py:363
  30.5 14.5 %collective-permute-start.14 = (f32[2,4,64,128]{3,2,1,0:T(8,128)S(1)}, f32[2,4,64,128]{3,2,1,0:T(8,128)S(1)}, u32[]{:S(2)}, u32[]{:S(2)}) collective-permute-start(f32[2,4,64,128]{3,2,1,0:T(8,128)S(1)} %get-tuple-element.34.two_high), channel_id=1, source_target_pairs={{0,2},{1,3},{2,4},{3,5},{4,6},{5,7},{6,0},{7,1},{8,10},{9,11},{10,... | collective-permute-start | bytes 786440 | tf_op jit(solution)/shard_map/ppermute | solution.py:363
  30.5 7.6 %collective-permute-start.12 = (f32[2,64,128]{2,1,0:T(8,128)S(1)}, f32[2,64,128]{2,1,0:T(8,128)S(1)}, u32[]{:S(2)}, u32[]{:S(2)}) collective-permute-start(f32[2,64,128]{2,1,0:T(8,128)S(1)} %get-tuple-element.33.one), channel_id=1, source_target_pairs={{0,16},{1,17},{2,18},{3,19},{4,20},{5,21},{6,22},{7,23},{8,24},{9,... | collective-permute-start | bytes 196616 | tf_op jit(solution)/shard_map/ppermute | solution.py:363
  34.2 12.8 %collective-permute-start.15 = (f32[2,4,64,128]{3,2,1,0:T(8,128)S(1)}, f32[2,4,64,128]{3,2,1,0:T(8,128)S(1)}, u32[]{:S(2)}, u32[]{:S(2)}) collective-permute-start(f32[2,4,64,128]{3,2,1,0:T(8,128)S(1)} %get-tuple-element.35.two_low), channel_id=1, source_target_pairs={{0,6},{1,7},{2,0},{3,1},{4,2},{5,3},{6,4},{7,5},{8,14},{9,15},{10,... | collective-permute-start | bytes 786440 | tf_op jit(solution)/shard_map/ppermute | solution.py:363
  38.1 4.3 %collective-permute-start.11 = (f32[2,64,128]{2,1,0:T(8,128)S(1)}, f32[2,64,128]{2,1,0:T(8,128)S(1)}, u32[]{:S(2)}, u32[]{:S(2)}) collective-permute-start(f32[2,64,128]{2,1,0:T(8,128)S(1)} %shard_map.55.upper), channel_id=1, source_target_pairs={{0,16},{1,17},{2,18},{3,19},{4,20},{5,21},{6,22},{7,23},{8,24},{9,... | collective-permute-start | bytes 196616 | tf_op jit(solution)/shard_map/ppermute | solution.py:363
  38.2 4.3 %collective-permute-start.13 = (f32[2,64,128]{2,1,0:T(8,128)S(1)}, f32[2,64,128]{2,1,0:T(8,128)S(1)}, u32[]{:S(2)}, u32[]{:S(2)}) collective-permute-start(f32[2,64,128]{2,1,0:T(8,128)S(1)} %shard_map.56.lower), channel_id=1, source_target_pairs={{0,1},{1,0},{2,3},{3,2},{4,5},{5,4},{6,7},{7,6},{8,9},{9,8},{10,11... | collective-permute-start | bytes 196616 | tf_op jit(solution)/shard_map/ppermute | solution.py:363
  42.5 6.6 %collective-permute-start.17 = (f32[4,64,128]{2,1,0:T(8,128)S(1)}, f32[4,64,128]{2,1,0:T(8,128)S(1)}, u32[]{:S(2)}, u32[]{:S(2)}) collective-permute-start(f32[4,64,128]{2,1,0:T(8,128)S(1)} %shard_map.57.refs_0_.j_mine), channel_id=1, source_target_pairs={{0,6},{1,7},{2,0},{3,1},{4,2},{5,3},{6,4},{7,5},{8,10},{9,11},{10,... | collective-permute-start | bytes 393224 | tf_op jit(solution)/shard_map/ppermute | solution.py:363
  47.1 2.0 %collective-permute-start.16 = (f32[4,64,128]{2,1,0:T(8,128)S(1)}, f32[4,64,128]{2,1,0:T(8,128)S(1)}, u32[]{:S(2)}, u32[]{:S(2)}) collective-permute-start(f32[4,64,128]{2,1,0:T(8,128)S(1)} %shard_map.57.refs_0_.j_mine), channel_id=1, source_target_pairs={{0,8},{1,9},{2,10},{3,11},{4,12},{5,13},{6,14},{7,15},{8,0},{9,1},... | collective-permute-start | bytes 393224 | tf_op jit(solution)/shard_map/ppermute | solution.py:363
  49.1 1.3 %collective-permute-start.18 = (f32[4,64,128]{2,1,0:T(8,128)S(1)}, f32[4,64,128]{2,1,0:T(8,128)S(1)}, u32[]{:S(2)}, u32[]{:S(2)}) collective-permute-start(f32[4,64,128]{2,1,0:T(8,128)S(1)} %collective-permute-done.17.refs_2_.j_halo), channel_id=1, source_target_pairs={{0,8},{1,9},{2,10},{3,11},{4,12},{5,13},{6,14},{7,15},{8,0},{9,1},... | collective-permute-start | bytes 393224 | tf_op jit(solution)/shard_map/ppermute | solution.py:363
  54.5 1.6 %collective-permute-start.20 = (f32[2,2,2,4,16,128]{5,4,3,2,1,0:T(8,128)S(1)}, f32[2,2,2,4,16,128]{5,4,3,2,1,0:T(8,128)S(1)}, u32[]{:S(2)}, u32[]{:S(2)}) collective-permute-start(f32[2,2,2,4,16,128]{5,4,3,2,1,0:T(8,128)S(1)} %get-tuple-element.41), channel_id=1, source_target_pairs={{0,8},{1,9},{2,10},{3,11},{4,12},{5,13},{6,14},{7,15},{8,0},{9,1},... | collective-permute-start | bytes 786440 | tf_op jit(solution)/shard_map/ppermute | solution.py:363
  56.2 8.6 %collective-permute-start.21 = (f32[2,4,16,128]{3,2,1,0:T(8,128)S(1)}, f32[2,4,16,128]{3,2,1,0:T(8,128)S(1)}, u32[]{:S(2)}, u32[]{:S(2)}) collective-permute-start(f32[2,4,16,128]{3,2,1,0:T(8,128)S(1)} %get-tuple-element.43), channel_id=1, source_target_pairs={{0,1},{1,0},{2,3},{3,2},{4,5},{5,4},{6,7},{7,6},{8,9},{9,8},{10,11... | collective-permute-start | bytes 196616 | tf_op jit(solution)/shard_map/ppermute | solution.py:363
  57.9 6.8 %collective-permute-start.22 = (f32[2,4,16,128]{3,2,1,0:T(8,128)S(1)}, f32[2,4,16,128]{3,2,1,0:T(8,128)S(1)}, u32[]{:S(2)}, u32[]{:S(2)}) collective-permute-start(f32[2,4,16,128]{3,2,1,0:T(8,128)S(1)} %get-tuple-element.44), channel_id=1, source_target_pairs={{0,16},{1,17},{2,18},{3,19},{4,20},{5,21},{6,22},{7,23},{8,24},{9,... | collective-permute-start | bytes 196616 | tf_op jit(solution)/shard_map/ppermute | solution.py:363
  58.9 5.8 %collective-permute-start.23 = (f32[2,4,16,128]{3,2,1,0:T(8,128)S(1)}, f32[2,4,16,128]{3,2,1,0:T(8,128)S(1)}, u32[]{:S(2)}, u32[]{:S(2)}) collective-permute-start(f32[2,4,16,128]{3,2,1,0:T(8,128)S(1)} %get-tuple-element.45), channel_id=1, source_target_pairs={{0,17},{1,16},{2,19},{3,18},{4,21},{5,20},{6,23},{7,22},{8,25},{9,... | collective-permute-start | bytes 196616 | tf_op jit(solution)/shard_map/ppermute | solution.py:363
  60.2 4.6 %collective-permute-start.19 = (f32[8,128]{1,0:T(8,128)S(1)}, f32[8,128]{1,0:T(8,128)S(1)}, u32[]{:S(2)}, u32[]{:S(2)}) collective-permute-start(f32[8,128]{1,0:T(8,128)S(1)} %shard_map.58), channel_id=1, source_target_pairs={{0,4},{1,5},{2,6},{3,7},{4,0},{5,1},{6,2},{7,3},{8,12},{9,13},{10,... | collective-permute-start | bytes 12296 | tf_op jit(solution)/shard_map/ppermute | solution.py:363

commit v7 on v6

--- a/solution.py
+++ b/solution.py
@@ -92,13 +92,16 @@
     )
 
 
-def pack_kernel(starts, fields, field_ref, other_ref, own_ref):
+def pack_kernel(starts, other_ref, own_ref):
     arms = starts.shape[0] // 2
     side = lax.rem(lax.axis_index("space"), 2)
-    field_ref[...] = fields[lax.rem(lax.axis_index("arm"), 2)]
     for j in range(arms):
         other_ref[j] = starts[(1 - side) * arms + j]
         own_ref[j] = starts[side * arms + j]
+
+
+def pick_kernel(fields, field_ref):
+    field_ref[...] = fields[lax.rem(lax.axis_index("arm"), 2)]
 
 
 def places(block):
@@ -377,18 +380,8 @@
     def to_across(value):
         return send(value, lambda x, c, p, h: (x, c, p + 2 * h - 1, 1 - h))
 
-    field_own, other_set, own_set = call(
-        pack_kernel,
-        (
-            f32((block, rows, columns)),
-            f32((arms, block, rows, columns)),
-            f32((arms, block, rows, columns)),
-        ),
-        [],
-        0,
-        starts,
-        fields,
-    )
+    field_own = call(pick_kernel, f32((block, rows, columns)), [], 0, fields)
+    other_set, own_set = call(pack_kernel, (f32((arms, block, rows, columns)),) * 2, [], 0, starts)
     field_got = send(field_own, lambda x, c, p, h: (x, c, p + 2 * h - 1, 1 - h if x else h))
     across = to_across(other_set)
     swap = to_side(other_set)

time: 65.8 us -> 65.4 us (level)
  starting transfers between devices: 28.4 us -> 26.8 us
  waiting for transfers between devices: 23.7 us -> 24.9 us
    ppermute x24, starting transfers between devices: 28.4 us -> 26.8 us  [send(): return lax.ppermute(value, AXES, perm)]
    ppermute x24, waiting for transfers between devices: 23.7 us -> 24.9 us  [send(): return lax.ppermute(value, AXES, perm)]
    pallas_call x12 -> x13, Pallas kernels: 10.7 us -> 10.7 us  [call(): pl.pallas_call(kernel, out_shape=out_shape, in_specs=specs, out_specs=jax...]
where the time goes in v7:
time: 65.4 us; the launch traced here: 65.2 us
  starting transfers between devices  26.8 us (41%)
  waiting for transfers between devices  24.9 us (38%)
  Pallas kernels  10.7 us (16%)
  local copies, waits for them, and re-layouts  2 us (3%)
  between operations  0.79 us (1%)
    ppermute x24, starting transfers between devices, send(): return lax.ppermute(value, AXES, perm)  26.8 us
    ppermute x24, waiting for transfers between devices, send(): return lax.ppermute(value, AXES, perm)  24.9 us
    pallas_call x13, Pallas kernels, call(): pl.pallas_call(kernel, out_shape=out_shape, in_specs=specs, out_specs=jax...  10.7 us
    unnamed x8, local copies, waits for them, and re-layouts  2 us
  transfers between devices with their start and end apart: 24, of which 14 were waited for; matrix products, arithmetic and copies ran while one was open for 0% of the time, Pallas kernels for 3%

profile of v7, /device:TPU:0, one launch (start us, length us, event | category | flops | bytes accessed | tf_op | source)
XLA Modules:
  0.0 65.2 jit_solution(16760474375136282932)
XLA Ops:
  0.6 0.0 copy-start
  0.6 0.9 %copy-done = f32[2,4,64,128]{3,2,1,0:T(8,128)S(1)} copy-done((f32[2,4,64,128]{3,2,1,0:T(8,128)S(1)}, f32[2,4,64,128]{3,2,1,0:T(8,128)}, u32[]{:S(2)}) %copy-start) | copy-done | bytes 262168
  1.6 5.1 %collective-permute-start.5 = (f32[4,64,128]{2,1,0:T(8,128)S(1)}, f32[4,64,128]{2,1,0:T(8,128)S(1)}, u32[]{:S(2)}, u32[]{:S(2)}) collective-permute-start(f32[4,64,128]{2,1,0:T(8,128)S(1)} %shard_map.52), channel_id=1, source_target_pairs={{0,6},{1,3},{2,0},{3,5},{4,2},{5,7},{6,4},{7,1},{8,14},{9,11},{10,... | collective-permute-start | bytes 393224 | tf_op jit(solution)/shard_map/ppermute | solution.py:366
  6.7 0.0 copy-start.2
  6.7 1.0 %copy-done.2 = f32[4,4,64,128]{3,2,1,0:T(8,128)S(1)} copy-done((f32[4,4,64,128]{3,2,1,0:T(8,128)S(1)}, f32[4,4,64,128]{3,2,1,0:T(8,128)}, u32[]{:S(2)}) %copy-start.2) | copy-done | bytes 524312
  7.8 0.0 copy-start.3
  7.8 1.2 %collective-permute-start = (f32[2,4,64,128]{3,2,1,0:T(8,128)S(1)}, f32[2,4,64,128]{3,2,1,0:T(8,128)S(1)}, u32[]{:S(2)}, u32[]{:S(2)}) collective-permute-start(f32[2,4,64,128]{3,2,1,0:T(8,128)S(1)} %get-tuple-element.23), channel_id=1, source_target_pairs={{0,7},{1,2},{2,1},{3,4},{4,3},{5,6},{6,5},{7,0},{8,15},{9,10},{10,... | collective-permute-start | bytes 786440 | tf_op jit(solution)/shard_map/ppermute | solution.py:366
  9.0 0.0 collective-permute-start.3
  9.0 1.1 %collective-permute-done.5.piece = f32[4,64,128]{2,1,0:T(8,128)S(1)} collective-permute-done((f32[4,64,128]{2,1,0:T(8,128)S(1)}, f32[4,64,128]{2,1,0:T(8,128)S(1)}, u32[]{:S(2)}, u32[]{:S(2)}) %collective-permute-start.5) | collective-permute-done | bytes 131104 | tf_op jit(solution)/shard_map/ppermute | solution.py:366
  10.1 1.2 %collective-permute-start.7 = (f32[4,64,128]{2,1,0:T(8,128)S(1)}, f32[4,64,128]{2,1,0:T(8,128)S(1)}, u32[]{:S(2)}, u32[]{:S(2)}) collective-permute-start(f32[4,64,128]{2,1,0:T(8,128)S(1)} %collective-permute-done.5.piece), channel_id=1, source_target_pairs={{0,24},{1,25},{2,26},{3,27},{4,28},{5,29},{6,30},{7,31},{8,16},{9,... | collective-permute-start | bytes 393224 | tf_op jit(solution)/shard_map/ppermute | solution.py:366
  11.3 0.0 copy-start.1
  11.3 3.1 %collective-permute-start.2 = (f32[2,4,64,128]{3,2,1,0:T(8,128)S(1)}, f32[2,4,64,128]{3,2,1,0:T(8,128)S(1)}, u32[]{:S(2)}, u32[]{:S(2)}) collective-permute-start(f32[2,4,64,128]{3,2,1,0:T(8,128)S(1)} %get-tuple-element.24), channel_id=1, source_target_pairs={{0,6},{1,3},{2,0},{3,5},{4,2},{5,7},{6,4},{7,1},{8,14},{9,11},{10,... | collective-permute-start | bytes 786440 | tf_op jit(solution)/shard_map/ppermute | solution.py:366
  14.4 0.0 collective-permute-start.1
  14.4 6.4 %collective-permute-done.3.f_swap = f32[4,64,128]{2,1,0:T(8,128)S(1)} collective-permute-done((f32[4,64,128]{2,1,0:T(8,128)S(1)}, f32[4,64,128]{2,1,0:T(8,128)S(1)}, u32[]{:S(2)}, u32[]{:S(2)}) %collective-permute-start.3) | collective-permute-done | bytes 131104 | tf_op jit(solution)/shard_map/ppermute | solution.py:366
  20.8 0.0 collective-permute-start.6
  20.8 0.0 collective-permute-done.7.piece_both
  20.8 0.5 collective-permute-start.4
  21.3 0.0 collective-permute-done.across
  21.3 0.1 collective-permute-start.8
  21.4 0.0 copy-done.3
  21.4 0.6 shard_map.51.window
  22.0 0.2 collective-permute-done.6.piece_core
  22.2 0.2 collective-permute-done.4.g_swap
  22.4 0.3 collective-permute-done.8.piece_chip
  22.7 0.0 copy-done.1
  22.7 1.3 %shard_map.53 = (f32[2,16,64,128]{3,2,1,0:T(8,128)S(1)}, f32[2,16,64,128]{3,2,1,0:T(8,128)S(1)}, f32[2,16,64,128]{3,2,1,0:T(8,128)S(1)}) custom-call(f32[2,4,64,128]{3,2,1,0:T(8,128)S(1)} %copy-done.1, f32[4,64,128]{2,1,0:T(8,128)S(1)} %collective-permute-done.3.f_swap, f32[4,64,128]{2,1,0:T(8,128)S(1)} %collective-permute-done.4.g_swap, ...), custom_call_target="tpu_custom_call" | custom-call | flops 1000000 | bytes 1000000 | tf_op jit(solution)/shard_map/pallas_call | solution.py:337
  24.0 0.0 collective-permute-done.2.straight
  24.0 1.2 %collective-permute-done.1.swap = f32[2,4,64,128]{3,2,1,0:T(8,128)S(1)} collective-permute-done((f32[2,4,64,128]{3,2,1,0:T(8,128)S(1)}, f32[2,4,64,128]{3,2,1,0:T(8,128)S(1)}, u32[]{:S(2)}, u32[]{:S(2)}) %collective-permute-start.1) | collective-permute-done | bytes 262176 | tf_op jit(solution)/shard_map/ppermute | solution.py:366
  25.2 3.8 %shard_map.54 = (f32[2,8,64,128]{3,2,1,0:T(8,128)S(1)}, f32[2,4,64,128]{3,2,1,0:T(8,128)S(1)}, f32[2,4,64,128]{3,2,1,0:T(8,128)S(1)}, f32[4,64,128]{2,1,0:T(8,128)S(1)}, f32[4,64,128]{2,1,0:T(8,128)S(1)}) custom-call(s32[4]{0:T(128)S(1)} %copy-done.3, f32[4,4,64,128]{3,2,1,0:T(8,128)S(1)} %shard_map.51.window, ...), custom_call_target="tpu_custom_call" | custom-call | flops 8000000 | bytes 8000000 | tf_op jit(solution)/shard_map/pallas_call | solution.py:337
  29.0 0.1 collective-permute-start.9
  29.1 1.3 %collective-permute-done.9.other = f32[4,64,128]{2,1,0:T(8,128)S(1)} collective-permute-done((f32[4,64,128]{2,1,0:T(8,128)S(1)}, f32[4,64,128]{2,1,0:T(8,128)S(1)}, u32[]{:S(2)}, u32[]{:S(2)}) %collective-permute-start.9) | collective-permute-done | bytes 131104 | tf_op jit(solution)/shard_map/ppermute | solution.py:366
  30.5 0.1 collective-permute-start.10
  30.5 0.1 collective-permute-start.14
  30.6 2.5 %collective-permute-start.12 = (f32[2,64,128]{2,1,0:T(8,128)S(1)}, f32[2,64,128]{2,1,0:T(8,128)S(1)}, u32[]{:S(2)}, u32[]{:S(2)}) collective-permute-start(f32[2,64,128]{2,1,0:T(8,128)S(1)} %get-tuple-element.31.one), channel_id=1, source_target_pairs={{0,16},{1,17},{2,18},{3,19},{4,20},{5,21},{6,22},{7,23},{8,24},{9,... | collective-permute-start | bytes 196616 | tf_op jit(solution)/shard_map/ppermute | solution.py:366
  33.2 3.8 %collective-permute-start.15 = (f32[2,4,64,128]{3,2,1,0:T(8,128)S(1)}, f32[2,4,64,128]{3,2,1,0:T(8,128)S(1)}, u32[]{:S(2)}, u32[]{:S(2)}) collective-permute-start(f32[2,4,64,128]{3,2,1,0:T(8,128)S(1)} %get-tuple-element.33.two_low), channel_id=1, source_target_pairs={{0,6},{1,7},{2,0},{3,1},{4,2},{5,3},{6,4},{7,5},{8,14},{9,15},{10,... | collective-permute-start | bytes 786440 | tf_op jit(solution)/shard_map/ppermute | solution.py:366
  37.0 0.0 collective-permute-done.10.other
  37.0 0.1 collective-permute-start.11
  37.1 0.0 collective-permute-done.12.other
  37.1 1.5 %collective-permute-start.13 = (f32[2,64,128]{2,1,0:T(8,128)S(1)}, f32[2,64,128]{2,1,0:T(8,128)S(1)}, u32[]{:S(2)}, u32[]{:S(2)}) collective-permute-start(f32[2,64,128]{2,1,0:T(8,128)S(1)} %shard_map.57.lower), channel_id=1, source_target_pairs={{0,1},{1,0},{2,3},{3,2},{4,5},{5,4},{6,7},{7,6},{8,9},{9,8},{10,11... | collective-permute-start | bytes 196616 | tf_op jit(solution)/shard_map/ppermute | solution.py:366
  38.6 2.8 %collective-permute-done.11.upper_other = f32[2,64,128]{2,1,0:T(8,128)S(1)} collective-permute-done((f32[2,64,128]{2,1,0:T(8,128)S(1)}, f32[2,64,128]{2,1,0:T(8,128)S(1)}, u32[]{:S(2)}, u32[]{:S(2)}) %collective-permute-start.11) | collective-permute-done | bytes 65568 | tf_op jit(solution)/shard_map/ppermute | solution.py:366
  41.3 0.1 collective-permute-done.13.lower_other
  41.5 2.4 %collective-permute-start.17 = (f32[4,64,128]{2,1,0:T(8,128)S(1)}, f32[4,64,128]{2,1,0:T(8,128)S(1)}, u32[]{:S(2)}, u32[]{:S(2)}) collective-permute-start(f32[4,64,128]{2,1,0:T(8,128)S(1)} %shard_map.58.refs_0_.j_mine), channel_id=1, source_target_pairs={{0,6},{1,7},{2,0},{3,1},{4,2},{5,3},{6,4},{7,5},{8,10},{9,11},{10,... | collective-permute-start | bytes 393224 | tf_op jit(solution)/shard_map/ppermute | solution.py:366
  43.9 0.0 collective-permute-done.14.two_left
  43.9 3.0 %collective-permute-done.15.two_right = f32[2,4,64,128]{3,2,1,0:T(8,128)S(1)} collective-permute-done((f32[2,4,64,128]{3,2,1,0:T(8,128)S(1)}, f32[2,4,64,128]{3,2,1,0:T(8,128)S(1)}, u32[]{:S(2)}, u32[]{:S(2)}) %collective-permute-start.15) | collective-permute-done | bytes 262176 | tf_op jit(solution)/shard_map/ppermute | solution.py:366
  46.9 0.0 collective-permute-start.16
  46.9 2.2 %collective-permute-done.17.refs_2_.j_halo = f32[4,64,128]{2,1,0:T(8,128)S(1)} collective-permute-done((f32[4,64,128]{2,1,0:T(8,128)S(1)}, f32[4,64,128]{2,1,0:T(8,128)S(1)}, u32[]{:S(2)}, u32[]{:S(2)}) %collective-permute-start.17) | collective-permute-done | bytes 131104 | tf_op jit(solution)/shard_map/ppermute | solution.py:366
  49.1 0.0 collective-permute-start.18
  49.1 0.0 collective-permute-done.16.refs_1_.j_other
  49.1 1.3 %collective-permute-done.18.refs_3_.j_halo_other = f32[4,64,128]{2,1,0:T(8,128)S(1)} collective-permute-done((f32[4,64,128]{2,1,0:T(8,128)S(1)}, f32[4,64,128]{2,1,0:T(8,128)S(1)}, u32[]{:S(2)}, u32[]{:S(2)}) %collective-permute-start.18) | collective-permute-done | bytes 131104 | tf_op jit(solution)/shard_map/ppermute | solution.py:366
  50.5 4.1 %shard_map.60 = (f32[2,2,2,4,16,128]{5,4,3,2,1,0:T(8,128)S(1)}, f32[2,2,2,4,16,128]{5,4,3,2,1,0:T(8,128)S(1)}) custom-call(s32[4]{0:T(128)S(1)} %copy-done.3, f32[2,16,64,128]{3,2,1,0:T(8,128)S(1)} %get-tuple-element.25.u_ref, f32[2,16,64,128]{3,2,1,0:T(8,128)S(1)} %get-tuple-element.26.u_left_ref, f32[2,16,64,128]{3,2,1,0:T(8,128)S(1)} %get-tuple-element.27.u_right_ref, ...), custom_call_target="tpu_custom_call" | custom-call | flops 8000000 | bytes 8000000 | tf_op jit(solution)/shard_map/pallas_call | solution.py:337
  54.5 0.2 collective-permute-start.20
  54.7 1.4 %collective-permute-done.20.received = f32[2,2,2,4,16,128]{5,4,3,2,1,0:T(8,128)S(1)} collective-permute-done((f32[2,2,2,4,16,128]{5,4,3,2,1,0:T(8,128)S(1)}, f32[2,2,2,4,16,128]{5,4,3,2,1,0:T(8,128)S(1)}, u32[]{:S(2)}, u32[]{:S(2)}) %collective-permute-start.20) | collective-permute-done | bytes 262176 | tf_op jit(solution)/shard_map/ppermute | solution.py:366
  56.2 1.2 %collective-permute-start.21 = (f32[2,4,16,128]{3,2,1,0:T(8,128)S(1)}, f32[2,4,16,128]{3,2,1,0:T(8,128)S(1)}, u32[]{:S(2)}, u32[]{:S(2)}) collective-permute-start(f32[2,4,16,128]{3,2,1,0:T(8,128)S(1)} %get-tuple-element.41), channel_id=1, source_target_pairs={{0,1},{1,0},{2,3},{3,2},{4,5},{5,4},{6,7},{7,6},{8,9},{9,8},{10,11... | collective-permute-start | bytes 196616 | tf_op jit(solution)/shard_map/ppermute | solution.py:366
  57.3 0.5 collective-permute-start.22
  57.8 1.9 %collective-permute-start.23 = (f32[2,4,16,128]{3,2,1,0:T(8,128)S(1)}, f32[2,4,16,128]{3,2,1,0:T(8,128)S(1)}, u32[]{:S(2)}, u32[]{:S(2)}) collective-permute-start(f32[2,4,16,128]{3,2,1,0:T(8,128)S(1)} %get-tuple-element.43), channel_id=1, source_target_pairs={{0,17},{1,16},{2,19},{3,18},{4,21},{5,20},{6,23},{7,22},{8,25},{9,... | collective-permute-start | bytes 196616 | tf_op jit(solution)/shard_map/ppermute | solution.py:366
  59.7 1.3 %collective-permute-start.19 = (f32[8,128]{1,0:T(8,128)S(1)}, f32[8,128]{1,0:T(8,128)S(1)}, u32[]{:S(2)}, u32[]{:S(2)}) collective-permute-start(f32[8,128]{1,0:T(8,128)S(1)} %shard_map.59), channel_id=1, source_target_pairs={{0,4},{1,5},{2,6},{3,7},{4,0},{5,1},{6,2},{7,3},{8,12},{9,13},{10,... | collective-permute-start | bytes 12296 | tf_op jit(solution)/shard_map/ppermute | solution.py:366
  61.0 3.3 %collective-permute-done.19 = f32[8,128]{1,0:T(8,128)S(1)} collective-permute-done((f32[8,128]{1,0:T(8,128)S(1)}, f32[8,128]{1,0:T(8,128)S(1)}, u32[]{:S(2)}, u32[]{:S(2)}) %collective-permute-start.19) | collective-permute-done | bytes 4128 | tf_op jit(solution)/shard_map/ppermute | solution.py:366
  64.3 0.0 collective-permute-done.21.refs_0_
  64.3 0.0 collective-permute-done.22.refs_1_
  64.3 0.0 collective-permute-done.23.refs_2_
  64.3 0.8 %shard_map.62 = (f32[2,4,16,128]{3,2,1,0:T(8,128)}, f32[2,4,16,128]{3,2,1,0:T(8,128)}) custom-call(f32[2,4,64,128]{3,2,1,0:T(8,128)S(1)} %copy-done.1, f32[8,128]{1,0:T(8,128)S(1)} %add.3.total, f32[2,4,16,128]{3,2,1,0:T(8,128)S(1)} %get-tuple-element.40.own, f32[2,4,16,128]{3,2,1,0:T(8,128)S(1)} %collective-permute-done.21.refs_0_, ...), custom_call_target="tpu_custom_call" | custom-call | flops 1000000 | bytes 1000000 | tf_op jit(solution)/shard_map/pallas_call | solution.py:337
  (9 shorter events, 0.2 us)
Async XLA Ops:
  0.6 1.0 %copy-start = (f32[2,4,64,128]{3,2,1,0:T(8,128)S(1)}, f32[2,4,64,128]{3,2,1,0:T(8,128)}, u32[]{:S(2)}) copy-start(f32[2,4,64,128]{3,2,1,0:T(8,128)} %fields.5) | copy-start | bytes 786436
  1.6 8.5 %collective-permute-start.5 = (f32[4,64,128]{2,1,0:T(8,128)S(1)}, f32[4,64,128]{2,1,0:T(8,128)S(1)}, u32[]{:S(2)}, u32[]{:S(2)}) collective-permute-start(f32[4,64,128]{2,1,0:T(8,128)S(1)} %shard_map.52), channel_id=1, source_target_pairs={{0,6},{1,3},{2,0},{3,5},{4,2},{5,7},{6,4},{7,1},{8,14},{9,11},{10,... | collective-permute-start | bytes 393224 | tf_op jit(solution)/shard_map/ppermute | solution.py:366
  6.7 1.0 %copy-start.2 = (f32[4,4,64,128]{3,2,1,0:T(8,128)S(1)}, f32[4,4,64,128]{3,2,1,0:T(8,128)}, u32[]{:S(2)}) copy-start(f32[4,4,64,128]{3,2,1,0:T(8,128)} %starts.3) | copy-start | bytes 1572868
  7.8 13.6 %copy-start.3 = (s32[4]{0:T(128)S(1)}, s32[4]{0:T(128)}, u32[]{:S(2)}) copy-start(s32[4]{0:T(128)} %labels.5) | copy-start | bytes 52
  7.8 13.5 %collective-permute-start = (f32[2,4,64,128]{3,2,1,0:T(8,128)S(1)}, f32[2,4,64,128]{3,2,1,0:T(8,128)S(1)}, u32[]{:S(2)}, u32[]{:S(2)}) collective-permute-start(f32[2,4,64,128]{3,2,1,0:T(8,128)S(1)} %get-tuple-element.23), channel_id=1, source_target_pairs={{0,7},{1,2},{2,1},{3,4},{4,3},{5,6},{6,5},{7,0},{8,15},{9,10},{10,... | collective-permute-start | bytes 786440 | tf_op jit(solution)/shard_map/ppermute | solution.py:366
  9.0 11.8 %collective-permute-start.3 = (f32[4,64,128]{2,1,0:T(8,128)S(1)}, f32[4,64,128]{2,1,0:T(8,128)S(1)}, u32[]{:S(2)}, u32[]{:S(2)}) collective-permute-start(f32[4,64,128]{2,1,0:T(8,128)S(1)} %shard_map.52), channel_id=1, source_target_pairs={{0,1},{1,0},{2,3},{3,2},{4,5},{5,4},{6,7},{7,6},{8,9},{9,8},{10,11... | collective-permute-start | bytes 393224 | tf_op jit(solution)/shard_map/ppermute | solution.py:366
  10.1 10.7 %collective-permute-start.7 = (f32[4,64,128]{2,1,0:T(8,128)S(1)}, f32[4,64,128]{2,1,0:T(8,128)S(1)}, u32[]{:S(2)}, u32[]{:S(2)}) collective-permute-start(f32[4,64,128]{2,1,0:T(8,128)S(1)} %collective-permute-done.5.piece), channel_id=1, source_target_pairs={{0,24},{1,25},{2,26},{3,27},{4,28},{5,29},{6,30},{7,31},{8,16},{9,... | collective-permute-start | bytes 393224 | tf_op jit(solution)/shard_map/ppermute | solution.py:366
  11.3 11.3 %copy-start.1 = (f32[2,4,64,128]{3,2,1,0:T(8,128)S(1)}, f32[2,4,64,128]{3,2,1,0:T(8,128)}, u32[]{:S(2)}) copy-start(f32[2,4,64,128]{3,2,1,0:T(8,128)} %fields.5) | copy-start | bytes 786436
  11.3 12.6 %collective-permute-start.2 = (f32[2,4,64,128]{3,2,1,0:T(8,128)S(1)}, f32[2,4,64,128]{3,2,1,0:T(8,128)S(1)}, u32[]{:S(2)}, u32[]{:S(2)}) collective-permute-start(f32[2,4,64,128]{3,2,1,0:T(8,128)S(1)} %get-tuple-element.24), channel_id=1, source_target_pairs={{0,6},{1,3},{2,0},{3,5},{4,2},{5,7},{6,4},{7,1},{8,14},{9,11},{10,... | collective-permute-start | bytes 786440 | tf_op jit(solution)/shard_map/ppermute | solution.py:366
  14.4 10.8 %collective-permute-start.1 = (f32[2,4,64,128]{3,2,1,0:T(8,128)S(1)}, f32[2,4,64,128]{3,2,1,0:T(8,128)S(1)}, u32[]{:S(2)}, u32[]{:S(2)}) collective-permute-start(f32[2,4,64,128]{3,2,1,0:T(8,128)S(1)} %get-tuple-element.23), channel_id=1, source_target_pairs={{0,1},{1,0},{2,3},{3,2},{4,5},{5,4},{6,7},{7,6},{8,9},{9,8},{10,11... | collective-permute-start | bytes 786440 | tf_op jit(solution)/shard_map/ppermute | solution.py:366
  20.8 1.3 %collective-permute-start.6 = (f32[4,64,128]{2,1,0:T(8,128)S(1)}, f32[4,64,128]{2,1,0:T(8,128)S(1)}, u32[]{:S(2)}, u32[]{:S(2)}) collective-permute-start(f32[4,64,128]{2,1,0:T(8,128)S(1)} %collective-permute-done.5.piece), channel_id=1, source_target_pairs={{0,8},{1,9},{2,10},{3,11},{4,12},{5,13},{6,14},{7,15},{8,0},{9,1},... | collective-permute-start | bytes 393224 | tf_op jit(solution)/shard_map/ppermute | solution.py:366
  20.8 1.5 %collective-permute-start.4 = (f32[4,64,128]{2,1,0:T(8,128)S(1)}, f32[4,64,128]{2,1,0:T(8,128)S(1)}, u32[]{:S(2)}, u32[]{:S(2)}) collective-permute-start(f32[4,64,128]{2,1,0:T(8,128)S(1)} %collective-permute-done.3.f_swap), channel_id=1, source_target_pairs={{0,8},{1,9},{2,10},{3,11},{4,12},{5,13},{6,14},{7,15},{8,0},{9,1},... | collective-permute-start | bytes 393224 | tf_op jit(solution)/shard_map/ppermute | solution.py:366
  21.3 1.3 %collective-permute-start.8 = (f32[4,64,128]{2,1,0:T(8,128)S(1)}, f32[4,64,128]{2,1,0:T(8,128)S(1)}, u32[]{:S(2)}, u32[]{:S(2)}) collective-permute-start(f32[4,64,128]{2,1,0:T(8,128)S(1)} %collective-permute-done.7.piece_both), channel_id=1, source_target_pairs={{0,8},{1,9},{2,10},{3,11},{4,12},{5,13},{6,14},{7,15},{8,0},{9,1},... | collective-permute-start | bytes 393224 | tf_op jit(solution)/shard_map/ppermute | solution.py:366
  29.0 1.4 %collective-permute-start.9 = (f32[4,64,128]{2,1,0:T(8,128)S(1)}, f32[4,64,128]{2,1,0:T(8,128)S(1)}, u32[]{:S(2)}, u32[]{:S(2)}) collective-permute-start(f32[4,64,128]{2,1,0:T(8,128)S(1)} %get-tuple-element.29), channel_id=1, source_target_pairs={{0,8},{1,9},{2,10},{3,11},{4,12},{5,13},{6,14},{7,15},{8,0},{9,1},... | collective-permute-start | bytes 393224 | tf_op jit(solution)/shard_map/ppermute | solution.py:366
  30.5 6.5 %collective-permute-start.10 = (f32[2,64,128]{2,1,0:T(8,128)S(1)}, f32[2,64,128]{2,1,0:T(8,128)S(1)}, u32[]{:S(2)}, u32[]{:S(2)}) collective-permute-start(f32[2,64,128]{2,1,0:T(8,128)S(1)} %get-tuple-element.30.one), channel_id=1, source_target_pairs={{0,1},{1,0},{2,3},{3,2},{4,5},{5,4},{6,7},{7,6},{8,9},{9,8},{10,11... | collective-permute-start | bytes 196616 | tf_op jit(solution)/shard_map/ppermute | solution.py:366
  30.5 13.3 %collective-permute-start.14 = (f32[2,4,64,128]{3,2,1,0:T(8,128)S(1)}, f32[2,4,64,128]{3,2,1,0:T(8,128)S(1)}, u32[]{:S(2)}, u32[]{:S(2)}) collective-permute-start(f32[2,4,64,128]{3,2,1,0:T(8,128)S(1)} %get-tuple-element.32.two_high), channel_id=1, source_target_pairs={{0,2},{1,3},{2,4},{3,5},{4,6},{5,7},{6,0},{7,1},{8,10},{9,11},{10,... | collective-permute-start | bytes 786440 | tf_op jit(solution)/shard_map/ppermute | solution.py:366
  30.6 6.5 %collective-permute-start.12 = (f32[2,64,128]{2,1,0:T(8,128)S(1)}, f32[2,64,128]{2,1,0:T(8,128)S(1)}, u32[]{:S(2)}, u32[]{:S(2)}) collective-permute-start(f32[2,64,128]{2,1,0:T(8,128)S(1)} %get-tuple-element.31.one), channel_id=1, source_target_pairs={{0,16},{1,17},{2,18},{3,19},{4,20},{5,21},{6,22},{7,23},{8,24},{9,... | collective-permute-start | bytes 196616 | tf_op jit(solution)/shard_map/ppermute | solution.py:366
  33.2 13.8 %collective-permute-start.15 = (f32[2,4,64,128]{3,2,1,0:T(8,128)S(1)}, f32[2,4,64,128]{3,2,1,0:T(8,128)S(1)}, u32[]{:S(2)}, u32[]{:S(2)}) collective-permute-start(f32[2,4,64,128]{3,2,1,0:T(8,128)S(1)} %get-tuple-element.33.two_low), channel_id=1, source_target_pairs={{0,6},{1,7},{2,0},{3,1},{4,2},{5,3},{6,4},{7,5},{8,14},{9,15},{10,... | collective-permute-start | bytes 786440 | tf_op jit(solution)/shard_map/ppermute | solution.py:366
  37.0 4.3 %collective-permute-start.11 = (f32[2,64,128]{2,1,0:T(8,128)S(1)}, f32[2,64,128]{2,1,0:T(8,128)S(1)}, u32[]{:S(2)}, u32[]{:S(2)}) collective-permute-start(f32[2,64,128]{2,1,0:T(8,128)S(1)} %shard_map.56.upper), channel_id=1, source_target_pairs={{0,16},{1,17},{2,18},{3,19},{4,20},{5,21},{6,22},{7,23},{8,24},{9,... | collective-permute-start | bytes 196616 | tf_op jit(solution)/shard_map/ppermute | solution.py:366
  37.1 4.3 %collective-permute-start.13 = (f32[2,64,128]{2,1,0:T(8,128)S(1)}, f32[2,64,128]{2,1,0:T(8,128)S(1)}, u32[]{:S(2)}, u32[]{:S(2)}) collective-permute-start(f32[2,64,128]{2,1,0:T(8,128)S(1)} %shard_map.57.lower), channel_id=1, source_target_pairs={{0,1},{1,0},{2,3},{3,2},{4,5},{5,4},{6,7},{7,6},{8,9},{9,8},{10,11... | collective-permute-start | bytes 196616 | tf_op jit(solution)/shard_map/ppermute | solution.py:366
  41.5 7.6 %collective-permute-start.17 = (f32[4,64,128]{2,1,0:T(8,128)S(1)}, f32[4,64,128]{2,1,0:T(8,128)S(1)}, u32[]{:S(2)}, u32[]{:S(2)}) collective-permute-start(f32[4,64,128]{2,1,0:T(8,128)S(1)} %shard_map.58.refs_0_.j_mine), channel_id=1, source_target_pairs={{0,6},{1,7},{2,0},{3,1},{4,2},{5,3},{6,4},{7,5},{8,10},{9,11},{10,... | collective-permute-start | bytes 393224 | tf_op jit(solution)/shard_map/ppermute | solution.py:366
  46.9 2.2 %collective-permute-start.16 = (f32[4,64,128]{2,1,0:T(8,128)S(1)}, f32[4,64,128]{2,1,0:T(8,128)S(1)}, u32[]{:S(2)}, u32[]{:S(2)}) collective-permute-start(f32[4,64,128]{2,1,0:T(8,128)S(1)} %shard_map.58.refs_0_.j_mine), channel_id=1, source_target_pairs={{0,8},{1,9},{2,10},{3,11},{4,12},{5,13},{6,14},{7,15},{8,0},{9,1},... | collective-permute-start | bytes 393224 | tf_op jit(solution)/shard_map/ppermute | solution.py:366
  49.1 1.3 %collective-permute-start.18 = (f32[4,64,128]{2,1,0:T(8,128)S(1)}, f32[4,64,128]{2,1,0:T(8,128)S(1)}, u32[]{:S(2)}, u32[]{:S(2)}) collective-permute-start(f32[4,64,128]{2,1,0:T(8,128)S(1)} %collective-permute-done.17.refs_2_.j_halo), channel_id=1, source_target_pairs={{0,8},{1,9},{2,10},{3,11},{4,12},{5,13},{6,14},{7,15},{8,0},{9,1},... | collective-permute-start | bytes 393224 | tf_op jit(solution)/shard_map/ppermute | solution.py:366
  54.5 1.6 %collective-permute-start.20 = (f32[2,2,2,4,16,128]{5,4,3,2,1,0:T(8,128)S(1)}, f32[2,2,2,4,16,128]{5,4,3,2,1,0:T(8,128)S(1)}, u32[]{:S(2)}, u32[]{:S(2)}) collective-permute-start(f32[2,2,2,4,16,128]{5,4,3,2,1,0:T(8,128)S(1)} %get-tuple-element.39), channel_id=1, source_target_pairs={{0,8},{1,9},{2,10},{3,11},{4,12},{5,13},{6,14},{7,15},{8,0},{9,1},... | collective-permute-start | bytes 786440 | tf_op jit(solution)/shard_map/ppermute | solution.py:366
  56.2 8.2 %collective-permute-start.21 = (f32[2,4,16,128]{3,2,1,0:T(8,128)S(1)}, f32[2,4,16,128]{3,2,1,0:T(8,128)S(1)}, u32[]{:S(2)}, u32[]{:S(2)}) collective-permute-start(f32[2,4,16,128]{3,2,1,0:T(8,128)S(1)} %get-tuple-element.41), channel_id=1, source_target_pairs={{0,1},{1,0},{2,3},{3,2},{4,5},{5,4},{6,7},{7,6},{8,9},{9,8},{10,11... | collective-permute-start | bytes 196616 | tf_op jit(solution)/shard_map/ppermute | solution.py:366
  57.3 7.0 %collective-permute-start.22 = (f32[2,4,16,128]{3,2,1,0:T(8,128)S(1)}, f32[2,4,16,128]{3,2,1,0:T(8,128)S(1)}, u32[]{:S(2)}, u32[]{:S(2)}) collective-permute-start(f32[2,4,16,128]{3,2,1,0:T(8,128)S(1)} %get-tuple-element.42), channel_id=1, source_target_pairs={{0,16},{1,17},{2,18},{3,19},{4,20},{5,21},{6,22},{7,23},{8,24},{9,... | collective-permute-start | bytes 196616 | tf_op jit(solution)/shard_map/ppermute | solution.py:366
  57.8 6.5 %collective-permute-start.23 = (f32[2,4,16,128]{3,2,1,0:T(8,128)S(1)}, f32[2,4,16,128]{3,2,1,0:T(8,128)S(1)}, u32[]{:S(2)}, u32[]{:S(2)}) collective-permute-start(f32[2,4,16,128]{3,2,1,0:T(8,128)S(1)} %get-tuple-element.43), channel_id=1, source_target_pairs={{0,17},{1,16},{2,19},{3,18},{4,21},{5,20},{6,23},{7,22},{8,25},{9,... | collective-permute-start | bytes 196616 | tf_op jit(solution)/shard_map/ppermute | solution.py:366
  59.7 4.6 %collective-permute-start.19 = (f32[8,128]{1,0:T(8,128)S(1)}, f32[8,128]{1,0:T(8,128)S(1)}, u32[]{:S(2)}, u32[]{:S(2)}) collective-permute-start(f32[8,128]{1,0:T(8,128)S(1)} %shard_map.59), channel_id=1, source_target_pairs={{0,4},{1,5},{2,6},{3,7},{4,0},{5,1},{6,2},{7,3},{8,12},{9,13},{10,... | collective-permute-start | bytes 12296 | tf_op jit(solution)/shard_map/ppermute | solution.py:366
